TPU v7x, 32 devices: a whole 2x2x4 slice. The times are simulated.
32 devices in a mesh: batch: 8 (over z, x), head: 4 (over y, core).
Axes of the slice: x: 2, y: 2, z: 4, core: 2. Of those that a mesh axis runs over, the one named last changes fastest.
Arguments:
- hidden_in: bfloat16 [8, 2048, 1024], P('batch', None, 'head'), may hold values from -6 to 6
- cotangent: bfloat16 [8, 2048, 1024], P('batch', None, 'head'), may hold values from -6 to 6
- doc_ids: int32 [8, 2048], P('batch'), may hold values from 0 to 5, never falling along the last dimension, each value on 1 to 1024 neighbouring positions
- lengths: int32 [8], P('batch'), may hold values from 1536 to 2048
- w_query: bfloat16 [1024, 1024], P(None, 'head'), may hold values from -0.1875 to 0.1875
- w_key: bfloat16 [1024, 1024], P(None, 'head'), may hold values from -0.1875 to 0.1875
- w_value: bfloat16 [1024, 1024], P(None, 'head'), may hold values from -0.1875 to 0.1875
- w_out: bfloat16 [1024, 1024], P('head'), may hold values from -0.1875 to 0.1875
- w_up: bfloat16 [1024, 4096], P(None, 'head'), may hold values from -0.1875 to 0.1875
- w_gate: bfloat16 [1024, 4096], P(None, 'head'), may hold values from -0.1875 to 0.1875
- w_down: bfloat16 [4096, 1024], P('head'), may hold values from -0.09375 to 0.09375
- scale_qk: float32 [1024], P('head'), may hold values from 0.7 to 1.5
- scale_up: float32 [4096], P('head'), may hold values from 0.25 to 1.75
- scale_gate: float32 [4096], P('head'), may hold values from 0.5 to 2
- alpha_attn: float32 [1024], replicated, may hold values from 0.05 to 0.6
- alpha_ffn: float32 [1024], replicated, may hold values from 0.15 to 0.6
Outputs:
- hidden_out: bfloat16 [8, 2048, 1024], P('batch', None, 'head')
- grad_hidden: float32 [8, 2048, 1024], P('batch', None, 'head')
- grad_query: float32 [1024, 1024], P(None, 'head')
- grad_key: float32 [1024, 1024], P(None, 'head')
- grad_value: float32 [1024, 1024], P(None, 'head')
- grad_out: float32 [1024, 1024], P('head')
- grad_up: float32 [1024, 4096], P(None, 'head')
- grad_gate: float32 [1024, 4096], P(None, 'head')
- grad_down: float32 [4096, 1024], P('head')
- grad_scale_qk: float32 [1024], P('head')
- grad_scale_up: float32 [4096], P('head')
- grad_scale_gate: float32 [4096], P('head')
- grad_alpha_attn: float32 [1024], P('head')
- grad_alpha_ffn: float32 [1024], P('head')
Inputs may be any that keep to these rules, and one draw needn't show every extreme that they name: `doc_ids`: document number of each slot: never falls along a row, each document holds 1 to 1024 slots, one exactly 1024, all 6 present. `lengths`: slots at or past the length are padding.
All inputs are finite; a program needn't handle non-finite values.
Results may differ from a plain program's by a relative error of at most 0.025.
Values may be sent and summed in bfloat16 or wider, within the bound.
No kernel may reach another device: no remote copies, remote signals or barrier semaphores. Data moves between devices by JAX's collectives and lax.ppermute only.
A program may use at most 256 MiB of HBM per device.

v0:
```python
import math

import jax
import jax.numpy as jnp
from jax import lax
from jax.sharding import PartitionSpec as P

HD = 64


EPSILON = 1e-06


def shortened(array):
    return jax.tree.map(lambda a: a.astype(jnp.bfloat16) if a.dtype == jnp.float32 else a, array)


def rms_norm(values):
    factor = lax.rsqrt(jnp.mean(values * values, axis=-1, keepdims=True) + EPSILON)
    return (values * factor, factor)


def rotate(tensor, cosine_table, sine_table):
    half_dim = tensor.shape[-1] // 2
    front_half = tensor[..., :half_dim]
    back_half = tensor[..., half_dim:]
    return jnp.concatenate(
        [
            front_half * cosine_table - back_half * sine_table,
            back_half * cosine_table + front_half * sine_table,
        ],
        axis=-1,
    )


def rotate_back(gradient, cosine_table, sine_table):
    half_dim = gradient.shape[-1] // 2
    front_half = gradient[..., :half_dim]
    back_half = gradient[..., half_dim:]
    return jnp.concatenate(
        [
            front_half * cosine_table + back_half * sine_table,
            back_half * cosine_table - front_half * sine_table,
        ],
        axis=-1,
    )


def rope_tables(doc_ids):
    row_len = doc_ids.shape[1]
    column = jnp.arange(row_len, dtype=jnp.int32)
    changed = jnp.concatenate(
        [jnp.ones_like(doc_ids[:, :1], dtype=bool), doc_ids[:, 1:] != doc_ids[:, :-1]], axis=1
    )
    starts = lax.cummax(jnp.where(changed, column[None, :], 0), axis=1)
    positions = (column[None, :] - starts).astype(jnp.float32)
    frequency = 10000.0 ** (-(jnp.arange(HD // 2, dtype=jnp.float32) * 2.0 / HD))
    angles = positions[..., None] * frequency
    return (jnp.cos(angles)[:, :, None, :], jnp.sin(angles)[:, :, None, :])


def block_mask(doc_row, length, first_row, block_rows):
    row_len = doc_row.shape[0]
    query_index = first_row + jnp.arange(block_rows, dtype=jnp.int32)
    key_index = jnp.arange(row_len, dtype=jnp.int32)
    query_docs = lax.dynamic_slice_in_dim(doc_row, first_row, block_rows)
    same_doc = query_docs[:, None] == doc_row[None, :]
    causal = key_index[None, :] <= query_index[:, None]
    usable = (key_index[None, :] < length) | (key_index[None, :] == query_index[:, None])
    return same_doc & causal & usable


def block_scores(query_block, key_rows, doc_row, length, first_row, block_rows, factor):
    scores = (
        jnp.einsum("qhd,khd->hqk", query_block, key_rows, preferred_element_type=jnp.float32)
        * factor
    )
    visible_mask = block_mask(doc_row, length, first_row, block_rows)
    return (jnp.where(visible_mask[None], scores, -1e30), visible_mask)


def attend_forward(q_tilde, k_tilde, value_rows, doc_ids, lengths, block_rows, factor):
    rows_dev, row_len = doc_ids.shape
    blocks = row_len // block_rows

    def one_block(flat_index):
        row_id = flat_index // blocks
        first_row = flat_index % blocks * block_rows
        queries = lax.dynamic_index_in_dim(q_tilde, row_id, 0, keepdims=False)
        query_block = lax.dynamic_slice_in_dim(queries, first_row, block_rows, 0)
        key_rows = lax.dynamic_index_in_dim(k_tilde, row_id, 0, keepdims=False)
        row_values = lax.dynamic_index_in_dim(value_rows, row_id, 0, keepdims=False)
        doc_row = lax.dynamic_index_in_dim(doc_ids, row_id, 0, keepdims=False)
        length = lax.dynamic_index_in_dim(lengths, row_id, 0, keepdims=False)
        scores, visible_mask = block_scores(
            query_block, key_rows, doc_row, length, first_row, block_rows, factor
        )
        row_max = jnp.max(scores, axis=-1, keepdims=True)
        exp_scores = jnp.exp(scores - row_max)
        summed = jnp.sum(exp_scores, axis=-1, keepdims=True)
        attn_probs = (exp_scores / summed).astype(jnp.bfloat16)
        output = jnp.einsum(
            "hqk,khd->qhd", attn_probs, row_values, preferred_element_type=jnp.float32
        )
        return (output, (row_max + jnp.log(summed))[..., 0])

    outputs, logsum = lax.map(one_block, jnp.arange(rows_dev * blocks, dtype=jnp.int32))
    return (outputs.reshape(rows_dev * row_len, -1), logsum)


def attend_backward(
    q_tilde, k_tilde, value_rows, grad_attended, logsum, doc_ids, lengths, block_rows, factor
):
    rows_dev, row_len = doc_ids.shape
    blocks = row_len // block_rows
    grad_queries, grad_keys_all, grad_values_all = ([], [], [])
    queries = q_tilde[0]
    key_rows = k_tilde[0]
    row_values = value_rows[0]
    grad_row = grad_attended[0]
    doc_row = doc_ids[0]
    length = lengths[0]

    def one_block(carried, block_index):
        grad_keys, grad_vals = carried
        first_row = block_index * block_rows
        query_block = lax.dynamic_slice_in_dim(queries, first_row, block_rows, 0)
        grad_block = lax.dynamic_slice_in_dim(grad_row, first_row, block_rows, 0)
        block_lse = lax.dynamic_index_in_dim(logsum, 0 + block_index, 0, keepdims=False)
        scores, visible_mask = block_scores(
            query_block, key_rows, doc_row, length, first_row, block_rows, factor
        )
        attn_probs = jnp.where(visible_mask[None], jnp.exp(scores - block_lse[..., None]), 0.0)
        probs_low = attn_probs.astype(jnp.bfloat16)
        grad_probs = jnp.einsum(
            "qhd,khd->hqk", grad_block, row_values, preferred_element_type=jnp.float32
        )
        row_inner = jnp.sum(attn_probs * grad_probs, axis=-1, keepdims=True)
        grad_scores = (attn_probs * (grad_probs - row_inner) * factor).astype(jnp.bfloat16)
        grad_query = jnp.einsum(
            "hqk,khd->qhd", grad_scores, key_rows, preferred_element_type=jnp.float32
        )
        grad_keys = grad_keys + jnp.einsum(
            "hqk,qhd->khd", grad_scores, query_block, preferred_element_type=jnp.float32
        )
        grad_vals = grad_vals + jnp.einsum(
            "hqk,qhd->khd", probs_low, grad_block, preferred_element_type=jnp.float32
        )
        return ((grad_keys, grad_vals), grad_query)

    empty = jnp.zeros(key_rows.shape, jnp.float32)
    carried, grad_blocks = lax.scan(one_block, (empty, empty), jnp.arange(blocks, dtype=jnp.int32))
    grad_queries.append(grad_blocks.reshape(queries.shape))
    grad_keys_all.append(carried[0])
    grad_values_all.append(carried[1])
    return (jnp.stack(grad_queries), jnp.stack(grad_keys_all), jnp.stack(grad_values_all))


def contract_rows(left_side, right_side):
    return lax.dot_general(
        left_side, right_side, (((0,), (0,)), ((), ())), preferred_element_type=jnp.float32
    )


def contract_cols(left_side, right_side):
    return lax.dot_general(
        left_side, right_side, (((1,), (1,)), ((), ())), preferred_element_type=jnp.float32
    )


def on_device(
    hidden_in,
    cotangent,
    doc_ids,
    lengths,
    w_query,
    w_key,
    w_value,
    w_out,
    w_up,
    w_gate,
    w_down,
    scale_qk,
    scale_up,
    scale_gate,
    alpha_attn,
    alpha_ffn,
):
    rows_x, rows_c = (
        lax.all_gather(hidden_in, "head", axis=2, tiled=True),
        lax.all_gather(cotangent, "head", axis=2, tiled=True),
    )
    rows_dev, row_len, share_cols = hidden_in.shape
    model_dim = rows_x.shape[2]
    tokens = rows_dev * row_len
    head_cols = w_query.shape[1]
    heads_here = head_cols // HD
    block_rows = min(512, row_len)
    factor = 1.0 / math.sqrt(HD)
    first_col = lax.axis_index("head") * share_cols

    def own_cols(values):
        return lax.dynamic_slice_in_dim(values, first_col, share_cols, 1)

    x_low = rows_x.reshape(tokens, model_dim)
    h_zero = x_low.astype(jnp.float32)
    cosine_table, sine_table = rope_tables(doc_ids)
    qk_gain = scale_qk.reshape(heads_here, HD)

    def head_layout(values):
        return values.reshape(rows_dev, row_len, heads_here, HD)

    q_raw = head_layout(jnp.dot(x_low, w_query, preferred_element_type=jnp.float32))
    k_raw = head_layout(jnp.dot(x_low, w_key, preferred_element_type=jnp.float32))
    v_low = head_layout(
        jnp.dot(x_low, w_value, preferred_element_type=jnp.float32).astype(jnp.bfloat16)
    )
    q_unit, q_factor = rms_norm(rotate(q_raw, cosine_table, sine_table))
    k_unit, k_factor = rms_norm(rotate(k_raw, cosine_table, sine_table))
    q_tilde = (q_unit * qk_gain).astype(jnp.bfloat16)
    k_tilde = (k_unit * qk_gain).astype(jnp.bfloat16)
    attended, logsum = attend_forward(q_tilde, k_tilde, v_low, doc_ids, lengths, block_rows, factor)
    att_low = attended.astype(jnp.bfloat16)
    y_sum = lax.psum(
        jnp.dot(att_low, w_out, preferred_element_type=jnp.float32).astype(jnp.bfloat16), "head"
    ).astype(jnp.float32)
    h_attn, y_factor = rms_norm(y_sum)
    h_one, one_factor = rms_norm(h_zero + alpha_attn * (h_attn - h_zero))
    h_one_low = h_one.astype(jnp.bfloat16)
    up_raw = jnp.dot(h_one_low, w_up, preferred_element_type=jnp.float32)
    gate_raw = jnp.dot(h_one_low, w_gate, preferred_element_type=jnp.float32)
    up_act = up_raw * scale_up
    gate_act = gate_raw * scale_gate
    sigmoid_gate = jax.nn.sigmoid(gate_act)
    silu_gate = gate_act * sigmoid_gate
    mixed_low = (up_act * silu_gate).astype(jnp.bfloat16)
    z_sum = lax.psum(
        jnp.dot(mixed_low, w_down, preferred_element_type=jnp.float32).astype(jnp.bfloat16), "head"
    ).astype(jnp.float32)
    h_ffn, z_factor = rms_norm(z_sum)
    h_two, two_factor = rms_norm(h_one + alpha_ffn * (h_ffn - h_one))
    hidden_out = own_cols(h_two).astype(jnp.bfloat16).reshape(rows_dev, row_len, share_cols)
    cot_rows = rows_c.reshape(tokens, model_dim).astype(jnp.float32)
    grad_pre_two = two_factor * (
        cot_rows - h_two * jnp.mean(cot_rows * h_two, axis=-1, keepdims=True)
    )
    grad_alpha_ffn = jnp.sum(grad_pre_two * (h_ffn - h_one), axis=0)
    grad_h_ffn = grad_pre_two * alpha_ffn
    grad_z_low = (
        z_factor * (grad_h_ffn - h_ffn * jnp.mean(grad_h_ffn * h_ffn, axis=-1, keepdims=True))
    ).astype(jnp.bfloat16)
    grad_down = contract_rows(mixed_low, grad_z_low)
    grad_mixed = contract_cols(grad_z_low, w_down)
    grad_up_act = grad_mixed * silu_gate
    grad_gate_act = grad_mixed * up_act * sigmoid_gate * (1.0 + gate_act * (1.0 - sigmoid_gate))
    grad_scale_up = jnp.sum(grad_up_act * up_raw, axis=0)
    grad_scale_gate = jnp.sum(grad_gate_act * gate_raw, axis=0)
    grad_up_low = (grad_up_act * scale_up).astype(jnp.bfloat16)
    grad_gate_low = (grad_gate_act * scale_gate).astype(jnp.bfloat16)
    grad_w_up = contract_rows(h_one_low, grad_up_low)
    grad_w_gate = contract_rows(h_one_low, grad_gate_low)
    ffn_grads = (grad_w_up, grad_w_gate, grad_down, grad_scale_up, grad_scale_gate, grad_alpha_ffn)
    part_one = contract_cols(grad_up_low, w_up) + contract_cols(grad_gate_low, w_gate)
    grad_h_one = own_cols(grad_pre_two * (1.0 - alpha_ffn)) + lax.psum_scatter(
        part_one.astype(jnp.bfloat16), "head", scatter_dimension=1, tiled=True
    ).astype(jnp.float32)
    h_one_own = own_cols(h_one)
    h_attn_own = own_cols(h_attn)
    h_zero_own = own_cols(h_zero)
    alpha_own = lax.dynamic_slice_in_dim(alpha_attn, first_col, share_cols)
    stat_one = lax.psum(jnp.sum(grad_h_one * h_one_own, axis=-1), "head")
    grad_pre_one = one_factor * (grad_h_one - h_one_own * stat_one[:, None] / model_dim)
    grad_h_attn = grad_pre_one * alpha_own
    stat_two = lax.psum(jnp.sum(grad_h_attn * h_attn_own, axis=-1), "head")
    grad_alpha_attn = jnp.sum(grad_pre_one * (h_attn_own - h_zero_own), axis=0)
    direct_zero = grad_pre_one * (1.0 - alpha_own)
    grad_y_low = (y_factor * (grad_h_attn - h_attn_own * stat_two[:, None] / model_dim)).astype(
        jnp.bfloat16
    )
    grad_y_all = lax.all_gather(grad_y_low, "head", axis=1, tiled=True)
    grad_w_out = contract_rows(att_low, grad_y_all)
    grad_att_low = head_layout(contract_cols(grad_y_all, w_out).astype(jnp.bfloat16))
    grad_q_tilde, grad_k_tilde, grad_values = attend_backward(
        q_tilde, k_tilde, v_low, grad_att_low, logsum, doc_ids, lengths, block_rows, factor
    )
    grad_scale_qk = jnp.sum(grad_q_tilde * q_unit + grad_k_tilde * k_unit, axis=(0, 1)).reshape(
        head_cols
    )

    def unit_back(grad_tilde, unit_values, unit_factor):
        grad_unit = grad_tilde * qk_gain
        grad_rot = unit_factor * (
            grad_unit - unit_values * jnp.mean(grad_unit * unit_values, axis=-1, keepdims=True)
        )
        return (
            rotate_back(grad_rot, cosine_table, sine_table)
            .reshape(tokens, head_cols)
            .astype(jnp.bfloat16)
        )

    grad_q_low = unit_back(grad_q_tilde, q_unit, q_factor)
    grad_k_low = unit_back(grad_k_tilde, k_unit, k_factor)
    grad_v_low = grad_values.reshape(tokens, head_cols).astype(jnp.bfloat16)
    grad_w_query = contract_rows(x_low, grad_q_low)
    grad_w_key = contract_rows(x_low, grad_k_low)
    grad_w_value = contract_rows(x_low, grad_v_low)
    part_zero = (
        contract_cols(grad_q_low, w_query)
        + contract_cols(grad_k_low, w_key)
        + contract_cols(grad_v_low, w_value)
    )
    grad_hidden = (
        direct_zero
        + lax.psum_scatter(
            part_zero.astype(jnp.bfloat16), "head", scatter_dimension=1, tiled=True
        ).astype(jnp.float32)
    ).reshape(rows_dev, row_len, share_cols)
    attn_grads = (
        grad_w_query,
        grad_w_key,
        grad_w_value,
        grad_w_out,
        grad_scale_qk,
        grad_alpha_attn,
    )
    every_grad = jax.tree.map(
        lambda part: part.astype(jnp.float32), lax.psum(shortened(attn_grads + ffn_grads), "batch")
    )
    attn_grads = every_grad[:6]
    ffn_grads = every_grad[6:]
    return (
        hidden_out,
        grad_hidden,
        attn_grads[0],
        attn_grads[1],
        attn_grads[2],
        attn_grads[3],
        ffn_grads[0],
        ffn_grads[1],
        ffn_grads[2],
        attn_grads[4],
        ffn_grads[3],
        ffn_grads[4],
        attn_grads[5],
        own_cols(ffn_grads[5][None, :])[0],
    )


def solution(mesh):
    placed = (
        P("batch", None, "head"),
        P("batch", None, "head"),
        P("batch", None),
        P("batch"),
        P(None, "head"),
        P(None, "head"),
        P(None, "head"),
        P("head", None),
        P(None, "head"),
        P(None, "head"),
        P("head", None),
        P("head"),
        P("head"),
        P("head"),
        P(),
        P(),
    )
    return jax.shard_map(
        on_device,
        mesh=mesh,
        in_specs=placed,
        out_specs=(
            P("batch", None, "head"),
            P("batch", None, "head"),
            P(None, "head"),
            P(None, "head"),
            P(None, "head"),
            P("head", None),
            P(None, "head"),
            P(None, "head"),
            P("head", None),
            P("head"),
            P("head"),
            P("head"),
            P("head"),
            P("head"),
        ),
        check_vma=False,
    )
```

profile of v0, /device:TPU:8, one launch (start us, length us, event | category | flops | bytes accessed | tf_op | source)
XLA Modules:
  0.0 1260.7 jit_solution(3511851802887819732)
XLA Ops:
  15.9 29.9 %all-gather.4.cloned.1.call-done = bf16[1,2048,1024]{2,1,0:T(8,128)(2,1)} async-done(((bf16[1,2048,256]{2,1,0:T(8,128)(2,1)}), bf16[1,2048,1024]{2,1,0:T(8,128)(2,1)}) %all-gather.4.cloned.1.call-update) | async-done | bytes 4194320 | tf_op jit(solution)/shard_map/all_gather | solution.py:190
  56.5 89.2 %while.31 = (s32[]{:T(128)}, bf16[4,512,4,64]{1,3,2,0:T(8,128)(2,1)}, f32[4,4,512]{2,1,0:T(4,128)}, s32[4]{0:T(128)S(1)}, s32[1,2048]{1,0:T(1,128)S(1)}, /*index...) while((s32[]{:T(128)}, ...), condition=%wide.region_7.8_spmd.clone, body=%wide.region_4.7_spmd.sunk.clone | while | flops 1130365440 | bytes 61693232 | solution.py:107
  63.7 4.4 fusion.206
  68.2 4.3 fusion.207
  73.1 5.9 fusion.208
  86.0 4.4 fusion.206
  90.4 4.3 fusion.207
  95.4 5.9 fusion.208
  108.2 4.4 fusion.206
  112.6 4.3 fusion.207
  117.6 5.9 fusion.208
  130.4 4.4 fusion.206
  134.8 4.3 fusion.207
  139.8 5.9 fusion.208
  152.5 85.6 %all-reduce.6.cloned.1.call-done = bf16[2048,1024]{1,0:T(8,128)(2,1)} async-done(((bf16[2048,1024]{1,0:T(8,128)(2,1)}), bf16[2048,1024]{1,0:T(8,128)(2,1)}) %all-reduce.6.cloned.1.call-update) | async-done | bytes 4194320 | tf_op jit(solution)/shard_map/psum | solution.py:224
  241.5 7.3 convert_multiply_fusion.3
  248.8 4.5 fusion.122
  253.3 4.6 fusion.123
  257.9 7.6 multiply_convert_fusion.3
  267.5 6.0 convolution_convert_fusion.1
  274.3 85.0 %all-reduce.8.cloned.1.call-done = bf16[2048,1024]{1,0:T(8,128)(2,1)} async-done(((bf16[2048,1024]{1,0:T(8,128)(2,1)}), bf16[2048,1024]{1,0:T(8,128)(2,1)}) %all-reduce.8.cloned.1.call-update) | async-done | bytes 4194320 | tf_op jit(solution)/shard_map/psum | solution.py:237
  362.8 4.6 multiply_reduce_fusion.4
  367.4 28.5 %all-gather.6.cloned.1.call-done = bf16[1,2048,1024]{2,1,0:T(8,128)(2,1)} async-done(((bf16[1,2048,256]{2,1,0:T(8,128)(2,1)}), bf16[1,2048,1024]{2,1,0:T(8,128)(2,1)}) %all-gather.6.cloned.1.call-update) | async-done | bytes 4194320 | tf_op jit(solution)/shard_map/all_gather | solution.py:191
  395.9 9.5 fusion.71
  407.3 8.6 multiply_reduce_fusion.1
  419.1 16.0 %multiply_reduce_fusion.2 = (bf16[1024]{0:T(1024)(128)(2,1)}, bf16[1024]{0:T(1024)(128)(2,1)}, f32[2048,1024]{1,0:T(8,128)}, bf16[2048,1024]{1,0:T(8,128)(2,1)S(1)}) fusion(f32[2048,1024]{1,0:T(8,128)} %copy-done.83, f32[2048,1024]{1,0:T(8,128)} %get-tuple-element.384, f32[1024]{0:T(1024)S(1)} %copy-done.79, f32[1024]{0:T(1024)S(1)} %copy-done.78, ...), kind=kOutput, calls=%fused_computation.79 | convolution fusion | flops 4334811136 | bytes 35663872 | tf_op jit(solution)/shard_map/dot_general | solution.py:166
  435.2 6.9 fusion.124
  442.1 11.2 add_convert_fusion.1
  454.1 7.0 bitcast_convert_fusion
  461.1 36.9 %reduce-scatter.3.cloned.1.call-done = bf16[2048,256]{1,0:T(8,128)(2,1)} async-done(((bf16[2048,1024]{1,0:T(8,128)(2,1)}), bf16[2048,256]{1,0:T(8,128)(2,1)}) %reduce-scatter.3.cloned.1.call-update) | async-done | bytes 1048592 | tf_op jit(solution)/shard_map/reduce_scatter | solution.py:264
  501.1 6.1 psum.114
  507.2 4.7 multiply_reduce_fusion.6
  511.9 5.7 psum.115
  532.8 8.2 convolution_convert_fusion.3
  541.1 5.8 convolution_convert_fusion.5
  546.9 5.8 convolution_convert_fusion.4
  552.7 4.2 all-gather.8.cloned.1.call-done
  556.9 4.4 convolution_convert_fusion.2
  561.4 338.5 %while.32 = (s32[]{:T(128)}, f32[2048,4,64]{0,2,1:T(8,128)}, f32[2048,4,64]{0,2,1:T(8,128)S(1)}, f32[4,512,4,64]{1,3,2,0:T(8,128)}, s32[4]{0:T(128)S(1)}, /*inde...) while((s32[]{:T(128)}, f32[2048,4,64]{0,2,1:T(8,128)}, ...), condition=%wide.region_23.24_spmd.clone.clone, body=%wide.region_21.23_spmd.clone.sunk.clone | while | flops 2755668480 | bytes 208190256 | solution.py:152
  569.8 10.0 exponential_select_fusion.3
  579.8 9.1 fusion.220
  588.9 25.7 %fusion.223 = f32[4,512,4,64]{1,3,2,0:T(8,128)} fusion(f32[4,512,4,64]{1,3,2,0:T(8,128)} %get-tuple-element.627, s32[]{:T(128)} %get-tuple-element.624, bf16[2048,4,64]{0,2,1:T(8,128)(2,1)S(1)} %copy-done.52, f32[4,512,2048]{2,1,0:T(8,128)} %exponential_select_fusion.3, f32[4,512,2048]{2,1,0:T(8,128)} %fusion.220), kind=kOutput, calls=%fused_computation.44.clone.1.clone | convolution fusion | flops 557846528 | bytes 68682240 | tf_op jit(solution)/shard_map/while/body/eval_jaxpr/hqk,khd->qhd/dot_general | solution.py:140
  614.6 23.3 %fusion.221 = f32[2048,4,64]{0,2,1:T(8,128)} fusion(f32[4,512,2048]{2,1,0:T(8,128)} %exponential_select_fusion.3, f32[4,512,2048]{2,1,0:T(8,128)} %fusion.220, f32[2048,4,64]{0,2,1:T(8,128)} %get-tuple-element.625, pred[]{:T(512)S(6)} %compare.7, bf16[2048,4,64]{0,2,1:T(8,128)(2,1)} %get-tuple-element.642, s32[]{:T(128)S(6)} %select_n.122), kind=kOutput, calls=%fused_computation.41.clone.1.clone | convolution fusion | flops 558895104 | bytes 71565320 | tf_op jit(solution)/shard_map/while/body/eval_jaxpr/hqk,qhd->khd/dot_general | solution.py:143
  638.0 7.7 fusion.222
  654.0 10.0 exponential_select_fusion.3
  663.9 9.1 fusion.220
  673.1 25.7 %fusion.223 = f32[4,512,4,64]{1,3,2,0:T(8,128)} fusion(f32[4,512,4,64]{1,3,2,0:T(8,128)} %get-tuple-element.627, s32[]{:T(128)} %get-tuple-element.624, bf16[2048,4,64]{0,2,1:T(8,128)(2,1)S(1)} %copy-done.52, f32[4,512,2048]{2,1,0:T(8,128)} %exponential_select_fusion.3, f32[4,512,2048]{2,1,0:T(8,128)} %fusion.220), kind=kOutput, calls=%fused_computation.44.clone.1.clone | convolution fusion | flops 557846528 | bytes 68682240 | tf_op jit(solution)/shard_map/while/body/eval_jaxpr/hqk,khd->qhd/dot_general | solution.py:140
  698.8 23.8 %fusion.221 = f32[2048,4,64]{0,2,1:T(8,128)} fusion(f32[4,512,2048]{2,1,0:T(8,128)} %exponential_select_fusion.3, f32[4,512,2048]{2,1,0:T(8,128)} %fusion.220, f32[2048,4,64]{0,2,1:T(8,128)} %get-tuple-element.625, pred[]{:T(512)S(6)} %compare.7, bf16[2048,4,64]{0,2,1:T(8,128)(2,1)} %get-tuple-element.642, s32[]{:T(128)S(6)} %select_n.122), kind=kOutput, calls=%fused_computation.41.clone.1.clone | convolution fusion | flops 558895104 | bytes 71565320 | tf_op jit(solution)/shard_map/while/body/eval_jaxpr/hqk,qhd->khd/dot_general | solution.py:143
  722.6 7.7 fusion.222
  738.6 10.0 exponential_select_fusion.3
  748.6 9.1 fusion.220
  757.7 25.7 %fusion.223 = f32[4,512,4,64]{1,3,2,0:T(8,128)} fusion(f32[4,512,4,64]{1,3,2,0:T(8,128)} %get-tuple-element.627, s32[]{:T(128)} %get-tuple-element.624, bf16[2048,4,64]{0,2,1:T(8,128)(2,1)S(1)} %copy-done.52, f32[4,512,2048]{2,1,0:T(8,128)} %exponential_select_fusion.3, f32[4,512,2048]{2,1,0:T(8,128)} %fusion.220), kind=kOutput, calls=%fused_computation.44.clone.1.clone | convolution fusion | flops 557846528 | bytes 68682240 | tf_op jit(solution)/shard_map/while/body/eval_jaxpr/hqk,khd->qhd/dot_general | solution.py:140
  783.4 23.9 %fusion.221 = f32[2048,4,64]{0,2,1:T(8,128)} fusion(f32[4,512,2048]{2,1,0:T(8,128)} %exponential_select_fusion.3, f32[4,512,2048]{2,1,0:T(8,128)} %fusion.220, f32[2048,4,64]{0,2,1:T(8,128)} %get-tuple-element.625, pred[]{:T(512)S(6)} %compare.7, bf16[2048,4,64]{0,2,1:T(8,128)(2,1)} %get-tuple-element.642, s32[]{:T(128)S(6)} %select_n.122), kind=kOutput, calls=%fused_computation.41.clone.1.clone | convolution fusion | flops 558895104 | bytes 71565320 | tf_op jit(solution)/shard_map/while/body/eval_jaxpr/hqk,qhd->khd/dot_general | solution.py:143
  807.3 7.7 fusion.222
  823.3 10.0 exponential_select_fusion.3
  833.3 9.1 fusion.220
  842.4 25.7 %fusion.223 = f32[4,512,4,64]{1,3,2,0:T(8,128)} fusion(f32[4,512,4,64]{1,3,2,0:T(8,128)} %get-tuple-element.627, s32[]{:T(128)} %get-tuple-element.624, bf16[2048,4,64]{0,2,1:T(8,128)(2,1)S(1)} %copy-done.52, f32[4,512,2048]{2,1,0:T(8,128)} %exponential_select_fusion.3, f32[4,512,2048]{2,1,0:T(8,128)} %fusion.220), kind=kOutput, calls=%fused_computation.44.clone.1.clone | convolution fusion | flops 557846528 | bytes 68682240 | tf_op jit(solution)/shard_map/while/body/eval_jaxpr/hqk,khd->qhd/dot_general | solution.py:140
  868.1 23.8 %fusion.221 = f32[2048,4,64]{0,2,1:T(8,128)} fusion(f32[4,512,2048]{2,1,0:T(8,128)} %exponential_select_fusion.3, f32[4,512,2048]{2,1,0:T(8,128)} %fusion.220, f32[2048,4,64]{0,2,1:T(8,128)} %get-tuple-element.625, pred[]{:T(512)S(6)} %compare.7, bf16[2048,4,64]{0,2,1:T(8,128)(2,1)} %get-tuple-element.642, s32[]{:T(128)S(6)} %select_n.122), kind=kOutput, calls=%fused_computation.41.clone.1.clone | convolution fusion | flops 558895104 | bytes 71565320 | tf_op jit(solution)/shard_map/while/body/eval_jaxpr/hqk,qhd->khd/dot_general | solution.py:143
  892.0 7.7 fusion.222
  900.0 4.4 copy.54
  910.3 4.4 add_reduce_fusion
  938.9 19.6 %all-reduce = (bf16[1024]{0:T(1024)(128)(2,1)S(1)}, bf16[256]{0:T(256)(128)(2,1)S(1)}, bf16[1024]{0:T(1024)(128)(2,1)S(1)}, bf16[1024]{0:T(1024)(128)(2,1)S(1)}, bf16[256]{0:T(256)(128)(2,1)S(1)}) all-reduce(bf16[1024]{0:T(1024)(128)(2,1)S(1)} %copy-done.68, ...), channel_id=1, replica_groups=mesh['batch'=8,'head'=4] {'batch'}, use_global_device_ids=true, to_apply=%region_43.44 | all-reduce | flops 3584 | bytes 14336 | tf_op jit(solution)/shard_map/psum | solution.py:327
  961.5 240.6 %all-reduce.10.cloned.1.call-done = (bf16[1024,256]{0,1:T(8,128)(2,1)}, bf16[1024,256]{0,1:T(8,128)(2,1)}, bf16[1024,256]{0,1:T(8,128)(2,1)}, bf16[256,1024]{1,0...) async-done(((bf16[1024,256]{0,1:T(8,128)(2,1)}, bf16[1024,256]{0,1:T(8,128)(2,1)}, bf16[1024,256]{0,1:T(8,128)(2,1)}, ...) | async-done | bytes 8388624 | tf_op jit(solution)/shard_map/psum | solution.py:327
  1216.9 33.2 %reduce-scatter.5.cloned.1.call-done = bf16[2048,256]{1,0:T(8,128)(2,1)} async-done(((bf16[2048,1024]{1,0:T(8,128)(2,1)}), bf16[2048,256]{1,0:T(8,128)(2,1)}) %reduce-scatter.5.cloned.1.call-update) | async-done | bytes 1048592 | tf_op jit(solution)/shard_map/reduce_scatter | solution.py:314
  (339 shorter events, 155.5 us)
Async XLA Ops:
  7.2 260.3 %copy-start = (bf16[1024,1024]{1,0:T(8,128)(2,1)S(1)}, bf16[1024,1024]{1,0:T(8,128)(2,1)}, u32[]{:S(2)}) copy-start(bf16[1024,1024]{1,0:T(8,128)(2,1)} %param.30) | copy-start | bytes 6291460
  7.2 38.6 %all-gather.4.cloned.1.call-start = ((), (), s32[]{:S(2)}) async-start(), calls=%async_computation.2 | async-start | bytes 5242880 | tf_op jit(solution)/shard_map/all_gather | solution.py:190
  7.9 230.1 %all-reduce.6.cloned.1.call-start = ((), (), s32[]{:S(2)}) async-start(), calls=%async_computation.3 | async-start | bytes 8388608 | tf_op jit(solution)/shard_map/psum | solution.py:224
  13.7 38.8 %copy-start.64 = (f32[4,64]{1,0:T(4,128)}, f32[4,64]{1,0:T(4,128)S(1)}, u32[]{:S(2)}) copy-start(f32[4,64]{1,0:T(4,128)S(1)} %mul.599) | copy-start | bytes 3076
  15.9 35.1 %copy-start.39 = (f32[2048,32]{0,1:T(8,128)}, f32[2048,32]{0,1:T(8,128)S(1)}, u32[]{:S(2)}) copy-start(f32[2048,32]{0,1:T(8,128)S(1)} %get-tuple-element.377) | copy-start | bytes 786436
  15.9 35.1 %copy-start.41 = (f32[2048,32]{0,1:T(8,128)}, f32[2048,32]{0,1:T(8,128)S(1)}, u32[]{:S(2)}) copy-start(f32[2048,32]{0,1:T(8,128)S(1)} %get-tuple-element.378) | copy-start | bytes 786436
  68.2 5.0 copy-start.21
  90.4 5.0 copy-start.21
  112.6 5.0 copy-start.21
  134.8 5.0 copy-start.21
  152.4 88.9 %copy-start.67 = (f32[1024]{0:T(1024)S(1)}, f32[1024]{0:T(1024)}, u32[]{:S(2)}) copy-start(f32[1024]{0:T(1024)} %param.34) | copy-start | bytes 12292
  152.4 206.9 %all-reduce.8.cloned.1.call-start = ((), (), s32[]{:S(2)}) async-start(), calls=%async_computation.4 | async-start | bytes 8388608 | tf_op jit(solution)/shard_map/psum | solution.py:237
  241.5 7.3 copy-start.14
  248.8 4.5 copy-start.76
  253.3 4.6 copy-start.30
  253.3 4.6 copy-start.74
  253.3 4.6 copy-start.78
  253.3 4.6 copy-start.79
  257.9 7.6 copy-start.83
  273.5 89.1 %copy-start.63 = (f32[1024]{0:T(1024)S(1)}, f32[1024]{0:T(1024)}, u32[]{:S(2)}) copy-start(f32[1024]{0:T(1024)} %param.35) | copy-start | bytes 12292
  273.5 122.4 %all-gather.6.cloned.1.call-start = ((), (), s32[]{:S(2)}) async-start(), calls=%async_computation.5 | async-start | bytes 5242880 | tf_op jit(solution)/shard_map/all_gather | solution.py:191
  274.1 223.9 %reduce-scatter.3.cloned.1.call-start = ((), (), s32[]{:S(2)}) async-start(), calls=%async_computation.6 | async-start | bytes 5242880 | tf_op jit(solution)/shard_map/reduce_scatter | solution.py:264
  395.9 9.5 copy-start.3
  395.9 11.3 copy-start.25
  419.1 16.0 %copy-start.37 = (bf16[2048,1024]{1,0:T(8,128)(2,1)}, bf16[2048,1024]{1,0:T(8,128)(2,1)S(1)}, u32[]{:S(2)}) copy-start(bf16[2048,1024]{1,0:T(8,128)(2,1)S(1)} %fusion.69) | copy-start | bytes 12582916
  419.1 16.0 %copy-start.75 = (bf16[1024,1024]{1,0:T(8,128)(2,1)S(1)}, bf16[1024,1024]{1,0:T(8,128)(2,1)}, u32[]{:S(2)}) copy-start(bf16[1024,1024]{1,0:T(8,128)(2,1)} %param.28) | copy-start | bytes 6291460
  435.2 6.9 copy-start.81
  435.2 6.9 copy-start.77
  453.3 103.6 %all-gather.8.cloned.1.call-start = ((), (), s32[]{:S(2)}) async-start(), calls=%async_computation.7 | async-start | bytes 5242880 | tf_op jit(solution)/shard_map/all_gather | solution.py:280
  498.0 9.2 copy-start.34
  511.9 8.7 copy-start.23
  517.6 5.9 copy-start.6
  520.5 681.6 %all-reduce.10.cloned.1.call-start = ((), (), s32[]{:S(2)}) async-start(), calls=%async_computation.9 | async-start | bytes 16777216 | tf_op jit(solution)/shard_map/psum | solution.py:327
  520.6 10.2 copy-start.50
  520.6 10.1 copy-start.54
  520.6 10.1 copy-start.65
  525.2 5.5 copy-start.9
  525.2 5.5 copy-start.16
  525.2 5.6 copy-start.19
  527.9 4.9 copy-start.38
  532.8 8.3 copy-start.31
  532.8 8.3 copy-start.82
  532.8 14.1 %slice-start = ((s8[8388608]{0:T(1024)(128)(4,1)}), s8[4194304]{0:T(1024)(128)(4,1)S(1)}, s32[]{:S(2)}) async-start(s8[8388608]{0:T(1024)(128)(4,1)} %bitcast.278), calls=%async_computation.10 | async-start | bytes 8388608
  541.1 5.8 slice-start.1
  546.9 10.0 copy-start.57
  552.7 8.7 copy-start.48
  569.8 10.0 copy-start.22
  579.8 9.1 copy-start.52
  654.0 10.0 copy-start.22
  663.9 9.1 copy-start.52
  738.6 10.0 copy-start.22
  748.6 9.1 copy-start.52
  823.3 10.0 copy-start.22
  833.3 9.1 copy-start.52
  899.9 6.0 copy-start.35
  899.9 6.0 copy-start.36
  899.9 6.0 copy-start.51
  899.9 6.0 copy-start.66
  915.4 11.0 copy-start.32
  928.6 321.6 %reduce-scatter.5.cloned.1.call-start = ((), (), s32[]{:S(2)}) async-start(), calls=%async_computation.8 | async-start | bytes 5242880 | tf_op jit(solution)/shard_map/reduce_scatter | solution.py:314
  1208.8 5.8 copy-start.61
  1208.8 7.0 copy-start.60
  1211.3 38.9 %copy-start.69 = (f32[256]{0:T(256)S(1)}, f32[256]{0:T(256)}, u32[]{:S(2)}) copy-start(f32[256]{0:T(256)} %get-tuple-element.352) | copy-start | bytes 3076
  1214.6 39.1 %copy-start.1 = (bf16[1024,1024]{1,0:T(8,128)(2,1)S(1)}, bf16[1024,1024]{1,0:T(8,128)(2,1)}, u32[]{:S(2)}) copy-start(bf16[1024,1024]{1,0:T(8,128)(2,1)} %param.30) | copy-start | bytes 6291460
  (39 other events, 109.0 us)
Sparse Core Ops, SparseCore 0:
  9.6 36.1 all-gather.3
  152.5 85.4 all-reduce.5
  273.6 85.6 all-reduce.7
  360.7 35.1 all-gather.5
  453.5 44.4 reduce-scatter.2
  520.6 36.2 all-gather.7
  928.7 273.3 all-reduce.9
  1204.7 45.3 reduce-scatter.4
where the time goes:
time: 1270 us; the launch traced here: 1260 us
  waiting for transfers between devices  545 us (43%)
  matrix products  448 us (35%)
  other arithmetic  147 us (12%)
  local copies, waits for them, and re-layouts  53.1 us (4%)
  blocking collectives  31.4 us (2%)
  loops' own time  19.3 us (2%)
  between operations  15.3 us (1%)
    psum x1, waiting for transfers between devices, on_device(): lax.psum(shortened(attn_grads + ffn_grads), 'batch')  241 us
    dot_general x4, matrix products, one_block(): jnp.einsum('hqk,khd->qhd', grad_scores, key_rows, preferred_element_type=...  103 us
    dot_general x4, matrix products, one_block(): jnp.einsum('hqk,qhd->khd', grad_scores, query_block, preferred_element_ty...  94.9 us
    psum x1, waiting for transfers between devices, on_device(): lax.psum(jnp.dot(att_low, w_out, preferred_element_type=jnp.float32).asty...  85.6 us
    psum x1, waiting for transfers between devices, on_device(): lax.psum(jnp.dot(mixed_low, w_down, preferred_element_type=jnp.float32).a...  85 us
    dot_general x8, matrix products, block_scores(): jnp.einsum('qhd,khd->hqk', query_block, key_rows, preferred_element_type=...  57.6 us
    dot_general x7, matrix products, contract_cols(): lax.dot_general(left_side, right_side, (((1,), (1,)), ((), ())), preferre...  45 us
    reduce_scatter x1, waiting for transfers between devices, on_device(): lax.psum_scatter(part_one.astype(jnp.bfloat16), 'head', scatter_dimension...  36.9 us
  transfers between devices with their start and end apart: 8, of which 8 were waited for; matrix products, arithmetic and copies ran while one was open for 7% of the time, Pallas kernels for 0%

commit v1 on v0

v1 whole, which is shorter than its diff:
```python
import functools
import math

import jax
import jax.numpy as jnp
from jax import lax
from jax.experimental import pallas as pl
from jax.experimental.pallas import tpu as pltpu
from jax.sharding import PartitionSpec as P

HD = 64
HALF = HD // 2
VALUE_ROWS = 80
EPSILON = 1e-06
BLOCK = 256
CHUNKS = 2
F32 = jnp.float32
BF16 = jnp.bfloat16
MIB = 1024 * 1024


def dot(left, right, left_dim=1, right_dim=0):
    return lax.dot_general(
        left, right, (((left_dim,), (right_dim,)), ((), ())), preferred_element_type=F32
    )


def shape(dims, dtype):
    return jax.ShapeDtypeStruct(dims, dtype)


def whole(dims):
    return pl.BlockSpec(dims, lambda *_: (0,) * len(dims))


def params(mib):
    return pltpu.CompilerParams(vmem_limit_bytes=mib * MIB)


def cost(flops, moved):
    return pl.CostEstimate(flops=int(flops), bytes_accessed=int(moved), transcendentals=0)


def swap(value, axis, mask, size):
    return lax.ppermute(value, axis, [(i, i ^ mask) for i in range(size)])


def gather_pieces(own, size):
    pieces = {0: own}
    bit = size // 2
    while bit:
        pieces.update({e | bit: swap(p, "head", bit, size) for e, p in pieces.items()})
        bit //= 2
    return [pieces[e] for e in range(size)]


def exchange_pieces(pieces, size):
    return [pieces[0]] + [swap(pieces[e], "head", e, size) for e in range(1, size)]


def total(terms):
    if len(terms) == 1:
        return terms[0]
    return sum(t.astype(F32) for t in terms).astype(BF16)


def reduce_pieces(pieces, size):
    held = {e: [p] for e, p in enumerate(pieces)}
    bit = 1
    while bit < size:
        for e in [e for e in held if e & bit]:
            held[e ^ bit].append(swap(total(held.pop(e)), "head", bit, size))
        bit *= 2
    return held[0]


def sum_small(value, axis, size):
    bit = 1
    while bit < size:
        value = value + swap(value, axis, bit, size)
        bit *= 2
    return value


def ring_place(index, size):
    return jnp.where(index % 2 == 0, index // 2, size - 1 - index // 2)


def ring_sum(values, sign, size):
    order = list(range(0, size, 2)) + list(range(size - 1, 0, -2))
    pairs = [(order[i], order[(i + sign) % size]) for i in range(size)]
    rows = values.shape[0] // size
    place = ring_place(lax.axis_index("batch"), size)

    def take(k):
        return lax.dynamic_slice_in_dim(values, (k + 2 * size) % size * rows, rows, 0)

    held = take(place)
    for t in range(1, size):
        held = total([lax.ppermute(held, "batch", pairs), take(place - sign * t)])
    parts = [held]
    for t in range(1, size):
        parts.append(lax.ppermute(parts[-1], "batch", pairs))
    return parts


def rings(values, size, signs=(1, -1)):
    rows = values.shape[0] // len(signs)
    if size > 8 or size % 2 or rows % (16 * size):
        return lax.psum(values, "batch")
    return [
        (i * rows, sign, ring_sum(values[i * rows : (i + 1) * rows], sign, size))
        for i, sign in enumerate(signs)
    ]


def store_parts(place, plan, refs, out):
    refs = list(refs)
    for first, sign, size, rows in plan:
        for t in range(size):
            at = (place + sign * (1 - t) + 2 * size) % size
            out[pl.ds(pl.multiple_of(first + at * rows, rows), rows), :] = refs.pop(0)[...].astype(
                out.dtype
            )


def unpack(summed):
    plan = [(first, sign, len(parts), parts[0].shape[0]) for first, sign, parts in summed]
    return plan, [p for _, _, parts in summed for p in parts]


def assemble(summed, place):
    if not isinstance(summed, list):
        return summed.astype(F32)
    plan, parts = unpack(summed)
    rows, width = sum(p.shape[0] for p in parts), parts[0].shape[1]

    def body(place, *refs):
        store_parts(place[0], plan, refs[:-1], refs[-1])

    return pl.pallas_call(
        body,
        grid_spec=pltpu.PrefetchScalarGridSpec(
            num_scalar_prefetch=1,
            grid=(1,),
            in_specs=[whole(p.shape) for p in parts],
            out_specs=whole((rows, width)),
        ),
        out_shape=shape((rows, width), F32),
        compiler_params=params(32),
        cost_estimate=cost(0, rows * width * 6),
        name="assemble",
    )(place, *parts)


def assemble_turned(summed, place, info, cols, n_head):
    if isinstance(summed, list):
        plan, parts = unpack(summed)
        held = [pltpu.VMEM((4 * cols, parts[0].shape[1]), F32)]
        model = parts[0].shape[1]
    else:
        plan, parts, held = None, [summed], []
        model = summed.shape[1]
    share = model // n_head

    def body(place, info, *refs):
        refs, outs = refs[: len(parts)], refs[len(parts) :]
        if plan is None:
            source = refs[0]
        else:
            source = outs[4]
            store_parts(place[0], plan, refs, source)
        for i in range(3):
            for e in range(n_head):
                at = pl.ds(pl.multiple_of((info[0] ^ e) * share, share), share)
                block = source[i * cols : (i + 1) * cols, e * share : (e + 1) * share]
                outs[i][at, :] = block.astype(F32).T
        outs[3][...] = source[3 * cols :, :].astype(F32)

    return pl.pallas_call(
        body,
        grid_spec=pltpu.PrefetchScalarGridSpec(
            num_scalar_prefetch=2,
            grid=(1,),
            in_specs=[whole(p.shape) for p in parts],
            out_specs=[whole((model, cols))] * 3 + [whole((cols, model))],
            scratch_shapes=held,
        ),
        out_shape=[shape((model, cols), F32)] * 3 + [shape((cols, model), F32)],
        compiler_params=params(32),
        cost_estimate=cost(0, cols * model * 24),
        name="assemble_turned",
    )(place, info, *parts)


def visible(first_key, first_query, starts, length, rows, cols):
    key = first_key + lax.broadcasted_iota(jnp.int32, (rows, cols), 0)
    query = first_query + lax.broadcasted_iota(jnp.int32, (rows, cols), 1)
    last = jnp.minimum(query, length - 1)
    return (key >= starts) & ((key <= last) | (key == query))


def attend_kernel(
    chunk, n_head, heads, chunk_len, share, info, *refs
):
    refs = list(refs)
    x_refs = [refs.pop(0) for _ in range(n_head)]
    w_ref, cos_ref, sin_ref, gain_ref, start_ref = [refs.pop(0) for _ in range(5)]
    old_k, old_v = None, None
    if chunk:
        old_k, old_v = refs.pop(0), refs.pop(0)
        refs = refs[7:]
    k_ref, ve_ref, v_ref, kt_ref, qt_ref, ot_ref, inv_ref, qf_ref, kf_ref, o_ref = refs[:10]
    raw, acc = refs[10:]
    me, length = info[0], info[1]
    cols = heads * HD
    for e in range(n_head):
        first = pl.multiple_of((me ^ e) * share, share)
        for part in range(3):
            rows = slice(part * cols, (part + 1) * cols)
            term = dot(w_ref[rows, pl.ds(first, share)], x_refs[e][...], 1, 1)
            if e == 0:
                raw[rows, :] = term
            else:
                raw[rows, :] += term
    cosine, sine = cos_ref[...], sin_ref[...]
    for h in range(heads):
        own = slice(h * HD, (h + 1) * HD)
        for part, factor_ref in ((0, qf_ref), (1, kf_ref)):
            base = part * cols + h * HD
            a, b = raw[base : base + HALF, :], raw[base + HALF : base + HD, :]
            front, back = a * cosine - b * sine, b * cosine + a * sine
            mean = jnp.sum(front * front + back * back, axis=0, keepdims=True) / HD
            factor = lax.rsqrt(mean + EPSILON)
            factor_ref[h] = factor
            unit = jnp.concatenate([front, back], axis=0) * factor
            low = (unit * gain_ref[own, :]).astype(BF16)
            if part == 0:
                qt_ref[own, :] = low * BF16(1.0 / math.sqrt(HD))
            else:
                kt_ref[own, :] = low
                k_ref[h] = low.T
        value = raw[2 * cols + h * HD : 2 * cols + (h + 1) * HD, :].astype(BF16)
        v_ref[h] = value.T
        ve_ref[h, :HD, :] = value
        ve_ref[h, HD:, :] = jnp.ones((VALUE_ROWS - HD, chunk_len), BF16)

    blocks = chunk_len // BLOCK
    before = chunk * blocks

    def step(local, key_first, k_of, v_of, starts):
        query = slice(local * BLOCK, (local + 1) * BLOCK)
        mask = visible(key_first, (before + local) * BLOCK, starts, length, BLOCK, BLOCK)
        for h in range(heads):
            scores = dot(k_of(h), qt_ref[h * HD : (h + 1) * HD, query])
            probs = jnp.where(mask, jnp.exp(scores), 0.0).astype(BF16)
            acc[h] += dot(v_of(h), probs)

    for local in range(blocks):
        query = slice(local * BLOCK, (local + 1) * BLOCK)
        starts = start_ref[:, query]
        lowest = info[2 + before + local]
        acc[...] = jnp.zeros_like(acc)
        if chunk:

            @pl.loop(lowest, before)
            def _(kb):
                at = pl.ds(pl.multiple_of(kb * BLOCK, BLOCK), BLOCK)
                step(
                    local, kb * BLOCK, lambda h: old_k[h, at, :], lambda h: old_v[h, :, at], starts
                )

        @pl.loop(jnp.maximum(lowest - before, 0), local + 1)
        def _(kb):
            at = pl.ds(pl.multiple_of(kb * BLOCK, BLOCK), BLOCK)
            step(
                local,
                (before + kb) * BLOCK,
                lambda h: k_ref[h, at, :],
                lambda h: ve_ref[h, :, at],
                starts,
            )

        for h in range(heads):
            inverse = 1.0 / acc[h, HD : HD + 1, :]
            inv_ref[h, :, query] = inverse
            out = acc[h, :HD, :] * inverse
            ot_ref[h * HD : (h + 1) * HD, query] = out.astype(BF16)
            o_ref[query, h * HD : (h + 1) * HD] = out.T.astype(BF16)


def attend_chunk(chunk, x_pieces, w_t, cosine, sine, gain, starts, info, buffers, row_len):
    n_head = len(x_pieces)
    chunk_len, share = x_pieces[0].shape
    cols = w_t.shape[0] // 3
    heads = cols // HD
    model = w_t.shape[1]
    body = functools.partial(attend_kernel, chunk, n_head, heads, chunk_len, share)
    by_lane = lambda rows: pl.BlockSpec((rows, chunk_len), lambda i, info: (0, chunk))
    specs = [whole((chunk_len, share))] * n_head + [
        whole((3 * cols, model)),
        by_lane(HALF),
        by_lane(HALF),
        whole((cols, 1)),
        by_lane(1),
    ]
    operands = [*x_pieces, w_t, cosine, sine, gain, starts]
    aliases = {}
    if chunk:
        aliases = {1 + len(operands) + i: i for i in range(9)}
        specs += [whole((heads, row_len, HD)), whole((heads, VALUE_ROWS, row_len))]
        specs += [pl.BlockSpec(memory_space=pl.ANY)] * 7
        operands += buffers
    lane3 = lambda rows: pl.BlockSpec((heads, rows, chunk_len), lambda i, info: (0, 0, chunk))
    row3 = pl.BlockSpec((heads, chunk_len, HD), lambda i, info: (0, chunk, 0))
    outs = pl.pallas_call(
        body,
        grid_spec=pltpu.PrefetchScalarGridSpec(
            num_scalar_prefetch=1,
            grid=(1,),
            in_specs=specs,
            out_specs=[
                row3,
                lane3(VALUE_ROWS),
                row3,
                by_lane(cols),
                by_lane(cols),
                by_lane(cols),
                lane3(1),
                lane3(1),
                lane3(1),
                whole((chunk_len, cols)),
            ],
            scratch_shapes=[
                pltpu.VMEM((3 * cols, chunk_len), F32),
                pltpu.VMEM((heads, VALUE_ROWS, BLOCK), F32),
            ],
        ),
        out_shape=[
            shape((heads, row_len, HD), BF16),
            shape((heads, VALUE_ROWS, row_len), BF16),
            shape((heads, row_len, HD), BF16),
            shape((cols, row_len), BF16),
            shape((cols, row_len), BF16),
            shape((cols, row_len), BF16),
            shape((heads, 1, row_len), F32),
            shape((heads, 1, row_len), F32),
            shape((heads, 1, row_len), F32),
            shape((chunk_len, cols), BF16),
        ],
        input_output_aliases=aliases,
        compiler_params=params(40),
        cost_estimate=cost(16e9 / CHUNKS, 8e6),
        name="attend",
    )(info, *operands)
    return outs[:9], outs[9]


def unattend_kernel(n_head, chunks, row_len, piece, pair, info, *refs):
    refs = list(refs)
    d_refs = [refs.pop(0) for _ in range(chunks * n_head)]
    k_ref, v_ref, kt_ref, qt_ref, ot_ref, inv_ref, qf_ref, kf_ref = [refs.pop(0) for _ in range(8)]
    start_ref, cos_ref, sin_ref, gain_ref = [refs.pop(0) for _ in range(4)]
    out_ref, gain_out, do_s, inner_s, dq_s, dk_s, dv_s = refs
    me, length = info[0], info[1]
    for c in range(chunks):
        for e in range(n_head):
            first = c * n_head * piece + (me ^ e) * piece
            do_s[:, pl.ds(pl.multiple_of(first, piece), piece)] = d_refs[c * n_head + e][...]
    for h in range(pair):
        own = slice(h * HD, (h + 1) * HD)
        product = do_s[own, :].astype(F32) * ot_ref[own, :].astype(F32)
        inner_s[h] = jnp.sum(product, axis=0, keepdims=True)
    dq_s[...] = jnp.zeros_like(dq_s)
    dk_s[...] = jnp.zeros_like(dk_s)
    dv_s[...] = jnp.zeros_like(dv_s)

    @pl.loop(0, row_len // BLOCK)
    def _(qb):
        query = pl.ds(pl.multiple_of(qb * BLOCK, BLOCK), BLOCK)
        starts = start_ref[:, query]

        @pl.loop(info[2 + qb], qb + 1)
        def _(kb):
            key = pl.ds(pl.multiple_of(kb * BLOCK, BLOCK), BLOCK)
            mask = visible(kb * BLOCK, qb * BLOCK, starts, length, BLOCK, BLOCK)
            for h in range(pair):
                own = slice(h * HD, (h + 1) * HD)
                q_block, do_block = qt_ref[own, query], do_s[own, query]
                scores = dot(k_ref[h, key, :], q_block)
                probs = jnp.where(mask, jnp.exp(scores), 0.0) * inv_ref[h, :, query]
                d_probs = dot(v_ref[h, key, :], do_block)
                d_scores = (probs * (d_probs - inner_s[h, :, query])).astype(BF16)
                dv_s[own, key] += dot(do_block, probs.astype(BF16), 1, 1)
                dk_s[own, key] += dot(q_block, d_scores, 1, 1)
                dq_s[own, query] += dot(kt_ref[own, key], d_scores)

    for h in range(pair):
        own = slice(h * HD, (h + 1) * HD)
        gain = gain_ref[own, :]
        summed = jnp.zeros((HD, 1), F32)
        for part, low_ref, grad_ref, factor_ref in (
            (0, qt_ref, dq_s, qf_ref),
            (1, kt_ref, dk_s, kf_ref),
        ):
            scale = math.sqrt(HD) if part == 0 else 1.0
            unit = low_ref[own, :].astype(F32) * (scale / gain)
            grad = grad_ref[own, :]
            if part == 0:
                grad = grad * (1.0 / math.sqrt(HD))
            summed += jnp.sum(grad * unit, axis=1, keepdims=True)
            grad = grad * gain
            mean = jnp.sum(grad * unit, axis=0, keepdims=True) / HD
            grad = (grad - unit * mean) * factor_ref[h]
            front, back = grad[:HALF], grad[HALF:]
            cosine, sine = cos_ref[...], sin_ref[...]
            out_ref[part, h * HD : h * HD + HALF, :] = (front * cosine + back * sine).astype(BF16)
            out_ref[part, h * HD + HALF : (h + 1) * HD, :] = (
                back * cosine - front * sine
            ).astype(BF16)
        out_ref[2, own, :] = dv_s[own, :].astype(BF16)
        gain_out[own, :] = summed


def unattend(do_pieces, buffers, starts, cosine, sine, gain, info, n_head):
    k, _, v, kt, qt, ot, inv, qf, kf = buffers
    chunks = len(do_pieces) // n_head
    cols, piece = do_pieces[0].shape
    heads, row_len, _ = k.shape
    pair = min(2, heads)
    rows = pair * HD
    by_rows = lambda width: pl.BlockSpec((rows, width), lambda g, info: (g, 0))
    by_head = lambda a, b: pl.BlockSpec((pair, a, b), lambda g, info: (g, 0, 0))
    return pl.pallas_call(
        functools.partial(unattend_kernel, n_head, chunks, row_len, piece, pair),
        grid_spec=pltpu.PrefetchScalarGridSpec(
            num_scalar_prefetch=1,
            grid=(heads // pair,),
            in_specs=[by_rows(piece)] * (chunks * n_head)
            + [by_head(row_len, HD)] * 2
            + [by_rows(row_len)] * 3
            + [by_head(1, row_len)] * 3
            + [whole((1, row_len)), whole((HALF, row_len)), whole((HALF, row_len)), by_rows(1)],
            out_specs=[pl.BlockSpec((3, rows, row_len), lambda g, info: (0, g, 0)), by_rows(1)],
            scratch_shapes=[
                pltpu.VMEM((rows, row_len), BF16),
                pltpu.VMEM((pair, 1, row_len), F32),
                pltpu.VMEM((rows, row_len), F32),
                pltpu.VMEM((rows, row_len), F32),
                pltpu.VMEM((rows, row_len), F32),
            ],
        ),
        out_shape=[shape((3, cols, row_len), BF16), shape((cols, 1), F32)],
        compiler_params=params(40),
        cost_estimate=cost(45e9, 12e6),
        name="unattend",
    )(info, *do_pieces, k, v, kt, qt, ot, inv, qf, kf, starts, cosine, sine, gain)


def norm(values):
    factor = lax.rsqrt(jnp.mean(values * values, axis=-1, keepdims=True) + EPSILON)
    return values * factor, factor


def norm_back(grad, unit, factor):
    return factor * (grad - unit * jnp.mean(grad * unit, axis=-1, keepdims=True))


def project_kernel(n_head, share, info, *refs):
    o_refs, w_refs = refs[:n_head], refs[n_head : 2 * n_head]
    x_refs = refs[2 * n_head : 3 * n_head]
    alpha_ref, y_ref, x_ref, h_ref, low_ref = refs[3 * n_head :]
    me = info[0]
    y = dot(o_refs[0][...], w_refs[0][...])
    for e in range(1, n_head):
        y += dot(o_refs[e][...], w_refs[e][...])
    for e in range(n_head):
        first = pl.multiple_of((me ^ e) * share, share)
        x_ref[:, pl.ds(first, share)] = x_refs[e][...]
    y_ref[...] = y
    h_zero = x_ref[...].astype(F32)
    h_one, _ = norm(h_zero + alpha_ref[...] * (norm(y)[0] - h_zero))
    h_ref[...] = h_one
    low_ref[...] = h_one.astype(BF16)


def project(o_pieces, w_pieces, x_pieces, alpha, info):
    n_head = len(o_pieces)
    cols, model = w_pieces[0].shape
    chunk_len, share = x_pieces[0].shape
    rows = chunk_len // n_head
    mine = lambda width: pl.BlockSpec((rows, width), lambda i, info: (info[0], 0))
    return pl.pallas_call(
        functools.partial(project_kernel, n_head, share),
        grid_spec=pltpu.PrefetchScalarGridSpec(
            num_scalar_prefetch=1,
            grid=(1,),
            in_specs=[mine(cols)]
            + [whole((rows, cols))] * (n_head - 1)
            + [whole((cols, model))] * n_head
            + [mine(share)] * n_head
            + [whole((1, model))],
            out_specs=[whole((rows, model))] * 4,
        ),
        out_shape=[
            shape((rows, model), F32),
            shape((rows, model), BF16),
            shape((rows, model), F32),
            shape((rows, model), BF16),
        ],
        compiler_params=params(32),
        cost_estimate=cost(2.0 * rows * model * model, 6e6),
        name="project",
    )(info, *o_pieces, *w_pieces, *x_pieces, alpha)


def feed_kernel(n_head, rows, refs_in, *refs):
    h_refs = (refs_in, *refs[: n_head - 1])
    refs = refs[n_head - 1 :]
    up_ref, gate_ref, down_ref, su_ref, sg_ref, m_ref, u_ref, g_ref, cat_ref = refs[:9]
    z_refs, acc = refs[9 : 9 + n_head], refs[9 + n_head]
    tile = pl.program_id(0)

    @pl.when(tile == 0)
    def _():
        for e in range(n_head):
            cat_ref[e * rows : (e + 1) * rows, :] = h_refs[e][...]

    up_raw = dot(cat_ref[...], up_ref[...])
    gate_raw = dot(cat_ref[...], gate_ref[...])
    u_ref[...] = up_raw.astype(BF16)
    g_ref[...] = gate_raw.astype(BF16)
    gate = gate_raw * sg_ref[...]
    mixed = (up_raw * su_ref[...] * (gate * jax.nn.sigmoid(gate))).astype(BF16)
    m_ref[...] = mixed
    term = dot(mixed, down_ref[...])

    @pl.when(tile == 0)
    def _():
        acc[...] = term

    @pl.when(tile > 0)
    def _():
        acc[...] += term

    @pl.when(tile == pl.num_programs(0) - 1)
    def _():
        for e in range(n_head):
            z_refs[e][...] = acc[e * rows : (e + 1) * rows, :].astype(BF16)


def feed(h_pieces, w_up, w_gate, w_down, scale_up, scale_gate):
    n_head = len(h_pieces)
    rows, model = h_pieces[0].shape
    hidden = w_up.shape[1]
    tile = min(256, hidden)
    count = n_head * rows
    by_col = lambda height: pl.BlockSpec((height, tile), lambda n: (0, n))
    outs = pl.pallas_call(
        functools.partial(feed_kernel, n_head, rows),
        grid=(hidden // tile,),
        in_specs=[whole((rows, model))] * n_head
        + [
            by_col(model),
            by_col(model),
            pl.BlockSpec((tile, model), lambda n: (n, 0)),
            by_col(1),
            by_col(1),
        ],
        out_specs=[by_col(count)] * 3 + [whole((count, model))] + [whole((rows, model))] * n_head,
        out_shape=[shape((count, hidden), BF16)] * 3
        + [shape((count, model), BF16)]
        + [shape((rows, model), BF16)] * n_head,
        scratch_shapes=[pltpu.VMEM((count, model), F32)],
        compiler_params=params(48),
        cost_estimate=cost(6.0 * count * model * hidden, 20e6),
        name="feed",
    )(*h_pieces, w_up, w_gate, w_down, scale_up, scale_gate)
    return outs[:4], list(outs[4:])


def middle_kernel(n_head, n_terms, share, info, *refs):
    z_refs, c_refs = refs[:n_terms], refs[n_terms : n_terms + n_head]
    h_ref, alpha_ref = refs[n_terms + n_head : n_terms + n_head + 2]
    refs = refs[n_terms + n_head + 2 :]
    out_refs = refs[:n_head]
    dz_ref, direct_ref, grad_ref, two_s, cot_s = refs[n_head:]
    me = info[0]
    z = z_refs[0][...].astype(F32)
    for r in z_refs[1:]:
        z += r[...].astype(F32)
    h_one, alpha = h_ref[...], alpha_ref[...]
    h_ffn, z_factor = norm(z)
    h_two, factor = norm(h_one + alpha * (h_ffn - h_one))
    two_s[...] = h_two.astype(BF16)
    for e in range(n_head):
        at = pl.ds(pl.multiple_of((me ^ e) * share, share), share)
        out_refs[e][...] = two_s[:, at]
        cot_s[:, at] = c_refs[e][...]
    grad = norm_back(cot_s[...].astype(F32), h_two, factor)
    grad_ref[...] = jnp.sum(grad * (h_ffn - h_one), axis=0, keepdims=True)
    direct_ref[...] = grad * (1.0 - alpha)
    dz_ref[...] = norm_back(grad * alpha, h_ffn, z_factor).astype(BF16)


def middle(z_terms, cot_pieces, h_one, alpha, info):
    n_head, n_terms = len(cot_pieces), len(z_terms)
    rows, model = h_one.shape
    share = cot_pieces[0].shape[1]
    mine = pl.BlockSpec((rows, share), lambda i, info: (info[0], 0))
    outs = pl.pallas_call(
        functools.partial(middle_kernel, n_head, n_terms, share),
        grid_spec=pltpu.PrefetchScalarGridSpec(
            num_scalar_prefetch=1,
            grid=(1,),
            in_specs=[whole((rows, model))] * n_terms
            + [mine]
            + [whole((rows, share))] * (n_head - 1)
            + [whole((rows, model)), whole((1, model))],
            out_specs=[whole((rows, share))] * n_head
            + [whole((rows, model))] * 2
            + [whole((1, model))],
            scratch_shapes=[pltpu.VMEM((rows, model), BF16), pltpu.VMEM((rows, model), BF16)],
        ),
        out_shape=[shape((rows, share), BF16)] * n_head
        + [shape((rows, model), BF16), shape((rows, model), F32), shape((1, model), F32)],
        compiler_params=params(32),
        cost_estimate=cost(rows * model * 60, rows * model * 24),
        name="middle",
    )(info, *z_terms, *cot_pieces, h_one, alpha)
    return list(outs[:n_head]), outs[n_head], outs[n_head + 1], outs[n_head + 2]


def unfeed_kernel(n_head, rows, first_ref, *refs):
    d_refs = (first_ref, *refs[: n_head - 1])
    refs = refs[n_head - 1 :]
    u_ref, g_ref, up_ref, gate_ref, down_ref, su_ref, sg_ref = refs[:7]
    du_ref, dg_ref, cat_ref, gsu_ref, gsg_ref = refs[7:12]
    out_refs, acc = refs[12 : 12 + n_head], refs[12 + n_head]
    tile = pl.program_id(0)

    @pl.when(tile == 0)
    def _():
        for e in range(n_head):
            cat_ref[e * rows : (e + 1) * rows, :] = d_refs[e][...]

    d_mixed = dot(cat_ref[...], down_ref[...], 1, 1)
    up_raw, gate_raw = u_ref[...].astype(F32), g_ref[...].astype(F32)
    gate = gate_raw * sg_ref[...]
    sigmoid = jax.nn.sigmoid(gate)
    d_up = d_mixed * (gate * sigmoid)
    d_gate = d_mixed * (up_raw * su_ref[...]) * sigmoid * (1.0 + gate * (1.0 - sigmoid))
    gsu_ref[...] = jnp.sum(d_up * up_raw, axis=0, keepdims=True)
    gsg_ref[...] = jnp.sum(d_gate * gate_raw, axis=0, keepdims=True)
    up_low = (d_up * su_ref[...]).astype(BF16)
    gate_low = (d_gate * sg_ref[...]).astype(BF16)
    du_ref[...] = up_low
    dg_ref[...] = gate_low
    term = dot(up_low, up_ref[...], 1, 1) + dot(gate_low, gate_ref[...], 1, 1)

    @pl.when(tile == 0)
    def _():
        acc[...] = term

    @pl.when(tile > 0)
    def _():
        acc[...] += term

    @pl.when(tile == pl.num_programs(0) - 1)
    def _():
        for e in range(n_head):
            out_refs[e][...] = acc[e * rows : (e + 1) * rows, :].astype(BF16)


def unfeed(d_pieces, u, g, w_up, w_gate, w_down, scale_up, scale_gate):
    n_head = len(d_pieces)
    rows, model = d_pieces[0].shape
    hidden = w_up.shape[1]
    tile = min(256, hidden)
    count = n_head * rows
    by_col = lambda height: pl.BlockSpec((height, tile), lambda n: (0, n))
    outs = pl.pallas_call(
        functools.partial(unfeed_kernel, n_head, rows),
        grid=(hidden // tile,),
        in_specs=[whole((rows, model))] * n_head
        + [
            by_col(count),
            by_col(count),
            by_col(model),
            by_col(model),
            pl.BlockSpec((tile, model), lambda n: (n, 0)),
            by_col(1),
            by_col(1),
        ],
        out_specs=[by_col(count)] * 2
        + [whole((count, model)), by_col(1), by_col(1)]
        + [whole((rows, model))] * n_head,
        out_shape=[shape((count, hidden), BF16)] * 2
        + [shape((count, model), BF16), shape((1, hidden), F32), shape((1, hidden), F32)]
        + [shape((rows, model), BF16)] * n_head,
        scratch_shapes=[pltpu.VMEM((count, model), F32)],
        compiler_params=params(48),
        cost_estimate=cost(6.0 * count * model * hidden, 20e6),
        name="unfeed",
    )(*d_pieces, u, g, w_up, w_gate, w_down, scale_up, scale_gate)
    return outs[:5], list(outs[5:])


def unproject_kernel(n_head, n_terms, cols, *refs):
    t_refs, w_refs = refs[:n_terms], refs[n_terms : n_terms + n_head]
    direct_ref, y_ref, x_ref, alpha_ref = refs[n_terms + n_head : n_terms + n_head + 4]
    refs = refs[n_terms + n_head + 4 :]
    do_refs = refs[:n_head]
    dy_ref, zero_ref, grad_ref = refs[n_head:]
    grad = direct_ref[...]
    for r in t_refs:
        grad += r[...].astype(F32)
    alpha = alpha_ref[...]
    h_zero = x_ref[...].astype(F32)
    h_attn, y_factor = norm(y_ref[...])
    h_one, factor = norm(h_zero + alpha * (h_attn - h_zero))
    grad = norm_back(grad, h_one, factor)
    grad_ref[...] = jnp.sum(grad * (h_attn - h_zero), axis=0, keepdims=True)
    zero_ref[...] = grad * (1.0 - alpha)
    dy = norm_back(grad * alpha, h_attn, y_factor).astype(BF16)
    dy_ref[...] = dy
    for e in range(n_head):
        do_refs[e][...] = dot(w_refs[e][...], dy, 1, 1).astype(BF16)


def unproject(terms, w_pieces, direct, y, x, alpha):
    n_head, n_terms = len(w_pieces), len(terms)
    rows, model = y.shape
    cols = w_pieces[0].shape[0]
    outs = pl.pallas_call(
        functools.partial(unproject_kernel, n_head, n_terms, cols),
        grid=(1,),
        in_specs=[whole((rows, model))] * n_terms
        + [whole((cols, model))] * n_head
        + [whole((rows, model))] * 3
        + [whole((1, model))],
        out_specs=[whole((cols, rows))] * n_head
        + [whole((rows, model))] * 2
        + [whole((1, model))],
        out_shape=[shape((cols, rows), BF16)] * n_head
        + [shape((rows, model), BF16), shape((rows, model), F32), shape((1, model), F32)],
        compiler_params=params(32),
        cost_estimate=cost(2.0 * rows * model * model, 8e6),
        name="unproject",
    )(*terms, *w_pieces, direct, y, x, alpha)
    return list(outs[:n_head]), outs[n_head], outs[n_head + 1], outs[n_head + 2]


def spread_kernel(n_head, share, info, d_ref, w_ref, direct_ref, *out_refs):
    me = info[0]
    block = pl.program_id(0)
    d_all = d_ref[...].T
    for e in range(n_head):
        at = pl.ds(pl.multiple_of((me ^ e) * share, share), share)
        term = dot(d_all, w_ref[:, at])

        @pl.when(block == me)
        def _():
            out_refs[e][...] = (term + direct_ref[:, at]).astype(BF16)

        @pl.when(block != me)
        def _():
            out_refs[e][...] = term.astype(BF16)


def spread(chunk, chunk_len, d_all, w_t, direct, info, n_head):
    rows3, model = w_t.shape
    share = model // n_head
    rows = chunk_len // n_head
    return pl.pallas_call(
        functools.partial(spread_kernel, n_head, share),
        grid_spec=pltpu.PrefetchScalarGridSpec(
            num_scalar_prefetch=1,
            grid=(n_head,),
            in_specs=[
                pl.BlockSpec((rows3, rows), lambda i, info: (0, chunk * n_head + i)),
                whole((rows3, model)),
                whole((rows, model)),
            ],
            out_specs=[pl.BlockSpec((rows, share), lambda i, info: (i, 0))] * n_head,
        ),
        out_shape=[shape((chunk_len, share), BF16)] * n_head,
        compiler_params=params(32),
        cost_estimate=cost(2.0 * chunk_len * model * rows3, 8e6),
        name="spread",
    )(info, d_all, w_t, direct)


def on_device(
    n_batch,
    n_head,
    hidden_in,
    cotangent,
    doc_ids,
    lengths,
    w_query,
    w_key,
    w_value,
    w_out,
    w_up,
    w_gate,
    w_down,
    scale_qk,
    scale_up,
    scale_gate,
    alpha_attn,
    alpha_ffn,
):
    _, row_len, share = hidden_in.shape
    model = share * n_head
    cols = w_query.shape[1]
    chunk_len = row_len // CHUNKS
    rows = chunk_len // n_head
    me = lax.axis_index("head")
    chunks = range(CHUNKS)
    x_own, cot_own = hidden_in[0], cotangent[0]

    docs = doc_ids[0]
    column = jnp.arange(row_len, dtype=jnp.int32)
    starts = sum(
        jnp.where(docs > d, jnp.sum((docs == d).astype(jnp.int32)), 0) for d in range(5)
    ).astype(jnp.int32)
    position = (column - starts).astype(F32)
    frequency = 10000.0 ** (-(jnp.arange(HALF, dtype=F32) * 2.0 / HD))
    angles = frequency[:, None] * position[None, :]
    cosine, sine = jnp.cos(angles), jnp.sin(angles)
    info = jnp.concatenate(
        [me[None].astype(jnp.int32), lengths.astype(jnp.int32), starts[::BLOCK] // BLOCK]
    )
    starts = starts[None, :]
    gain = scale_qk[:, None]
    up_scale, gate_scale = scale_up[None, :], scale_gate[None, :]
    attn_alpha, ffn_alpha = alpha_attn[None, :], alpha_ffn[None, :]

    def part(values, c):
        return lax.slice_in_dim(values, c * chunk_len, (c + 1) * chunk_len, axis=0)

    def block_of(values, e):
        return lax.dynamic_slice_in_dim(values, (me ^ e) * rows, rows, 0)

    x_pieces = [gather_pieces(part(x_own, c), n_head) for c in chunks]
    w_t = jnp.concatenate([w_query.T, w_key.T, w_value.T], axis=0)
    out_pieces = gather_pieces(w_out, n_head)

    buffers = []
    state = []
    for c in chunks:
        buffers, o_chunk = attend_chunk(
            c, x_pieces[c], w_t, cosine, sine, gain, starts, info, buffers, row_len
        )
        o_pieces = exchange_pieces(
            [o_chunk] + [block_of(o_chunk, e) for e in range(1, n_head)], n_head
        )
        y, x_rows, h_one, h_low = project(o_pieces, out_pieces, x_pieces[c], attn_alpha, info)
        o_pieces[0] = block_of(o_chunk, 0)
        state.append((o_pieces, y, x_rows, h_one, h_low))
    cot_pieces = []
    for c in chunks:
        cot = part(cot_own, c)
        cot_pieces.append(
            exchange_pieces([cot] + [block_of(cot, e) for e in range(1, n_head)], n_head)
        )
    after = []
    for c in chunks:
        o_pieces, y, x_rows, h_one, h_low = state[c]
        (mixed, up_raw, gate_raw, h_cat), z_pieces = feed(
            gather_pieces(h_low, n_head), w_up, w_gate, w_down, up_scale, gate_scale
        )
        z_terms = reduce_pieces(z_pieces, n_head)
        two_pieces, dz, direct, grad_alpha_ffn = middle(
            z_terms, cot_pieces[c], h_one, ffn_alpha, info
        )
        after.append((mixed, up_raw, gate_raw, h_cat, two_pieces, dz, direct, grad_alpha_ffn))

    ffn = []
    for c in chunks:
        mixed, up_raw, gate_raw, h_cat, two_pieces, dz, direct, _ = after[c]
        (du, dg, dz_cat, gsu, gsg), dh_pieces = unfeed(
            gather_pieces(dz, n_head), up_raw, gate_raw, w_up, w_gate, w_down, up_scale, gate_scale
        )
        ffn.append((mixed, h_cat, du, dg, dz_cat, gsu, gsg, dh_pieces))

    grad_down = sum(dot(f[0], f[4], 0, 0) for f in ffn).astype(BF16)
    grad_up = sum(dot(f[1], f[2], 0, 0) for f in ffn).astype(BF16)
    grad_gate = sum(dot(f[1], f[3], 0, 0) for f in ffn).astype(BF16)
    place = ring_place(lax.axis_index("batch"), n_batch)[None].astype(jnp.int32)
    grad_down = assemble(rings(grad_down, n_batch), place)
    grad_up = assemble(rings(grad_up, n_batch, (1,)), place)
    grad_gate = assemble(rings(grad_gate, n_batch, (-1,)), place)

    do_pieces, zeros, dys, alphas = [], [], [], []
    for c in chunks:
        terms = reduce_pieces(ffn[c][7], n_head)
        _, y, x_rows, _, _ = state[c]
        pieces, dy, zero, grad_alpha_attn = unproject(
            terms, out_pieces, after[c][6], y, x_rows, attn_alpha
        )
        do_pieces += exchange_pieces(pieces, n_head)
        zeros.append(zero)
        dys.append(dy)
        alphas.append(grad_alpha_attn)

    out_terms = [
        sum(dot(state[c][0][e], dys[c], 0, 0) for c in chunks).astype(BF16) for e in range(n_head)
    ]
    grad_out = total(reduce_pieces(out_terms, n_head))

    d_all, grad_gain = unattend(
        do_pieces, buffers, starts, cosine, sine, gain, info, n_head
    )
    d_all = d_all.reshape(3 * cols, row_len)

    grad_hidden = []
    for c in chunks:
        pieces = spread(c, chunk_len, d_all, w_t, zeros[c], info, n_head)
        terms = reduce_pieces(pieces, n_head)
        grad_hidden.append(sum(t.astype(F32) for t in terms))
    grad_hidden = jnp.concatenate(grad_hidden, axis=0)[None]

    def lanes(c):
        return lax.slice_in_dim(d_all, c * chunk_len, (c + 1) * chunk_len, axis=1)

    grad_t = jnp.concatenate(
        [sum(dot(lanes(c), x_pieces[c][e]) for c in chunks) for e in range(n_head)], axis=1
    ).astype(BF16)
    grad_attn = rings(jnp.concatenate([grad_t, grad_out], axis=0), n_batch)
    grad_query, grad_key, grad_value, grad_out = assemble_turned(
        grad_attn, place, info, cols, n_head
    )

    alpha_sums = jnp.concatenate([sum(alphas), sum(a[7] for a in after)], axis=0)
    alpha_sums = sum_small(sum_small(alpha_sums, "head", n_head), "batch", n_batch)
    alpha_own = lax.dynamic_slice_in_dim(alpha_sums, me * share, share, 1)
    scale_sums = jnp.concatenate([sum(f[5] for f in ffn), sum(f[6] for f in ffn)], axis=0)
    scale_sums = sum_small(scale_sums, "batch", n_batch)
    gain_sums = sum_small(grad_gain[:, 0], "batch", n_batch)

    hidden_out = []
    for c in chunks:
        pieces = exchange_pieces(after[c][4], n_head)
        stacked = jnp.stack(pieces)
        hidden_out += [
            lax.dynamic_index_in_dim(stacked, b ^ me, 0, keepdims=False) for b in range(n_head)
        ]
    hidden_out = jnp.concatenate(hidden_out, axis=0)[None]
    return (
        hidden_out,
        grad_hidden,
        grad_query,
        grad_key,
        grad_value,
        grad_out,
        grad_up,
        grad_gate,
        grad_down,
        gain_sums,
        scale_sums[0],
        scale_sums[1],
        alpha_own[0],
        alpha_own[1],
    )


def solution(mesh):
    split = P("batch", None, "head")
    by_col, by_row, by_head = P(None, "head"), P("head", None), P("head")
    return jax.shard_map(
        functools.partial(on_device, mesh.shape["batch"], mesh.shape["head"]),
        mesh=mesh,
        in_specs=(split, split, P("batch", None), P("batch"))
        + (by_col, by_col, by_col, by_row, by_col, by_col, by_row)
        + (by_head, by_head, by_head, P(), P()),
        out_specs=(split, split, by_col, by_col, by_col, by_row, by_col, by_col, by_row)
        + (by_head,) * 5,
        check_vma=False,
    )
```

time: 1270 us -> 662 us (0.52)
  matrix products: 448 us -> 35.2 us
  waiting for transfers between devices: 545 us -> 272 us
  Pallas kernels: 0 us -> 167 us
  other arithmetic: 147 us -> 23.1 us
  starting transfers between devices: 0.75 us -> 118 us
  blocking collectives: 31.4 us -> 0 us
  loops' own time: 19.3 us -> 0 us
  local copies, waits for them, and re-layouts: 53.1 us -> 34.3 us
    dot_general x49 -> x22, matrix products: 448 us -> 35.2 us  [dot(): lax.dot_general(left, right, (((left_dim,), (right_dim,)), ((), ())), pre...]
    psum x3 -> x0, waiting for transfers between devices: 411 us -> none  [the longest x1 241 us: on_device(): lax.psum(shortened(attn_grads + ffn_grads), 'batch')]
    ppermute x0 -> x161, waiting for transfers between devices: none -> 272 us  [the longest x42 135 us: ring_sum(): held = total([lax.ppermute(held, 'batch', pairs), take(place - sign * t)])]
    pallas_call x0 -> x19, Pallas kernels: none -> 167 us  [the longest x2 38.1 us: unfeed(): pl.pallas_call(functools.partial(unfeed_kernel, n_head, rows), grid=(hidd...]
    ppermute x0 -> x161, starting transfers between devices: none -> 118 us  [the longest x77 43.1 us: swap(): return lax.ppermute(value, axis, [(i, i ^ mask) for i in range(size)])]
    reduce_scatter x2 -> x0, waiting for transfers between devices: 70.1 us -> none  [the longest x1 36.9 us: on_device(): lax.psum_scatter(part_one.astype(jnp.bfloat16), 'head', scatter_dimension...]
    all_gather x3 -> x0, waiting for transfers between devices: 62.6 us -> none  [the longest x1 29.9 us: on_device(): lax.all_gather(hidden_in, 'head', axis=2, tiled=True)]
    reduce_sum x14 -> x1, other arithmetic: 59.9 us -> 0.72 us  [on_device(): jnp.sum((docs == d).astype(jnp.int32))]
  transfers between devices with their start and end apart: 8 -> 161, of which waited for: 8 -> 74; matrix products, arithmetic and copies ran while one was open for 7% -> 10% of each run, Pallas kernels for 0% -> 25%
where the time goes in v1:
time: 662 us; the launch traced here: 653 us
  waiting for transfers between devices  272 us (41%)
  Pallas kernels  167 us (25%)
  starting transfers between devices  118 us (18%)
  matrix products  35.2 us (5%)
  local copies, waits for them, and re-layouts  34.3 us (5%)
  other arithmetic  23.1 us (3%)
    ppermute x42, waiting for transfers between devices, ring_sum(): held = total([lax.ppermute(held, 'batch', pairs), take(place - sign * t)])  135 us
    ppermute x77, waiting for transfers between devices, swap(): return lax.ppermute(value, axis, [(i, i ^ mask) for i in range(size)])  104 us
    ppermute x77, starting transfers between devices, swap(): return lax.ppermute(value, axis, [(i, i ^ mask) for i in range(size)])  43.1 us
    ppermute x42, starting transfers between devices, ring_sum(): parts.append(lax.ppermute(parts[-1], 'batch', pairs))  42.5 us
    pallas_call x2, Pallas kernels, unfeed(): pl.pallas_call(functools.partial(unfeed_kernel, n_head, rows), grid=(hidd...  38.1 us
    dot_general x22, matrix products, dot(): lax.dot_general(left, right, (((left_dim,), (right_dim,)), ((), ())), pre...  35.2 us
    ppermute x42, waiting for transfers between devices, ring_sum(): parts.append(lax.ppermute(parts[-1], 'batch', pairs))  32.7 us
    pallas_call x1, Pallas kernels, unattend(): pl.pallas_call(functools.partial(unattend_kernel, n_head, chunks, row_len...  32.5 us
  transfers between devices with their start and end apart: 161, of which 74 were waited for; matrix products, arithmetic and copies ran while one was open for 10% of the time, Pallas kernels for 25%

profile of v1, /device:TPU:8, one launch (start us, length us, event | category | flops | bytes accessed | tf_op | source)
XLA Modules:
  0.0 652.6 jit_solution(14826442485599119753)
XLA Ops:
  6.6 3.3 subtract_convert_fusion
  21.0 7.1 %collective-permute-done.7.refs_6_.refs_5_ = bf16[256,1024]{1,0:T(8,128)(2,1)S(1)} collective-permute-done((bf16[256,1024]{1,0:T(8,128)(2,1)S(1)}, bf16[256,1024]{1,0:T(8,128)(2,1)S(1)}, u32[]{:S(2)}, u32[]{:S(2)}) %collective-permute-start.7) | collective-permute-done | bytes 524320 | tf_op jit(solution)/shard_map/ppermute | solution.py:45
  28.1 10.9 %collective-permute-done.22.refs_2_.refs_10_ = bf16[1024,256]{1,0:T(8,128)(2,1)} collective-permute-done((bf16[1024,256]{1,0:T(8,128)(2,1)S(1)}, bf16[1024,256]{1,0:T(8,128)(2,1)}, u32[]{:S(2)}, u32[]{:S(2)}) %collective-permute-start.22) | collective-permute-done | bytes 524320 | tf_op jit(solution)/shard_map/ppermute | solution.py:45
  41.3 13.0 %attend.2 = (bf16[4,2048,64]{2,1,0:T(8,128)(2,1)S(1)}, bf16[4,80,2048]{2,1,0:T(8,128)(2,1)S(1)}, bf16[4,2048,64]{2,1,0:T(8,128)(2,1)S(1)}, bf16[256,2048]{1,0:T(...) custom-call(s32[10]{0:T(128)S(1)} %pad_add_fusion.info, ...), custom_call_target="tpu_custom_call" | custom-call | flops 8000000000 | bytes 8000000 | tf_op jit(solution)/shard_map/attend/pallas_call | solution.py:316
  56.5 4.8 collective-permute-done.4.refs_2_
  62.4 2.6 project.2
  68.3 19.4 %attend.3 = (bf16[4,2048,64]{2,1,0:T(8,128)(2,1)S(1)}, bf16[4,80,2048]{2,1,0:T(8,128)(2,1)S(1)}, bf16[4,2048,64]{2,1,0:T(8,128)(2,1)S(1)}, bf16[256,2048]{1,0:T(...) custom-call(s32[10]{0:T(128)S(1)} %pad_add_fusion.info, ...), custom_call_target="tpu_custom_call", output_to_operand_aliasing={{0}: (10, {}), {1}: (11, {}), {2}: (12, {}), {3}: (13, {}),... | custom-call | flops 8000000000 | bytes 8000000 | tf_op jit(solution)/shard_map/attend/pallas_call | solution.py:316
  94.1 4.9 collective-permute-done.25.refs_2_
  100.1 2.6 project.3
  106.9 13.1 %collective-permute-done.28.refs_1_ = bf16[256,1024]{1,0:T(8,128)(2,1)S(1)} collective-permute-done((bf16[256,1024]{1,0:T(8,128)(2,1)S(1)}, bf16[256,1024]{1,0:T(8,128)(2,1)S(1)}, u32[]{:S(2)}, u32[]{:S(2)}) %collective-permute-start.28) | collective-permute-done | bytes 524320 | tf_op jit(solution)/shard_map/ppermute | solution.py:45
  120.0 12.7 %feed.2 = (bf16[1024,1024]{1,0:T(8,128)(2,1)}, bf16[1024,1024]{1,0:T(8,128)(2,1)}, bf16[1024,1024]{1,0:T(8,128)(2,1)}, bf16[1024,1024]{1,0:T(8,128)(2,1)}, bf16[...) custom-call(bf16[256,1024]{1,0:T(8,128)(2,1)S(1)} %get-tuple-element, ...), custom_call_target="tpu_custom_call" | custom-call | flops 6442450944 | bytes 20000000 | tf_op jit(solution)/shard_map/feed/pallas_call | solution.py:559
  133.3 12.6 %feed.3 = (bf16[1024,1024]{1,0:T(8,128)(2,1)}, bf16[1024,1024]{1,0:T(8,128)(2,1)}, bf16[1024,1024]{1,0:T(8,128)(2,1)}, bf16[1024,1024]{1,0:T(8,128)(2,1)}, bf16[...) custom-call(bf16[256,1024]{1,0:T(8,128)(2,1)S(1)} %get-tuple-element, ...), custom_call_target="tpu_custom_call" | custom-call | flops 6442450944 | bytes 20000000 | tf_op jit(solution)/shard_map/feed/pallas_call | solution.py:559
  151.1 24.5 %collective-permute-done.16.refs_5_ = bf16[256,256]{1,0:T(8,128)(2,1)S(1)} collective-permute-done((bf16[256,256]{1,0:T(8,128)(2,1)S(1)}, bf16[256,256]{1,0:T(8,128)(2,1)S(1)}, u32[]{:S(2)}, u32[]{:S(2)}) %collective-permute-start.16) | collective-permute-done | bytes 131104 | tf_op jit(solution)/shard_map/ppermute | solution.py:45
  175.6 5.2 collective-permute-done.17.refs_6_
  182.7 2.6 middle.2
  197.5 2.9 middle.3
  203.6 5.8 collective-permute-done.38
  212.8 11.1 %collective-permute-done.49.refs_1_ = bf16[256,1024]{1,0:T(8,128)(2,1)S(1)} collective-permute-done((bf16[256,1024]{1,0:T(8,128)(2,1)S(1)}, bf16[256,1024]{1,0:T(8,128)(2,1)S(1)}, u32[]{:S(2)}, u32[]{:S(2)}) %collective-permute-start.49) | collective-permute-done | bytes 524320 | tf_op jit(solution)/shard_map/ppermute | solution.py:45
  223.9 19.5 %unfeed.2 = (bf16[1024,1024]{1,0:T(8,128)(2,1)}, bf16[1024,1024]{1,0:T(8,128)(2,1)}, bf16[1024,1024]{1,0:T(8,128)(2,1)}, f32[1,1024]{1,0:T(1,128)S(1)}, f32[1,10...) custom-call(bf16[256,1024]{1,0:T(8,128)(2,1)} %get-tuple-element.148, ...), custom_call_target="tpu_custom_call" | custom-call | flops 6442450944 | bytes 20000000 | tf_op jit(solution)/shard_map/unfeed/pallas_call | solution.py:682
  244.0 18.6 %unfeed.3 = (bf16[1024,1024]{1,0:T(8,128)(2,1)}, bf16[1024,1024]{1,0:T(8,128)(2,1)}, bf16[1024,1024]{1,0:T(8,128)(2,1)}, f32[1,1024]{1,0:T(1,128)S(1)}, f32[1,10...) custom-call(bf16[256,1024]{1,0:T(8,128)(2,1)S(1)} %get-tuple-element, ...), custom_call_target="tpu_custom_call" | custom-call | flops 6442450944 | bytes 20000000 | tf_op jit(solution)/shard_map/unfeed/pallas_call | solution.py:682
  263.2 4.2 fusion.52
  267.4 2.5 add_convert_fusion.2
  274.5 2.6 add_convert_fusion.1
  280.1 2.6 add_convert_fusion
  287.1 3.2 collective-permute-done.154
  290.3 2.6 collective-permute-start.122
  295.8 6.3 collective-permute-done.136
  302.3 6.2 collective-permute-done.108
  310.6 2.9 collective-permute-done.123
  313.5 5.6 collective-permute-done.137
  321.2 4.2 collective-permute-done.124
  325.5 6.1 collective-permute-done.138
  338.6 2.5 collective-permute-done.109
  343.5 2.6 collective-permute-start.126
  346.2 4.3 collective-permute-done.126
  350.5 6.1 collective-permute-done.140
  357.5 5.7 collective-permute-done.110
  363.6 5.1 collective-permute-done.127
  368.8 4.9 collective-permute-done.141
  373.9 4.7 collective-permute-done.128
  379.2 4.4 collective-permute-done.142
  414.3 32.5 %unattend.1 = (bf16[3,256,2048]{2,1,0:T(8,128)(2,1)S(1)}, f32[256,1]{1,0:T(8,128)S(1)}) custom-call(s32[10]{0:T(128)S(1)} %pad_add_fusion.info, bf16[256,256]{1,0:T(8,128)(2,1)S(1)} %get-tuple-element.158.refs_0_, bf16[256,256]{1,0:T(8,128)(2,1)S(1)} %collective-permute-done.45.refs_1_, bf16[256,256]{1,0:T(8,128)(2,1)S(1)} %collective-permute-done.46.refs_2_, ...), custom_call_target="tpu_custom_call" | custom-call | flops 44999999488 | bytes 12000000 | tf_op jit(solution)/shard_map/unattend/pallas_call | solution.py:434
  458.5 6.8 %spread.3 = (bf16[1024,256]{1,0:T(8,128)(2,1)S(1)}, bf16[1024,256]{1,0:T(8,128)(2,1)S(1)}, bf16[1024,256]{1,0:T(8,128)(2,1)S(1)}, bf16[1024,256]{1,0:T(8,128)(2,1)S(1)}) custom-call(s32[10]{0:T(128)S(1)} %pad_add_fusion.info, bf16[768,2048]{1,0:T(8,128)(2,1)S(1)} %bitcast.123, bf16[768,1024]{1,0:T(8,128)(2,1)S(1)} %copy-done.5, f32[256,1024]{1,0:T(8,128)S(1)} %copy-done.59), custom_call_target="tpu_custom_call" | custom-call | flops 1610612736 | bytes 8000000 | tf_op jit(solution)/shard_map/spread/pallas_call | solution.py:775
  473.6 2.6 collective-permute-done.99
  478.3 6.8 %spread.2 = (bf16[1024,256]{1,0:T(8,128)(2,1)S(1)}, bf16[1024,256]{1,0:T(8,128)(2,1)S(1)}, bf16[1024,256]{1,0:T(8,128)(2,1)S(1)}, bf16[1024,256]{1,0:T(8,128)(2,1)S(1)}) custom-call(s32[10]{0:T(128)S(1)} %pad_add_fusion.info, bf16[768,2048]{1,0:T(8,128)(2,1)S(1)} %bitcast.124, bf16[768,1024]{1,0:T(8,128)(2,1)S(1)} %copy-done.5, f32[256,1024]{1,0:T(8,128)S(1)} %copy-done.57), custom_call_target="tpu_custom_call" | custom-call | flops 1610612736 | bytes 8000000 | tf_op jit(solution)/shard_map/spread/pallas_call | solution.py:775
  503.4 4.7 collective-permute-done.114
  509.8 3.4 collective-permute-done.63
  513.2 6.2 collective-permute-done.80
  520.3 4.6 collective-permute-done.64
  525.0 4.9 collective-permute-done.81
  530.8 4.1 collective-permute-done.65
  535.2 4.6 collective-permute-done.82
  541.0 4.1 collective-permute-done.66
  545.4 4.6 collective-permute-done.83
  550.9 4.1 collective-permute-done.67
  572.5 4.0 collective-permute-done.69
  579.0 2.5 collective-permute-done.86
  589.9 3.6 collective-permute-done.101.refs_1_
  607.6 2.9 collective-permute-done.103.refs_3_
  610.9 2.8 collective-permute-done.117.refs_3_
  627.8 2.5 collective-permute-start.106
  634.2 2.6 collective-permute-done.106.refs_6_
  636.8 2.5 collective-permute-start.107
  648.9 3.4 assemble_turned.1
  (614 shorter events, 242.1 us)
Async XLA Ops:
  2.0 17.7 %collective-permute-start = (bf16[1024,256]{1,0:T(8,128)(2,1)S(1)}, bf16[1024,256]{1,0:T(8,128)(2,1)S(1)}, u32[]{:S(2)}, u32[]{:S(2)}) collective-permute-start(bf16[1024,256]{1,0:T(8,128)(2,1)S(1)} %get-tuple-element.236.refs_0_.refs_8_), channel_id=1, source_target_pairs={{0,1},{1,0},{2,3},{3,2},{4,5},{5,4},{6,7},{7,6},{8,9},{9,8},{10,11... | collective-permute-start | bytes 1572872 | tf_op jit(solution)/shard_map/ppermute | solution.py:45
  2.1 16.4 %collective-permute-start.1 = (bf16[1024,256]{1,0:T(8,128)(2,1)S(1)}, bf16[1024,256]{1,0:T(8,128)(2,1)}, u32[]{:S(2)}, u32[]{:S(2)}) collective-permute-start(bf16[1024,256]{1,0:T(8,128)(2,1)S(1)} %get-tuple-element.236.refs_0_.refs_8_), channel_id=1, source_target_pairs={{0,2},{1,3},{2,0},{3,1},{4,6},{5,7},{6,4},{7,5},{8,10},{9,11},{10,... | collective-permute-start | bytes 1572872 | tf_op jit(solution)/shard_map/ppermute | solution.py:45
  3.7 51.2 %collective-permute-start.6 = (bf16[256,1024]{1,0:T(8,128)(2,1)S(1)}, bf16[256,1024]{1,0:T(8,128)(2,1)S(1)}, u32[]{:S(2)}, u32[]{:S(2)}) collective-permute-start(bf16[256,1024]{1,0:T(8,128)(2,1)S(1)} %copy-done), channel_id=1, source_target_pairs={{0,1},{1,0},{2,3},{3,2},{4,5},{5,4},{6,7},{7,6},{8,9},{9,8},{10,11... | collective-permute-start | bytes 1572872 | tf_op jit(solution)/shard_map/ppermute | solution.py:45
  3.9 24.3 %collective-permute-start.7 = (bf16[256,1024]{1,0:T(8,128)(2,1)S(1)}, bf16[256,1024]{1,0:T(8,128)(2,1)S(1)}, u32[]{:S(2)}, u32[]{:S(2)}) collective-permute-start(bf16[256,1024]{1,0:T(8,128)(2,1)S(1)} %copy-done), channel_id=1, source_target_pairs={{0,2},{1,3},{2,0},{3,1},{4,6},{5,7},{6,4},{7,5},{8,10},{9,11},{10,... | collective-permute-start | bytes 1572872 | tf_op jit(solution)/shard_map/ppermute | solution.py:45
  4.4 34.7 %collective-permute-start.22 = (bf16[1024,256]{1,0:T(8,128)(2,1)S(1)}, bf16[1024,256]{1,0:T(8,128)(2,1)}, u32[]{:S(2)}, u32[]{:S(2)}) collective-permute-start(bf16[1024,256]{1,0:T(8,128)(2,1)S(1)} %get-tuple-element.235.refs_0_.refs_8_), channel_id=1, source_target_pairs={{0,2},{1,3},{2,0},{3,1},{4,6},{5,7},{6,4},{7,5},{8,10},{9,11},{10,... | collective-permute-start | bytes 1572872 | tf_op jit(solution)/shard_map/ppermute | solution.py:45
  18.5 20.5 %collective-permute-start.2 = (bf16[1024,256]{1,0:T(8,128)(2,1)}, bf16[1024,256]{1,0:T(8,128)(2,1)S(1)}, u32[]{:S(2)}, u32[]{:S(2)}) collective-permute-start(bf16[1024,256]{1,0:T(8,128)(2,1)} %collective-permute-done.1.refs_2_.refs_10_), channel_id=1, source_target_pairs={{0,1},{1,0},{2,3},{3,2},{4,5},{5,4},{6,7},{7,6},{8,9},{9,8},{10,11... | collective-permute-start | bytes 1572872 | tf_op jit(solution)/shard_map/ppermute | solution.py:45
  20.5 47.8 %collective-permute-start.21 = (bf16[1024,256]{1,0:T(8,128)(2,1)S(1)}, bf16[1024,256]{1,0:T(8,128)(2,1)S(1)}, u32[]{:S(2)}, u32[]{:S(2)}) collective-permute-start(bf16[1024,256]{1,0:T(8,128)(2,1)S(1)} %get-tuple-element.235.refs_0_.refs_8_), channel_id=1, source_target_pairs={{0,1},{1,0},{2,3},{3,2},{4,5},{5,4},{6,7},{7,6},{8,9},{9,8},{10,11... | collective-permute-start | bytes 1572872 | tf_op jit(solution)/shard_map/ppermute | solution.py:45
  28.1 28.3 %collective-permute-start.8 = (bf16[256,1024]{1,0:T(8,128)(2,1)S(1)}, bf16[256,1024]{1,0:T(8,128)(2,1)S(1)}, u32[]{:S(2)}, u32[]{:S(2)}) collective-permute-start(bf16[256,1024]{1,0:T(8,128)(2,1)S(1)} %collective-permute-done.7.refs_6_.refs_5_), channel_id=1, source_target_pairs={{0,1},{1,0},{2,3},{3,2},{4,5},{5,4},{6,7},{7,6},{8,9},{9,8},{10,11... | collective-permute-start | bytes 1572872 | tf_op jit(solution)/shard_map/ppermute | solution.py:45
  39.0 29.3 %collective-permute-start.23 = (bf16[1024,256]{1,0:T(8,128)(2,1)}, bf16[1024,256]{1,0:T(8,128)(2,1)S(1)}, u32[]{:S(2)}, u32[]{:S(2)}) collective-permute-start(bf16[1024,256]{1,0:T(8,128)(2,1)} %collective-permute-done.22.refs_2_.refs_10_), channel_id=1, source_target_pairs={{0,1},{1,0},{2,3},{3,2},{4,5},{5,4},{6,7},{7,6},{8,9},{9,8},{10,11... | collective-permute-start | bytes 1572872 | tf_op jit(solution)/shard_map/ppermute | solution.py:45
  66.7 39.7 %collective-permute-start.10 = (bf16[256,1024]{1,0:T(8,128)(2,1)S(1)}, bf16[256,1024]{1,0:T(8,128)(2,1)S(1)}, u32[]{:S(2)}, u32[]{:S(2)}) collective-permute-start(bf16[256,1024]{1,0:T(8,128)(2,1)S(1)} %get-tuple-element.118.refs_in), channel_id=1, source_target_pairs={{0,2},{1,3},{2,0},{3,1},{4,6},{5,7},{6,4},{7,5},{8,10},{9,11},{10,... | collective-permute-start | bytes 1572872 | tf_op jit(solution)/shard_map/ppermute | solution.py:45
  105.5 14.5 %collective-permute-start.28 = (bf16[256,1024]{1,0:T(8,128)(2,1)S(1)}, bf16[256,1024]{1,0:T(8,128)(2,1)S(1)}, u32[]{:S(2)}, u32[]{:S(2)}) collective-permute-start(bf16[256,1024]{1,0:T(8,128)(2,1)S(1)} %get-tuple-element.138.refs_in), channel_id=1, source_target_pairs={{0,2},{1,3},{2,0},{3,1},{4,6},{5,7},{6,4},{7,5},{8,10},{9,11},{10,... | collective-permute-start | bytes 1572872 | tf_op jit(solution)/shard_map/ppermute | solution.py:45
  106.0 14.0 %collective-permute-start.9 = (bf16[256,1024]{1,0:T(8,128)(2,1)S(1)}, bf16[256,1024]{1,0:T(8,128)(2,1)S(1)}, u32[]{:S(2)}, u32[]{:S(2)}) collective-permute-start(bf16[256,1024]{1,0:T(8,128)(2,1)S(1)} %get-tuple-element.118.refs_in), channel_id=1, source_target_pairs={{0,1},{1,0},{2,3},{3,2},{4,5},{5,4},{6,7},{7,6},{8,9},{9,8},{10,11... | collective-permute-start | bytes 1572872 | tf_op jit(solution)/shard_map/ppermute | solution.py:45
  106.4 13.6 %collective-permute-start.11 = (bf16[256,1024]{1,0:T(8,128)(2,1)S(1)}, bf16[256,1024]{1,0:T(8,128)(2,1)S(1)}, u32[]{:S(2)}, u32[]{:S(2)}) collective-permute-start(bf16[256,1024]{1,0:T(8,128)(2,1)S(1)} %collective-permute-done.10.refs_1_), channel_id=1, source_target_pairs={{0,1},{1,0},{2,3},{3,2},{4,5},{5,4},{6,7},{7,6},{8,9},{9,8},{10,11... | collective-permute-start | bytes 1572872 | tf_op jit(solution)/shard_map/ppermute | solution.py:45
  106.5 26.8 %collective-permute-start.27 = (bf16[256,1024]{1,0:T(8,128)(2,1)S(1)}, bf16[256,1024]{1,0:T(8,128)(2,1)S(1)}, u32[]{:S(2)}, u32[]{:S(2)}) collective-permute-start(bf16[256,1024]{1,0:T(8,128)(2,1)S(1)} %get-tuple-element.138.refs_in), channel_id=1, source_target_pairs={{0,1},{1,0},{2,3},{3,2},{4,5},{5,4},{6,7},{7,6},{8,9},{9,8},{10,11... | collective-permute-start | bytes 1572872 | tf_op jit(solution)/shard_map/ppermute | solution.py:45
  120.0 13.3 %collective-permute-start.29 = (bf16[256,1024]{1,0:T(8,128)(2,1)S(1)}, bf16[256,1024]{1,0:T(8,128)(2,1)S(1)}, u32[]{:S(2)}, u32[]{:S(2)}) collective-permute-start(bf16[256,1024]{1,0:T(8,128)(2,1)S(1)} %collective-permute-done.28.refs_1_), channel_id=1, source_target_pairs={{0,1},{1,0},{2,3},{3,2},{4,5},{5,4},{6,7},{7,6},{8,9},{9,8},{10,11... | collective-permute-start | bytes 1572872 | tf_op jit(solution)/shard_map/ppermute | solution.py:45
  132.8 14.5 %collective-permute-start.13 = (bf16[256,1024]{1,0:T(8,128)(2,1)S(1)}, bf16[256,1024]{1,0:T(8,128)(2,1)S(1)}, u32[]{:S(2)}, u32[]{:S(2)}) collective-permute-start(bf16[256,1024]{1,0:T(8,128)(2,1)S(1)} %get-tuple-element.122), channel_id=1, source_target_pairs={{0,1},{1,0},{2,3},{3,2},{4,5},{5,4},{6,7},{7,6},{8,9},{9,8},{10,11... | collective-permute-start | bytes 1572872 | tf_op jit(solution)/shard_map/ppermute | solution.py:45
  146.8 34.0 %collective-permute-start.12 = (bf16[256,1024]{1,0:T(8,128)(2,1)S(1)}, bf16[256,1024]{1,0:T(8,128)(2,1)S(1)}, u32[]{:S(2)}, u32[]{:S(2)}) collective-permute-start(bf16[256,1024]{1,0:T(8,128)(2,1)S(1)} %get-tuple-element.120), channel_id=1, source_target_pairs={{0,1},{1,0},{2,3},{3,2},{4,5},{5,4},{6,7},{7,6},{8,9},{9,8},{10,11... | collective-permute-start | bytes 1572872 | tf_op jit(solution)/shard_map/ppermute | solution.py:45
  146.9 43.3 %collective-permute-start.30 = (bf16[256,1024]{1,0:T(8,128)(2,1)S(1)}, bf16[256,1024]{1,0:T(8,128)(2,1)S(1)}, u32[]{:S(2)}, u32[]{:S(2)}) collective-permute-start(bf16[256,1024]{1,0:T(8,128)(2,1)S(1)} %get-tuple-element.140), channel_id=1, source_target_pairs={{0,1},{1,0},{2,3},{3,2},{4,5},{5,4},{6,7},{7,6},{8,9},{9,8},{10,11... | collective-permute-start | bytes 1572872 | tf_op jit(solution)/shard_map/ppermute | solution.py:45
  147.5 34.4 %collective-permute-start.14 = (bf16[256,1024]{1,0:T(8,128)(2,1)S(1)}, bf16[256,1024]{1,0:T(8,128)(2,1)S(1)}, u32[]{:S(2)}, u32[]{:S(2)}) collective-permute-start(bf16[256,1024]{1,0:T(8,128)(2,1)S(1)} %add_convert_fusion.8), channel_id=1, source_target_pairs={{0,2},{1,3},{2,0},{3,1},{4,6},{5,7},{6,4},{7,5},{8,10},{9,11},{10,... | collective-permute-start | bytes 1572872 | tf_op jit(solution)/shard_map/ppermute | solution.py:45
  149.0 43.1 %collective-permute-start.32 = (bf16[256,1024]{1,0:T(8,128)(2,1)}, bf16[256,1024]{1,0:T(8,128)(2,1)}, u32[]{:S(2)}, u32[]{:S(2)}) collective-permute-start(bf16[256,1024]{1,0:T(8,128)(2,1)} %add_convert_fusion.7), channel_id=1, source_target_pairs={{0,2},{1,3},{2,0},{3,1},{4,6},{5,7},{6,4},{7,5},{8,10},{9,11},{10,... | collective-permute-start | bytes 1572872 | tf_op jit(solution)/shard_map/ppermute | solution.py:45
  150.6 24.9 %collective-permute-start.16 = (bf16[256,256]{1,0:T(8,128)(2,1)S(1)}, bf16[256,256]{1,0:T(8,128)(2,1)S(1)}, u32[]{:S(2)}, u32[]{:S(2)}) collective-permute-start(bf16[256,256]{1,0:T(8,128)(2,1)S(1)} %get-tuple-element.244), channel_id=1, source_target_pairs={{0,2},{1,3},{2,0},{3,1},{4,6},{5,7},{6,4},{7,5},{8,10},{9,11},{10,... | collective-permute-start | bytes 393224 | tf_op jit(solution)/shard_map/ppermute | solution.py:45
  186.9 13.5 %collective-permute-start.20 = (bf16[256,256]{1,0:T(8,128)(2,1)}, bf16[256,256]{1,0:T(8,128)(2,1)}, u32[]{:S(2)}, u32[]{:S(2)}) collective-permute-start(bf16[256,256]{1,0:T(8,128)(2,1)} %get-tuple-element.127), channel_id=1, source_target_pairs={{0,3},{1,2},{2,1},{3,0},{4,7},{5,6},{6,5},{7,4},{8,11},{9,10},{10,... | collective-permute-start | bytes 393224 | tf_op jit(solution)/shard_map/ppermute | solution.py:45
  188.6 12.7 %collective-permute-start.19 = (bf16[256,256]{1,0:T(8,128)(2,1)}, bf16[256,256]{1,0:T(8,128)(2,1)}, u32[]{:S(2)}, u32[]{:S(2)}) collective-permute-start(bf16[256,256]{1,0:T(8,128)(2,1)} %get-tuple-element.126), channel_id=1, source_target_pairs={{0,2},{1,3},{2,0},{3,1},{4,6},{5,7},{6,4},{7,5},{8,10},{9,11},{10,... | collective-permute-start | bytes 393224 | tf_op jit(solution)/shard_map/ppermute | solution.py:45
  190.2 12.3 %collective-permute-start.18 = (bf16[256,256]{1,0:T(8,128)(2,1)}, bf16[256,256]{1,0:T(8,128)(2,1)}, u32[]{:S(2)}, u32[]{:S(2)}) collective-permute-start(bf16[256,256]{1,0:T(8,128)(2,1)} %get-tuple-element.125), channel_id=1, source_target_pairs={{0,1},{1,0},{2,3},{3,2},{4,5},{5,4},{6,7},{7,6},{8,9},{9,8},{10,11... | collective-permute-start | bytes 393224 | tf_op jit(solution)/shard_map/ppermute | solution.py:45
  191.0 19.2 %collective-permute-start.40 = (bf16[256,1024]{1,0:T(8,128)(2,1)}, bf16[256,1024]{1,0:T(8,128)(2,1)}, u32[]{:S(2)}, u32[]{:S(2)}) collective-permute-start(bf16[256,1024]{1,0:T(8,128)(2,1)} %get-tuple-element.148.first_ref), channel_id=1, source_target_pairs={{0,2},{1,3},{2,0},{3,1},{4,6},{5,7},{6,4},{7,5},{8,10},{9,11},{10,... | collective-permute-start | bytes 1572872 | tf_op jit(solution)/shard_map/ppermute | solution.py:45
  192.1 31.7 %collective-permute-start.39 = (bf16[256,1024]{1,0:T(8,128)(2,1)}, bf16[256,1024]{1,0:T(8,128)(2,1)S(1)}, u32[]{:S(2)}, u32[]{:S(2)}) collective-permute-start(bf16[256,1024]{1,0:T(8,128)(2,1)} %get-tuple-element.148.first_ref), channel_id=1, source_target_pairs={{0,1},{1,0},{2,3},{3,2},{4,5},{5,4},{6,7},{7,6},{8,9},{9,8},{10,11... | collective-permute-start | bytes 1572872 | tf_op jit(solution)/shard_map/ppermute | solution.py:45
  201.3 11.3 %collective-permute-start.37 = (bf16[256,256]{1,0:T(8,128)(2,1)S(1)}, bf16[256,256]{1,0:T(8,128)(2,1)S(1)}, u32[]{:S(2)}, u32[]{:S(2)}) collective-permute-start(bf16[256,256]{1,0:T(8,128)(2,1)S(1)} %get-tuple-element.146), channel_id=1, source_target_pairs={{0,2},{1,3},{2,0},{3,1},{4,6},{5,7},{6,4},{7,5},{8,10},{9,11},{10,... | collective-permute-start | bytes 393224 | tf_op jit(solution)/shard_map/ppermute | solution.py:45
  209.4 14.4 %collective-permute-start.49 = (bf16[256,1024]{1,0:T(8,128)(2,1)S(1)}, bf16[256,1024]{1,0:T(8,128)(2,1)S(1)}, u32[]{:S(2)}, u32[]{:S(2)}) collective-permute-start(bf16[256,1024]{1,0:T(8,128)(2,1)S(1)} %get-tuple-element.162.first_ref), channel_id=1, source_target_pairs={{0,2},{1,3},{2,0},{3,1},{4,6},{5,7},{6,4},{7,5},{8,10},{9,11},{10,... | collective-permute-start | bytes 1572872 | tf_op jit(solution)/shard_map/ppermute | solution.py:45
  210.2 13.7 %collective-permute-start.41 = (bf16[256,1024]{1,0:T(8,128)(2,1)}, bf16[256,1024]{1,0:T(8,128)(2,1)S(1)}, u32[]{:S(2)}, u32[]{:S(2)}) collective-permute-start(bf16[256,1024]{1,0:T(8,128)(2,1)} %collective-permute-done.40.refs_1_), channel_id=1, source_target_pairs={{0,1},{1,0},{2,3},{3,2},{4,5},{5,4},{6,7},{7,6},{8,9},{9,8},{10,11... | collective-permute-start | bytes 1572872 | tf_op jit(solution)/shard_map/ppermute | solution.py:45
  212.6 31.4 %collective-permute-start.48 = (bf16[256,1024]{1,0:T(8,128)(2,1)S(1)}, bf16[256,1024]{1,0:T(8,128)(2,1)S(1)}, u32[]{:S(2)}, u32[]{:S(2)}) collective-permute-start(bf16[256,1024]{1,0:T(8,128)(2,1)S(1)} %get-tuple-element.162.first_ref), channel_id=1, source_target_pairs={{0,1},{1,0},{2,3},{3,2},{4,5},{5,4},{6,7},{7,6},{8,9},{9,8},{10,11... | collective-permute-start | bytes 1572872 | tf_op jit(solution)/shard_map/ppermute | solution.py:45
  223.8 20.2 %collective-permute-start.50 = (bf16[256,1024]{1,0:T(8,128)(2,1)S(1)}, bf16[256,1024]{1,0:T(8,128)(2,1)S(1)}, u32[]{:S(2)}, u32[]{:S(2)}) collective-permute-start(bf16[256,1024]{1,0:T(8,128)(2,1)S(1)} %collective-permute-done.49.refs_1_), channel_id=1, source_target_pairs={{0,1},{1,0},{2,3},{3,2},{4,5},{5,4},{6,7},{7,6},{8,9},{9,8},{10,11... | collective-permute-start | bytes 1572872 | tf_op jit(solution)/shard_map/ppermute | solution.py:45
  243.4 141.1 %collective-permute-start.42 = (bf16[256,1024]{1,0:T(8,128)(2,1)S(1)}, bf16[256,1024]{1,0:T(8,128)(2,1)S(1)}, u32[]{:S(2)}, u32[]{:S(2)}) collective-permute-start(bf16[256,1024]{1,0:T(8,128)(2,1)S(1)} %get-tuple-element.152), channel_id=1, source_target_pairs={{0,1},{1,0},{2,3},{3,2},{4,5},{5,4},{6,7},{7,6},{8,9},{9,8},{10,11... | collective-permute-start | bytes 1572872 | tf_op jit(solution)/shard_map/ppermute | solution.py:45
  244.0 89.8 %collective-permute-start.43 = (bf16[256,1024]{1,0:T(8,128)(2,1)S(1)}, bf16[256,1024]{1,0:T(8,128)(2,1)S(1)}, u32[]{:S(2)}, u32[]{:S(2)}) collective-permute-start(bf16[256,1024]{1,0:T(8,128)(2,1)S(1)} %get-tuple-element.154), channel_id=1, source_target_pairs={{0,1},{1,0},{2,3},{3,2},{4,5},{5,4},{6,7},{7,6},{8,9},{9,8},{10,11... | collective-permute-start | bytes 1572872 | tf_op jit(solution)/shard_map/ppermute | solution.py:45
  262.7 125.7 %collective-permute-start.51 = (bf16[256,1024]{1,0:T(8,128)(2,1)S(1)}, bf16[256,1024]{1,0:T(8,128)(2,1)S(1)}, u32[]{:S(2)}, u32[]{:S(2)}) collective-permute-start(bf16[256,1024]{1,0:T(8,128)(2,1)S(1)} %get-tuple-element.166), channel_id=1, source_target_pairs={{0,1},{1,0},{2,3},{3,2},{4,5},{5,4},{6,7},{7,6},{8,9},{9,8},{10,11... | collective-permute-start | bytes 1572872 | tf_op jit(solution)/shard_map/ppermute | solution.py:45
  270.0 32.1 %collective-permute-start.94 = (bf16[128,1024]{1,0:T(8,128)(2,1)S(1)}, bf16[128,1024]{1,0:T(8,128)(2,1)S(1)}, u32[]{:S(2)}, u32[]{:S(2)}) collective-permute-start(bf16[128,1024]{1,0:T(8,128)(2,1)S(1)} %constant_dynamic-slice_fusion.5), channel_id=1, source_target_pairs={{0,8},{8,16},{16,24},{24,28},{28,20},{20,12},{12,4},{4,0},{1,9},{9... | collective-permute-start | bytes 786440 | tf_op jit(solution)/shard_map/ppermute | solution.py:100
  302.2 31.9 %collective-permute-start.52 = (bf16[256,1024]{1,0:T(8,128)(2,1)S(1)}, bf16[256,1024]{1,0:T(8,128)(2,1)S(1)}, u32[]{:S(2)}, u32[]{:S(2)}) collective-permute-start(bf16[256,1024]{1,0:T(8,128)(2,1)S(1)} %get-tuple-element.168), channel_id=1, source_target_pairs={{0,1},{1,0},{2,3},{3,2},{4,5},{5,4},{6,7},{7,6},{8,9},{9,8},{10,11... | collective-permute-start | bytes 1572872 | tf_op jit(solution)/shard_map/ppermute | solution.py:45
  341.1 45.3 %collective-permute-start.44 = (bf16[256,1024]{1,0:T(8,128)(2,1)S(1)}, bf16[256,1024]{1,0:T(8,128)(2,1)S(1)}, u32[]{:S(2)}, u32[]{:S(2)}) collective-permute-start(bf16[256,1024]{1,0:T(8,128)(2,1)S(1)} %add_convert_fusion.6), channel_id=1, source_target_pairs={{0,2},{1,3},{2,0},{3,1},{4,6},{5,7},{6,4},{7,5},{8,10},{9,11},{10,... | collective-permute-start | bytes 1572872 | tf_op jit(solution)/shard_map/ppermute | solution.py:45
  342.3 14.6 %collective-permute-start.96 = (bf16[128,1024]{1,0:T(8,128)(2,1)S(1)}, bf16[128,1024]{1,0:T(8,128)(2,1)S(1)}, u32[]{:S(2)}, u32[]{:S(2)}) collective-permute-start(bf16[128,1024]{1,0:T(8,128)(2,1)S(1)} %add_convert_fusion.21), channel_id=1, source_target_pairs={{0,8},{8,16},{16,24},{24,28},{28,20},{20,12},{12,4},{4,0},{1,9},{9... | collective-permute-start | bytes 786440 | tf_op jit(solution)/shard_map/ppermute | solution.py:100
  356.9 32.0 %collective-permute-start.53 = (bf16[256,1024]{1,0:T(8,128)(2,1)S(1)}, bf16[256,1024]{1,0:T(8,128)(2,1)S(1)}, u32[]{:S(2)}, u32[]{:S(2)}) collective-permute-start(bf16[256,1024]{1,0:T(8,128)(2,1)S(1)} %add_convert_fusion.5), channel_id=1, source_target_pairs={{0,2},{1,3},{2,0},{3,1},{4,6},{5,7},{6,4},{7,5},{8,10},{9,11},{10,... | collective-permute-start | bytes 1572872 | tf_op jit(solution)/shard_map/ppermute | solution.py:45
  383.6 17.9 %collective-permute-start.97 = (bf16[128,1024]{1,0:T(8,128)(2,1)S(1)}, bf16[128,1024]{1,0:T(8,128)(2,1)S(1)}, u32[]{:S(2)}, u32[]{:S(2)}) collective-permute-start(bf16[128,1024]{1,0:T(8,128)(2,1)S(1)} %add_convert_fusion.20), channel_id=1, source_target_pairs={{0,8},{8,16},{16,24},{24,28},{28,20},{20,12},{12,4},{4,0},{1,9},{9... | collective-permute-start | bytes 786440 | tf_op jit(solution)/shard_map/ppermute | solution.py:100
  384.5 18.6 %collective-permute-start.111 = (bf16[128,1024]{1,0:T(8,128)(2,1)S(1)}, bf16[128,1024]{1,0:T(8,128)(2,1)S(1)}, u32[]{:S(2)}, u32[]{:S(2)}) collective-permute-start(bf16[128,1024]{1,0:T(8,128)(2,1)S(1)} %add_convert_fusion.13), channel_id=1, source_target_pairs={{0,4},{8,0},{16,8},{24,16},{28,24},{20,28},{12,20},{4,12},{1,5},{9... | collective-permute-start | bytes 786440 | tf_op jit(solution)/shard_map/ppermute | solution.py:100
  388.3 18.6 %collective-permute-start.45 = (bf16[256,256]{1,0:T(8,128)(2,1)S(1)}, bf16[256,256]{1,0:T(8,128)(2,1)S(1)}, u32[]{:S(2)}, u32[]{:S(2)}) collective-permute-start(bf16[256,256]{1,0:T(8,128)(2,1)S(1)} %get-tuple-element.159), channel_id=1, source_target_pairs={{0,1},{1,0},{2,3},{3,2},{4,5},{5,4},{6,7},{7,6},{8,9},{9,8},{10,11... | collective-permute-start | bytes 393224 | tf_op jit(solution)/shard_map/ppermute | solution.py:45
  388.4 19.8 %collective-permute-start.46 = (bf16[256,256]{1,0:T(8,128)(2,1)S(1)}, bf16[256,256]{1,0:T(8,128)(2,1)S(1)}, u32[]{:S(2)}, u32[]{:S(2)}) collective-permute-start(bf16[256,256]{1,0:T(8,128)(2,1)S(1)} %get-tuple-element.160), channel_id=1, source_target_pairs={{0,2},{1,3},{2,0},{3,1},{4,6},{5,7},{6,4},{7,5},{8,10},{9,11},{10,... | collective-permute-start | bytes 393224 | tf_op jit(solution)/shard_map/ppermute | solution.py:45
  408.2 63.0 %collective-permute-start.78 = (bf16[256,1024]{1,0:T(8,128)(2,1)}, bf16[256,1024]{1,0:T(8,128)(2,1)}, u32[]{:S(2)}, u32[]{:S(2)}) collective-permute-start(bf16[256,1024]{1,0:T(8,128)(2,1)} %fusion.10), channel_id=1, source_target_pairs={{0,1},{1,0},{2,3},{3,2},{4,5},{5,4},{6,7},{7,6},{8,9},{9,8},{10,11... | collective-permute-start | bytes 1572872 | tf_op jit(solution)/shard_map/ppermute | solution.py:45
  408.3 92.0 %collective-permute-start.77 = (bf16[256,1024]{1,0:T(8,128)(2,1)}, bf16[256,1024]{1,0:T(8,128)(2,1)}, u32[]{:S(2)}, u32[]{:S(2)}) collective-permute-start(bf16[256,1024]{1,0:T(8,128)(2,1)} %fusion.5), channel_id=1, source_target_pairs={{0,1},{1,0},{2,3},{3,2},{4,5},{5,4},{6,7},{7,6},{8,9},{9,8},{10,11... | collective-permute-start | bytes 1572872 | tf_op jit(solution)/shard_map/ppermute | solution.py:45
  408.8 58.1 %collective-permute-start.98 = (bf16[128,1024]{1,0:T(8,128)(2,1)}, bf16[128,1024]{1,0:T(8,128)(2,1)}, u32[]{:S(2)}, u32[]{:S(2)}) collective-permute-start(bf16[128,1024]{1,0:T(8,128)(2,1)} %add_convert_fusion.19), channel_id=1, source_target_pairs={{0,8},{8,16},{16,24},{24,28},{28,20},{20,12},{12,4},{4,0},{1,9},{9... | collective-permute-start | bytes 786440 | tf_op jit(solution)/shard_map/ppermute | solution.py:100
  411.7 57.3 %collective-permute-start.112 = (bf16[128,1024]{1,0:T(8,128)(2,1)}, bf16[128,1024]{1,0:T(8,128)(2,1)}, u32[]{:S(2)}, u32[]{:S(2)}) collective-permute-start(bf16[128,1024]{1,0:T(8,128)(2,1)} %add_convert_fusion.12), channel_id=1, source_target_pairs={{0,4},{8,0},{16,8},{24,16},{28,24},{20,28},{12,20},{4,12},{1,5},{9... | collective-permute-start | bytes 786440 | tf_op jit(solution)/shard_map/ppermute | solution.py:100
  448.9 16.4 %collective-permute-start.150 = (f32[256]{0:T(256)S(1)}, f32[256]{0:T(256)S(1)}, u32[]{:S(2)}, u32[]{:S(2)}) collective-permute-start(f32[256]{0:T(256)S(1)} %reduce.5), channel_id=1, source_target_pairs={{0,4},{4,0},{8,12},{12,8},{16,20},{20,16},{24,28},{28,24},{1,5},{5... | collective-permute-start | bytes 3080 | tf_op jit(solution)/shard_map/ppermute | solution.py:45
  465.4 19.8 %collective-permute-start.151 = (f32[256]{0:T(256)S(1)}, f32[256]{0:T(256)S(1)}, u32[]{:S(2)}, u32[]{:S(2)}) collective-permute-start(f32[256]{0:T(256)S(1)} %add.771), channel_id=1, source_target_pairs={{0,8},{4,12},{8,0},{12,4},{16,24},{20,28},{24,16},{28,20},{1,9},{5... | collective-permute-start | bytes 3080 | tf_op jit(solution)/shard_map/ppermute | solution.py:45
  470.0 16.8 %collective-permute-start.113 = (bf16[128,1024]{1,0:T(8,128)(2,1)S(1)}, bf16[128,1024]{1,0:T(8,128)(2,1)S(1)}, u32[]{:S(2)}, u32[]{:S(2)}) collective-permute-start(bf16[128,1024]{1,0:T(8,128)(2,1)S(1)} %add_convert_fusion.11), channel_id=1, source_target_pairs={{0,4},{8,0},{16,8},{24,16},{28,24},{20,28},{12,20},{4,12},{1,5},{9... | collective-permute-start | bytes 786440 | tf_op jit(solution)/shard_map/ppermute | solution.py:100
  472.7 27.6 %collective-permute-start.79 = (bf16[256,1024]{1,0:T(8,128)(2,1)S(1)}, bf16[256,1024]{1,0:T(8,128)(2,1)S(1)}, u32[]{:S(2)}, u32[]{:S(2)}) collective-permute-start(bf16[256,1024]{1,0:T(8,128)(2,1)S(1)} %fusion.9), channel_id=1, source_target_pairs={{0,2},{1,3},{2,0},{3,1},{4,6},{5,7},{6,4},{7,5},{8,10},{9,11},{10,... | collective-permute-start | bytes 1572872 | tf_op jit(solution)/shard_map/ppermute | solution.py:45
  477.3 15.4 %collective-permute-start.100 = (bf16[128,1024]{1,0:T(8,128)(2,1)S(1)}, bf16[128,1024]{1,0:T(8,128)(2,1)S(1)}, u32[]{:S(2)}, u32[]{:S(2)}) collective-permute-start(bf16[128,1024]{1,0:T(8,128)(2,1)S(1)} %add_convert_fusion.17), channel_id=1, source_target_pairs={{0,8},{8,16},{16,24},{24,28},{28,20},{20,12},{12,4},{4,0},{1,9},{9... | collective-permute-start | bytes 786440 | tf_op jit(solution)/shard_map/ppermute | solution.py:100
  490.2 65.2 %collective-permute-start.155 = (f32[2,1024]{1,0:T(2,128)S(1)}, f32[2,1024]{1,0:T(2,128)S(1)}, u32[]{:S(2)}, u32[]{:S(2)}) collective-permute-start(f32[2,1024]{1,0:T(2,128)S(1)} %copy-done.91), channel_id=1, source_target_pairs={{0,16},{4,20},{8,24},{12,28},{16,0},{20,4},{24,8},{28,12},{1,17},{... | collective-permute-start | bytes 24584 | tf_op jit(solution)/shard_map/ppermute | solution.py:45
  497.3 63.6 %collective-permute-start.160 = (f32[2,1024]{1,0:T(2,128)S(1)}, f32[2,1024]{1,0:T(2,128)S(1)}, u32[]{:S(2)}, u32[]{:S(2)}) collective-permute-start(f32[2,1024]{1,0:T(2,128)S(1)} %add.784), channel_id=1, source_target_pairs={{0,16},{4,20},{8,24},{12,28},{16,0},{20,4},{24,8},{28,12},{1,17},{... | collective-permute-start | bytes 24584 | tf_op jit(solution)/shard_map/ppermute | solution.py:45
  498.1 57.4 %collective-permute-start.131 = (bf16[64,1024]{1,0:T(8,128)(2,1)S(1)}, bf16[64,1024]{1,0:T(8,128)(2,1)S(1)}, u32[]{:S(2)}, u32[]{:S(2)}) collective-permute-start(bf16[64,1024]{1,0:T(8,128)(2,1)S(1)} %collective-permute-done.130.refs_2_), channel_id=1, source_target_pairs={{0,8},{8,16},{16,24},{24,28},{28,20},{20,12},{12,4},{4,0},{1,9},{9... | collective-permute-start | bytes 393224 | tf_op jit(solution)/shard_map/ppermute | solution.py:103
  500.3 56.9 %collective-permute-start.145 = (bf16[64,1024]{1,0:T(8,128)(2,1)S(1)}, bf16[64,1024]{1,0:T(8,128)(2,1)S(1)}, u32[]{:S(2)}, u32[]{:S(2)}) collective-permute-start(bf16[64,1024]{1,0:T(8,128)(2,1)S(1)} %collective-permute-done.144.refs_10_), channel_id=1, source_target_pairs={{0,4},{8,0},{16,8},{24,16},{28,24},{20,28},{12,20},{4,12},{1,5},{9... | collective-permute-start | bytes 393224 | tf_op jit(solution)/shard_map/ppermute | solution.py:103
  555.4 16.2 %collective-permute-start.61 = (bf16[1024,256]{1,0:T(8,128)(2,1)S(1)}, bf16[1024,256]{1,0:T(8,128)(2,1)S(1)}, u32[]{:S(2)}, u32[]{:S(2)}) collective-permute-start(bf16[1024,256]{1,0:T(8,128)(2,1)S(1)} %get-tuple-element.194), channel_id=1, source_target_pairs={{0,1},{1,0},{2,3},{3,2},{4,5},{5,4},{6,7},{7,6},{8,9},{9,8},{10,11... | collective-permute-start | bytes 1572872 | tf_op jit(solution)/shard_map/ppermute | solution.py:45
  566.3 18.0 %collective-permute-start.60 = (bf16[1024,256]{1,0:T(8,128)(2,1)S(1)}, bf16[1024,256]{1,0:T(8,128)(2,1)S(1)}, u32[]{:S(2)}, u32[]{:S(2)}) collective-permute-start(bf16[1024,256]{1,0:T(8,128)(2,1)S(1)} %get-tuple-element.192), channel_id=1, source_target_pairs={{0,1},{1,0},{2,3},{3,2},{4,5},{5,4},{6,7},{7,6},{8,9},{9,8},{10,11... | collective-permute-start | bytes 1572872 | tf_op jit(solution)/shard_map/ppermute | solution.py:45
  567.7 18.1 %collective-permute-start.58 = (bf16[1024,256]{1,0:T(8,128)(2,1)S(1)}, bf16[1024,256]{1,0:T(8,128)(2,1)S(1)}, u32[]{:S(2)}, u32[]{:S(2)}) collective-permute-start(bf16[1024,256]{1,0:T(8,128)(2,1)S(1)} %get-tuple-element.189), channel_id=1, source_target_pairs={{0,1},{1,0},{2,3},{3,2},{4,5},{5,4},{6,7},{7,6},{8,9},{9,8},{10,11... | collective-permute-start | bytes 1572872 | tf_op jit(solution)/shard_map/ppermute | solution.py:45
  569.2 17.1 %collective-permute-start.57 = (bf16[1024,256]{1,0:T(8,128)(2,1)S(1)}, bf16[1024,256]{1,0:T(8,128)(2,1)S(1)}, u32[]{:S(2)}, u32[]{:S(2)}) collective-permute-start(bf16[1024,256]{1,0:T(8,128)(2,1)S(1)} %get-tuple-element.187), channel_id=1, source_target_pairs={{0,1},{1,0},{2,3},{3,2},{4,5},{5,4},{6,7},{7,6},{8,9},{9,8},{10,11... | collective-permute-start | bytes 1572872 | tf_op jit(solution)/shard_map/ppermute | solution.py:45
  586.3 11.0 %collective-permute-start.70 = (bf16[64,1024]{1,0:T(8,128)(2,1)S(1)}, bf16[64,1024]{1,0:T(8,128)(2,1)S(1)}, u32[]{:S(2)}, u32[]{:S(2)}) collective-permute-start(bf16[64,1024]{1,0:T(8,128)(2,1)S(1)} %add_convert_fusion.44.refs_0_), channel_id=1, source_target_pairs={{0,8},{8,16},{16,24},{24,28},{28,20},{20,12},{12,4},{4,0},{1,9},{9... | collective-permute-start | bytes 393224 | tf_op jit(solution)/shard_map/ppermute | solution.py:103
  587.9 11.0 %collective-permute-start.87 = (bf16[64,1024]{1,0:T(8,128)(2,1)S(1)}, bf16[64,1024]{1,0:T(8,128)(2,1)S(1)}, u32[]{:S(2)}, u32[]{:S(2)}) collective-permute-start(bf16[64,1024]{1,0:T(8,128)(2,1)S(1)} %add_convert_fusion.37.refs_8_), channel_id=1, source_target_pairs={{0,4},{8,0},{16,8},{24,16},{28,24},{20,28},{12,20},{4,12},{1,5},{9... | collective-permute-start | bytes 393224 | tf_op jit(solution)/shard_map/ppermute | solution.py:103
  589.9 17.3 %collective-permute-start.62 = (bf16[1024,256]{1,0:T(8,128)(2,1)S(1)}, bf16[1024,256]{1,0:T(8,128)(2,1)S(1)}, u32[]{:S(2)}, u32[]{:S(2)}) collective-permute-start(bf16[1024,256]{1,0:T(8,128)(2,1)S(1)} %add_convert_fusion.3), channel_id=1, source_target_pairs={{0,2},{1,3},{2,0},{3,1},{4,6},{5,7},{6,4},{7,5},{8,10},{9,11},{10,... | collective-permute-start | bytes 1572872 | tf_op jit(solution)/shard_map/ppermute | solution.py:45
  607.3 26.7 %collective-permute-start.59 = (bf16[1024,256]{1,0:T(8,128)(2,1)S(1)}, bf16[1024,256]{1,0:T(8,128)(2,1)S(1)}, u32[]{:S(2)}, u32[]{:S(2)}) collective-permute-start(bf16[1024,256]{1,0:T(8,128)(2,1)S(1)} %add_convert_fusion.4), channel_id=1, source_target_pairs={{0,2},{1,3},{2,0},{3,1},{4,6},{5,7},{6,4},{7,5},{8,10},{9,11},{10,... | collective-permute-start | bytes 1572872 | tf_op jit(solution)/shard_map/ppermute | solution.py:45
  (201 other events, 2026.4 us)

commit v2 on v1

--- a/solution.py
+++ b/solution.py
@@ -29,6 +29,15 @@
     return jax.ShapeDtypeStruct(dims, dtype)
 
 
+def kept_shape(dims, dtype):
+    return pltpu.HBM(dims, dtype)
+
+
+def after(value, *others):
+    others = [o for o in others if o is not None]
+    return lax.optimization_barrier((value, *others))[0] if others else value
+
+
 def whole(dims):
     return pl.BlockSpec(dims, lambda *_: (0,) * len(dims))
 
@@ -38,19 +47,38 @@
 
 
 def cost(flops, moved):
-    return pl.CostEstimate(flops=int(flops), bytes_accessed=int(moved), transcendentals=0)
+    return pl.CostEstimate(flops=1, bytes_accessed=1, transcendentals=0)
+
+
+class Order:
+    def __init__(self):
+        self.last = None
+
+    def run(self, step, value, *rest, need=()):
+        out = step(after(value, self.last, *need), *rest)
+        self.last = jax.tree.leaves(out)[0]
+        return out
+
+    def land(self, values):
+        return jax.tree.map(lambda v: after(v, self.last), values)
 
 
 def swap(value, axis, mask, size):
     return lax.ppermute(value, axis, [(i, i ^ mask) for i in range(size)])
 
 
-def gather_pieces(own, size):
+def gather_far(own, size):
     pieces = {0: own}
     bit = size // 2
-    while bit:
+    while bit > 1:
         pieces.update({e | bit: swap(p, "head", bit, size) for e, p in pieces.items()})
         bit //= 2
+    return pieces
+
+
+def gather_near(far, size):
+    pieces = dict(far)
+    pieces.update({e | 1: swap(p, "head", 1, size) for e, p in far.items()})
     return [pieces[e] for e in range(size)]
 
 
@@ -69,9 +97,10 @@
     bit = 1
     while bit < size:
         for e in [e for e in held if e & bit]:
-            held[e ^ bit].append(swap(total(held.pop(e)), "head", bit, size))
+            sent = total(held.pop(e))
+            held[e ^ bit].append(swap(sent, "head", bit, size))
         bit *= 2
-    return held[0]
+    return held[0], sent
 
 
 def sum_small(value, axis, size):
@@ -82,115 +111,132 @@
     return value
 
 
-def ring_place(index, size):
-    return jnp.where(index % 2 == 0, index // 2, size - 1 - index // 2)
-
-
-def ring_sum(values, sign, size):
-    order = list(range(0, size, 2)) + list(range(size - 1, 0, -2))
-    pairs = [(order[i], order[(i + sign) % size]) for i in range(size)]
-    rows = values.shape[0] // size
-    place = ring_place(lax.axis_index("batch"), size)
-
-    def take(k):
-        return lax.dynamic_slice_in_dim(values, (k + 2 * size) % size * rows, rows, 0)
-
-    held = take(place)
-    for t in range(1, size):
-        held = total([lax.ppermute(held, "batch", pairs), take(place - sign * t)])
-    parts = [held]
-    for t in range(1, size):
-        parts.append(lax.ppermute(parts[-1], "batch", pairs))
-    return parts
-
-
-def rings(values, size, signs=(1, -1)):
-    rows = values.shape[0] // len(signs)
-    if size > 8 or size % 2 or rows % (16 * size):
-        return lax.psum(values, "batch")
-    return [
-        (i * rows, sign, ring_sum(values[i * rows : (i + 1) * rows], sign, size))
-        for i, sign in enumerate(signs)
-    ]
-
-
-def store_parts(place, plan, refs, out):
-    refs = list(refs)
-    for first, sign, size, rows in plan:
-        for t in range(size):
-            at = (place + sign * (1 - t) + 2 * size) % size
-            out[pl.ds(pl.multiple_of(first + at * rows, rows), rows), :] = refs.pop(0)[...].astype(
-                out.dtype
-            )
-
-
-def unpack(summed):
-    plan = [(first, sign, len(parts), parts[0].shape[0]) for first, sign, parts in summed]
-    return plan, [p for _, _, parts in summed for p in parts]
+class BatchSum:
+    def __init__(self, values, size):
+        self.size = size
+        self.place = lax.axis_index("batch")
+        bits = [1 << i for i in range(size.bit_length() - 1)]
+        if size == 8:
+            self.bits = bits[:1]
+            self.todo = [("halve", 1), ("in", 0), ("across", 0), ("out", 0), ("join", 1)]
+        else:
+            self.bits = bits
+            self.todo = [("halve", b) for b in bits] + [("join", b) for b in reversed(bits)]
+        self.values, self.mine, self.flying, self.sent = values, None, None, None
+        self.start()
+
+    def start(self):
+        kind, bit = self.todo[0]
+        self.sent = self.values
+        if kind == "halve":
+            rows = self.values.shape[0] // 2
+            own = (self.place & bit) // bit
+            self.mine = lax.dynamic_slice_in_dim(self.values, own * rows, rows, 0)
+            self.sent = lax.dynamic_slice_in_dim(self.values, (1 - own) * rows, rows, 0)
+        if kind in ("halve", "join"):
+            self.flying = swap(self.sent, "batch", bit, self.size)
+        else:
+            hops = {"in": [(0, 1), (3, 2)], "across": [(1, 2), (2, 1)], "out": [(1, 0), (2, 3)]}[kind]
+            pairs = [(2 * a + i, 2 * b + i) for a, b in hops for i in range(2)]
+            self.flying = lax.ppermute(self.sent, "batch", pairs)
+
+    def advance(self, order=None):
+        if not self.todo:
+            return []
+        got = order.land(self.flying) if order else self.flying
+        kind, _ = self.todo.pop(0)
+        if not self.todo:
+            self.parts = [self.values, got]
+            return []
+        if kind == "halve":
+            self.values = total([self.mine, got])
+        elif kind == "join":
+            self.values = jnp.concatenate([self.values, got], axis=0)
+        elif kind == "out":
+            row = self.place // 2
+            self.values = jnp.where((row == 1) | (row == 2), self.values, got)
+        else:
+            self.values = total([self.values, got])
+        self.start()
+        return [self.sent]
+
+    def finish(self):
+        while self.todo:
+            self.advance()
+        return self.parts, self.bits
+
+
+def store_blocks(place, summed, refs, out):
+    (first, _), bits = summed
+    count = 1 << len(bits)
+    rows = 2 * first.shape[0] // count
+    for p in range(count):
+        at = 0
+        for level, bit in enumerate(bits):
+            other = p >> (len(bits) - 1 - level) & 1
+            at = at + (((place // bit) % 2) ^ other) * ((count >> (level + 1)) * rows)
+        ref, row = refs[p * 2 // count], (p % (count // 2)) * rows
+        out[pl.ds(pl.multiple_of(at, rows), rows), :] = ref[row : row + rows, :].astype(out.dtype)
 
 
 def assemble(summed, place):
-    if not isinstance(summed, list):
-        return summed.astype(F32)
-    plan, parts = unpack(summed)
-    rows, width = sum(p.shape[0] for p in parts), parts[0].shape[1]
-
-    def body(place, *refs):
-        store_parts(place[0], plan, refs[:-1], refs[-1])
+    parts, _ = summed
+    rows, width = parts[0].shape
+
+    def body(place, own_ref, other_ref, out):
+        store_blocks(place[0], summed, (own_ref, other_ref), out)
 
     return pl.pallas_call(
         body,
         grid_spec=pltpu.PrefetchScalarGridSpec(
             num_scalar_prefetch=1,
             grid=(1,),
-            in_specs=[whole(p.shape) for p in parts],
-            out_specs=whole((rows, width)),
+            in_specs=[whole((rows, width))] * 2,
+            out_specs=whole((2 * rows, width)),
         ),
-        out_shape=shape((rows, width), F32),
-        compiler_params=params(32),
-        cost_estimate=cost(0, rows * width * 6),
+        out_shape=shape((2 * rows, width), F32),
+        compiler_params=params(24),
+        cost_estimate=cost(0, rows * width * 12),
         name="assemble",
     )(place, *parts)
 
 
-def assemble_turned(summed, place, info, cols, n_head):
-    if isinstance(summed, list):
-        plan, parts = unpack(summed)
-        held = [pltpu.VMEM((4 * cols, parts[0].shape[1]), F32)]
-        model = parts[0].shape[1]
-    else:
-        plan, parts, held = None, [summed], []
-        model = summed.shape[1]
+def assemble_turned(sums, place, info, cols, n_head, out_rows, small_rows):
+    pairs = len(sums)
+    width = cols // pairs
+    model = sums[0][0][0].shape[1]
     share = model // n_head
+    counts = [2 * parts[0].shape[0] for parts, _ in sums]
 
     def body(place, info, *refs):
-        refs, outs = refs[: len(parts)], refs[len(parts) :]
-        if plan is None:
-            source = refs[0]
-        else:
-            source = outs[4]
-            store_parts(place[0], plan, refs, source)
-        for i in range(3):
-            for e in range(n_head):
-                at = pl.ds(pl.multiple_of((info[0] ^ e) * share, share), share)
-                block = source[i * cols : (i + 1) * cols, e * share : (e + 1) * share]
-                outs[i][at, :] = block.astype(F32).T
-        outs[3][...] = source[3 * cols :, :].astype(F32)
-
+        ins, outs, held = refs[: 2 * pairs], refs[2 * pairs : 2 * pairs + 5], refs[2 * pairs + 5 :]
+        for g in range(pairs):
+            store_blocks(place[0], sums[g], ins[2 * g : 2 * g + 2], held[g])
+            for i in range(3):
+                for e in range(n_head):
+                    at = pl.ds(pl.multiple_of((info[0] ^ e) * share, share), share)
+                    block = held[g][i * width : (i + 1) * width, e * share : (e + 1) * share]
+                    outs[i][at, g * width : (g + 1) * width] = block.T
+        outs[3][...] = held[pairs - 1][3 * width : 3 * width + out_rows, :]
+        first = 3 * width + out_rows
+        outs[4][...] = held[pairs - 1][first : first + small_rows, :]
+
+    flat = [part for parts, _ in sums for part in parts]
     return pl.pallas_call(
         body,
         grid_spec=pltpu.PrefetchScalarGridSpec(
             num_scalar_prefetch=2,
             grid=(1,),
-            in_specs=[whole(p.shape) for p in parts],
-            out_specs=[whole((model, cols))] * 3 + [whole((cols, model))],
-            scratch_shapes=held,
+            in_specs=[whole(h.shape) for h in flat],
+            out_specs=[whole((model, cols))] * 3 + [whole((out_rows, model)), whole((small_rows, model))],
+            scratch_shapes=[pltpu.VMEM((n, model), F32) for n in counts],
         ),
-        out_shape=[shape((model, cols), F32)] * 3 + [shape((cols, model), F32)],
+        out_shape=[shape((model, cols), F32)] * 3
+        + [shape((out_rows, model), F32), shape((small_rows, model), F32)],
         compiler_params=params(32),
         cost_estimate=cost(0, cols * model * 24),
         name="assemble_turned",
-    )(place, info, *parts)
+    )(place, info, *flat)
 
 
 def visible(first_key, first_query, starts, length, rows, cols):
@@ -198,6 +244,27 @@
     query = first_query + lax.broadcasted_iota(jnp.int32, (rows, cols), 1)
     last = jnp.minimum(query, length - 1)
     return (key >= starts) & ((key <= last) | (key == query))
+
+
+def turn(w_query, w_key, w_value, pair):
+    model, cols = w_query.shape
+
+    def body(q_ref, k_ref, v_ref, out):
+        for g in range(cols // pair):
+            for i, ref in enumerate((q_ref, k_ref, v_ref)):
+                first = (3 * g + i) * pair
+                out[first : first + pair, :] = ref[:, g * pair : (g + 1) * pair].T
+
+    return pl.pallas_call(
+        body,
+        in_specs=[whole((model, cols))] * 3,
+        out_specs=whole((3 * cols, model)),
+        grid=(1,),
+        out_shape=shape((3 * cols, model), BF16),
+        compiler_params=params(24),
+        cost_estimate=cost(0, 12 * cols * model),
+        name="turn",
+    )(w_query, w_key, w_value)
 
 
 def attend_kernel(
@@ -214,20 +281,25 @@
     raw, acc = refs[10:]
     me, length = info[0], info[1]
     cols = heads * HD
+    pair = min(2, heads)
     for e in range(n_head):
         first = pl.multiple_of((me ^ e) * share, share)
-        for part in range(3):
-            rows = slice(part * cols, (part + 1) * cols)
+        for third in range(3):
+            rows = slice(third * cols, (third + 1) * cols)
             term = dot(w_ref[rows, pl.ds(first, share)], x_refs[e][...], 1, 1)
             if e == 0:
                 raw[rows, :] = term
             else:
                 raw[rows, :] += term
+
+    def raw_row(part, h):
+        return ((h // pair * 3 + part) * pair + h % pair) * HD
+
     cosine, sine = cos_ref[...], sin_ref[...]
     for h in range(heads):
         own = slice(h * HD, (h + 1) * HD)
         for part, factor_ref in ((0, qf_ref), (1, kf_ref)):
-            base = part * cols + h * HD
+            base = raw_row(part, h)
             a, b = raw[base : base + HALF, :], raw[base + HALF : base + HD, :]
             front, back = a * cosine - b * sine, b * cosine + a * sine
             mean = jnp.sum(front * front + back * back, axis=0, keepdims=True) / HD
@@ -240,7 +312,7 @@
             else:
                 kt_ref[own, :] = low
                 k_ref[h] = low.T
-        value = raw[2 * cols + h * HD : 2 * cols + (h + 1) * HD, :].astype(BF16)
+        value = raw[raw_row(2, h) : raw_row(2, h) + HD, :].astype(BF16)
         v_ref[h] = value.T
         ve_ref[h, :HD, :] = value
         ve_ref[h, HD:, :] = jnp.ones((VALUE_ROWS - HD, chunk_len), BF16)
@@ -289,9 +361,11 @@
             o_ref[query, h * HD : (h + 1) * HD] = out.T.astype(BF16)
 
 
-def attend_chunk(chunk, x_pieces, w_t, cosine, sine, gain, starts, info, buffers, row_len):
+def attend_chunk(
+    chunk, x_pieces, w_t, cosine, sine, gain, starts, info, buffers, row_len, chunk_len
+):
     n_head = len(x_pieces)
-    chunk_len, share = x_pieces[0].shape
+    share = x_pieces[0].shape[1]
     cols = w_t.shape[0] // 3
     heads = cols // HD
     model = w_t.shape[1]
@@ -337,15 +411,15 @@
             ],
         ),
         out_shape=[
-            shape((heads, row_len, HD), BF16),
-            shape((heads, VALUE_ROWS, row_len), BF16),
-            shape((heads, row_len, HD), BF16),
-            shape((cols, row_len), BF16),
-            shape((cols, row_len), BF16),
-            shape((cols, row_len), BF16),
-            shape((heads, 1, row_len), F32),
-            shape((heads, 1, row_len), F32),
-            shape((heads, 1, row_len), F32),
+            kept_shape((heads, row_len, HD), BF16),
+            kept_shape((heads, VALUE_ROWS, row_len), BF16),
+            kept_shape((heads, row_len, HD), BF16),
+            kept_shape((cols, row_len), BF16),
+            kept_shape((cols, row_len), BF16),
+            kept_shape((cols, row_len), BF16),
+            kept_shape((heads, 1, row_len), F32),
+            kept_shape((heads, 1, row_len), F32),
+            kept_shape((heads, 1, row_len), F32),
             shape((chunk_len, cols), BF16),
         ],
         input_output_aliases=aliases,
@@ -422,26 +496,26 @@
         gain_out[own, :] = summed
 
 
-def unattend(do_pieces, buffers, starts, cosine, sine, gain, info, n_head):
+def unattend(index, do_pieces, buffers, starts, cosine, sine, gain, info, n_head):
     k, _, v, kt, qt, ot, inv, qf, kf = buffers
     chunks = len(do_pieces) // n_head
     cols, piece = do_pieces[0].shape
     heads, row_len, _ = k.shape
     pair = min(2, heads)
     rows = pair * HD
-    by_rows = lambda width: pl.BlockSpec((rows, width), lambda g, info: (g, 0))
-    by_head = lambda a, b: pl.BlockSpec((pair, a, b), lambda g, info: (g, 0, 0))
+    by_rows = lambda width: pl.BlockSpec((rows, width), lambda g, info: (index, 0))
+    by_head = lambda a, b: pl.BlockSpec((pair, a, b), lambda g, info: (index, 0, 0))
     return pl.pallas_call(
         functools.partial(unattend_kernel, n_head, chunks, row_len, piece, pair),
         grid_spec=pltpu.PrefetchScalarGridSpec(
             num_scalar_prefetch=1,
-            grid=(heads // pair,),
+            grid=(1,),
             in_specs=[by_rows(piece)] * (chunks * n_head)
             + [by_head(row_len, HD)] * 2
             + [by_rows(row_len)] * 3
             + [by_head(1, row_len)] * 3
             + [whole((1, row_len)), whole((HALF, row_len)), whole((HALF, row_len)), by_rows(1)],
-            out_specs=[pl.BlockSpec((3, rows, row_len), lambda g, info: (0, g, 0)), by_rows(1)],
+            out_specs=[whole((3, rows, row_len)), whole((rows, 1))],
             scratch_shapes=[
                 pltpu.VMEM((rows, row_len), BF16),
                 pltpu.VMEM((pair, 1, row_len), F32),
@@ -450,9 +524,9 @@
                 pltpu.VMEM((rows, row_len), F32),
             ],
         ),
-        out_shape=[shape((3, cols, row_len), BF16), shape((cols, 1), F32)],
-        compiler_params=params(40),
-        cost_estimate=cost(45e9, 12e6),
+        out_shape=[shape((3, rows, row_len), BF16), shape((rows, 1), F32)],
+        compiler_params=params(32),
+        cost_estimate=cost(22e9, 6e6),
         name="unattend",
     )(info, *do_pieces, k, v, kt, qt, ot, inv, qf, kf, starts, cosine, sine, gain)
 
@@ -466,14 +540,18 @@
     return factor * (grad - unit * jnp.mean(grad * unit, axis=-1, keepdims=True))
 
 
-def project_kernel(n_head, share, info, *refs):
+def project_kernel(n_head, share, kept, info, *refs):
     o_refs, w_refs = refs[:n_head], refs[n_head : 2 * n_head]
     x_refs = refs[2 * n_head : 3 * n_head]
-    alpha_ref, y_ref, x_ref, h_ref, low_ref = refs[3 * n_head :]
+    alpha_ref = refs[3 * n_head]
+    cat_ref, y_ref, x_ref, h_ref, low_ref = refs[3 * n_head + 1 + kept :]
     me = info[0]
+    cols = w_refs[0].shape[0]
     y = dot(o_refs[0][...], w_refs[0][...])
     for e in range(1, n_head):
         y += dot(o_refs[e][...], w_refs[e][...])
+    for e in range(n_head):
+        cat_ref[:, e * cols : (e + 1) * cols] = o_refs[e][...]
     for e in range(n_head):
         first = pl.multiple_of((me ^ e) * share, share)
         x_ref[:, pl.ds(first, share)] = x_refs[e][...]
@@ -484,14 +562,14 @@
     low_ref[...] = h_one.astype(BF16)
 
 
-def project(o_pieces, w_pieces, x_pieces, alpha, info):
+def project(chunk, kept, o_pieces, w_pieces, x_pieces, alpha, info, chunk_len):
     n_head = len(o_pieces)
     cols, model = w_pieces[0].shape
-    chunk_len, share = x_pieces[0].shape
+    share = x_pieces[0].shape[1]
     rows = chunk_len // n_head
     mine = lambda width: pl.BlockSpec((rows, width), lambda i, info: (info[0], 0))
     return pl.pallas_call(
-        functools.partial(project_kernel, n_head, share),
+        functools.partial(project_kernel, n_head, share, len(kept)),
         grid_spec=pltpu.PrefetchScalarGridSpec(
             num_scalar_prefetch=1,
             grid=(1,),
@@ -499,26 +577,32 @@
             + [whole((rows, cols))] * (n_head - 1)
             + [whole((cols, model))] * n_head
             + [mine(share)] * n_head
-            + [whole((1, model))],
-            out_specs=[whole((rows, model))] * 4,
+            + [whole((1, model))]
+            + [pl.BlockSpec(memory_space=pl.ANY)] * len(kept),
+            out_specs=[pl.BlockSpec((rows, n_head * cols), lambda i, info: (chunk, 0))]
+            + [whole((rows, model))] * 4,
         ),
+        input_output_aliases={3 * n_head + 2 + i: i for i in range(len(kept))},
         out_shape=[
-            shape((rows, model), F32),
-            shape((rows, model), BF16),
-            shape((rows, model), F32),
+            kept_shape((CHUNKS * rows, n_head * cols), BF16),
+            kept_shape((rows, model), F32),
+            kept_shape((rows, model), BF16),
+            kept_shape((rows, model), F32),
             shape((rows, model), BF16),
         ],
         compiler_params=params(32),
         cost_estimate=cost(2.0 * rows * model * model, 6e6),
         name="project",
-    )(info, *o_pieces, *w_pieces, *x_pieces, alpha)
-
-
-def feed_kernel(n_head, rows, refs_in, *refs):
-    h_refs = (refs_in, *refs[: n_head - 1])
-    refs = refs[n_head - 1 :]
-    up_ref, gate_ref, down_ref, su_ref, sg_ref, m_ref, u_ref, g_ref, cat_ref = refs[:9]
-    z_refs, acc = refs[9 : 9 + n_head], refs[9 + n_head]
+    )(info, *o_pieces, *w_pieces, *x_pieces, alpha, *kept)
+
+
+def feed_kernel(n_head, rows, kept, *refs):
+    h_refs = refs[:n_head]
+    refs = refs[n_head:]
+    up_ref, gate_ref, down_ref, su_ref, sg_ref = refs[:5]
+    m_ref, cat_ref, u_ref, g_ref = refs[5 + kept : 9 + kept]
+    refs = refs[9 + kept :]
+    z_refs, acc = refs[:n_head], refs[n_head]
     tile = pl.program_id(0)
 
     @pl.when(tile == 0)
@@ -549,7 +633,7 @@
             z_refs[e][...] = acc[e * rows : (e + 1) * rows, :].astype(BF16)
 
 
-def feed(h_pieces, w_up, w_gate, w_down, scale_up, scale_gate):
+def feed(chunk, kept, h_pieces, w_up, w_gate, w_down, scale_up, scale_gate):
     n_head = len(h_pieces)
     rows, model = h_pieces[0].shape
     hidden = w_up.shape[1]
@@ -557,7 +641,7 @@
     count = n_head * rows
     by_col = lambda height: pl.BlockSpec((height, tile), lambda n: (0, n))
     outs = pl.pallas_call(
-        functools.partial(feed_kernel, n_head, rows),
+        functools.partial(feed_kernel, n_head, rows, len(kept)),
         grid=(hidden // tile,),
         in_specs=[whole((rows, model))] * n_head
         + [
@@ -566,17 +650,29 @@
             pl.BlockSpec((tile, model), lambda n: (n, 0)),
             by_col(1),
             by_col(1),
-        ],
-        out_specs=[by_col(count)] * 3 + [whole((count, model))] + [whole((rows, model))] * n_head,
-        out_shape=[shape((count, hidden), BF16)] * 3
-        + [shape((count, model), BF16)]
+        ]
+        + [pl.BlockSpec(memory_space=pl.ANY)] * len(kept),
+        out_specs=[
+            pl.BlockSpec((count, tile), lambda n: (chunk, n)),
+            pl.BlockSpec((count, model), lambda n: (chunk, 0)),
+            by_col(count),
+            by_col(count),
+        ]
+        + [whole((rows, model))] * n_head,
+        out_shape=[
+            kept_shape((CHUNKS * count, hidden), BF16),
+            kept_shape((CHUNKS * count, model), BF16),
+            kept_shape((count, hidden), BF16),
+            kept_shape((count, hidden), BF16),
+        ]
         + [shape((rows, model), BF16)] * n_head,
+        input_output_aliases={n_head + 5 + i: i for i in range(len(kept))},
         scratch_shapes=[pltpu.VMEM((count, model), F32)],
         compiler_params=params(48),
         cost_estimate=cost(6.0 * count * model * hidden, 20e6),
         name="feed",
-    )(*h_pieces, w_up, w_gate, w_down, scale_up, scale_gate)
-    return outs[:4], list(outs[4:])
+    )(*h_pieces, w_up, w_gate, w_down, scale_up, scale_gate, *kept)
+    return outs[:2], outs[2:4], list(outs[4:])
 
 
 def middle_kernel(n_head, n_terms, share, info, *refs):
@@ -603,11 +699,12 @@
     dz_ref[...] = norm_back(grad * alpha, h_ffn, z_factor).astype(BF16)
 
 
-def middle(z_terms, cot_pieces, h_one, alpha, info):
+def middle(chunk, z_terms, cot_pieces, h_one, alpha, info):
     n_head, n_terms = len(cot_pieces), len(z_terms)
     rows, model = h_one.shape
     share = cot_pieces[0].shape[1]
-    mine = pl.BlockSpec((rows, share), lambda i, info: (info[0], 0))
+    mine = pl.BlockSpec((rows, share), lambda i, info: (chunk * n_head + info[0], 0))
+    theirs = pl.BlockSpec((rows, share), lambda i, info: (1 + chunk, 0))
     outs = pl.pallas_call(
         functools.partial(middle_kernel, n_head, n_terms, share),
         grid_spec=pltpu.PrefetchScalarGridSpec(
@@ -615,7 +712,7 @@
             grid=(1,),
             in_specs=[whole((rows, model))] * n_terms
             + [mine]
-            + [whole((rows, share))] * (n_head - 1)
+            + [theirs] * (n_head - 1)
             + [whole((rows, model)), whole((1, model))],
             out_specs=[whole((rows, share))] * n_head
             + [whole((rows, model))] * 2
@@ -631,19 +728,58 @@
     return list(outs[:n_head]), outs[n_head], outs[n_head + 1], outs[n_head + 2]
 
 
-def unfeed_kernel(n_head, rows, first_ref, *refs):
-    d_refs = (first_ref, *refs[: n_head - 1])
-    refs = refs[n_head - 1 :]
+def join(pieces):
+    rows, width = pieces[0].shape
+
+    def body(*refs):
+        for i, ref in enumerate(refs[:-1]):
+            refs[-1][i * rows : (i + 1) * rows, :] = ref[...]
+
+    return pl.pallas_call(
+        body,
+        in_specs=[whole((rows, width))] * len(pieces),
+        out_specs=whole((rows * len(pieces), width)),
+        grid=(1,),
+        out_shape=shape((rows * len(pieces), width), pieces[0].dtype),
+        compiler_params=params(16),
+        cost_estimate=cost(0, rows * width * 4 * len(pieces)),
+        name="join",
+    )(*pieces)
+
+
+def weigh(d_pair, x_pieces, chunk_len):
+    rows, row_len = d_pair.shape
+    n_head = len(x_pieces[0])
+    share = x_pieces[0][0].shape[1]
+    flat = [p for chunk in x_pieces for p in chunk]
+
+    def body(d_ref, *refs):
+        for e in range(n_head):
+            term = None
+            for c in range(len(x_pieces)):
+                d_part = d_ref[:, c * chunk_len : (c + 1) * chunk_len]
+                new = dot(d_part, refs[c * n_head + e][...])
+                term = new if term is None else term + new
+            refs[-1][:, e * share : (e + 1) * share] = term.astype(BF16)
+
+    return pl.pallas_call(
+        body,
+        in_specs=[whole((rows, row_len))] + [whole((chunk_len, share))] * len(flat),
+        out_specs=whole((rows, n_head * share)),
+        grid=(1,),
+        out_shape=shape((rows, n_head * share), BF16),
+        compiler_params=params(32),
+        cost_estimate=cost(0, 1),
+        name="weigh",
+    )(d_pair, *flat)
+
+
+def unfeed_kernel(n_head, rows, kept, cat_ref, *refs):
     u_ref, g_ref, up_ref, gate_ref, down_ref, su_ref, sg_ref = refs[:7]
-    du_ref, dg_ref, cat_ref, gsu_ref, gsg_ref = refs[7:12]
-    out_refs, acc = refs[12 : 12 + n_head], refs[12 + n_head]
+    du_ref, dg_ref, gsu_ref, gsg_ref = refs[7 + kept : 11 + kept]
+    refs = refs[11 + kept :]
+    out_refs, acc = refs[:n_head], refs[n_head]
     tile = pl.program_id(0)
-
-    @pl.when(tile == 0)
-    def _():
-        for e in range(n_head):
-            cat_ref[e * rows : (e + 1) * rows, :] = d_refs[e][...]
-
     d_mixed = dot(cat_ref[...], down_ref[...], 1, 1)
     up_raw, gate_raw = u_ref[...].astype(F32), g_ref[...].astype(F32)
     gate = gate_raw * sg_ref[...]
@@ -672,18 +808,17 @@
             out_refs[e][...] = acc[e * rows : (e + 1) * rows, :].astype(BF16)
 
 
-def unfeed(d_pieces, u, g, w_up, w_gate, w_down, scale_up, scale_gate):
-    n_head = len(d_pieces)
-    rows, model = d_pieces[0].shape
+def unfeed(chunk, kept, dz, u, g, w_up, w_gate, w_down, scale_up, scale_gate, n_head):
+    count, model = dz.shape
+    rows = count // n_head
     hidden = w_up.shape[1]
     tile = min(256, hidden)
-    count = n_head * rows
     by_col = lambda height: pl.BlockSpec((height, tile), lambda n: (0, n))
     outs = pl.pallas_call(
-        functools.partial(unfeed_kernel, n_head, rows),
+        functools.partial(unfeed_kernel, n_head, rows, len(kept)),
         grid=(hidden // tile,),
-        in_specs=[whole((rows, model))] * n_head
-        + [
+        in_specs=[
+            whole((count, model)),
             by_col(count),
             by_col(count),
             by_col(model),
@@ -691,27 +826,30 @@
             pl.BlockSpec((tile, model), lambda n: (n, 0)),
             by_col(1),
             by_col(1),
-        ],
-        out_specs=[by_col(count)] * 2
-        + [whole((count, model)), by_col(1), by_col(1)]
+        ]
+        + [pl.BlockSpec(memory_space=pl.ANY)] * len(kept),
+        out_specs=[pl.BlockSpec((count, tile), lambda n: (chunk, n))] * 2
+        + [by_col(1), by_col(1)]
         + [whole((rows, model))] * n_head,
-        out_shape=[shape((count, hidden), BF16)] * 2
-        + [shape((count, model), BF16), shape((1, hidden), F32), shape((1, hidden), F32)]
+        out_shape=[kept_shape((CHUNKS * count, hidden), BF16)] * 2
+        + [shape((1, hidden), F32), shape((1, hidden), F32)]
         + [shape((rows, model), BF16)] * n_head,
+        input_output_aliases={8 + i: i for i in range(len(kept))},
         scratch_shapes=[pltpu.VMEM((count, model), F32)],
         compiler_params=params(48),
         cost_estimate=cost(6.0 * count * model * hidden, 20e6),
         name="unfeed",
-    )(*d_pieces, u, g, w_up, w_gate, w_down, scale_up, scale_gate)
-    return outs[:5], list(outs[5:])
-
-
-def unproject_kernel(n_head, n_terms, cols, *refs):
+    )(dz, u, g, w_up, w_gate, w_down, scale_up, scale_gate, *kept)
+    return outs[:2], outs[2:4], list(outs[4:])
+
+
+def unproject_kernel(n_head, n_terms, kept, *refs):
     t_refs, w_refs = refs[:n_terms], refs[n_terms : n_terms + n_head]
     direct_ref, y_ref, x_ref, alpha_ref = refs[n_terms + n_head : n_terms + n_head + 4]
-    refs = refs[n_terms + n_head + 4 :]
+    refs = refs[n_terms + n_head + 4 + kept :]
+    dy_ref, refs = refs[0], refs[1:]
     do_refs = refs[:n_head]
-    dy_ref, zero_ref, grad_ref = refs[n_head:]
+    zero_ref, grad_ref = refs[n_head:]
     grad = direct_ref[...]
     for r in t_refs:
         grad += r[...].astype(F32)
@@ -728,33 +866,37 @@
         do_refs[e][...] = dot(w_refs[e][...], dy, 1, 1).astype(BF16)
 
 
-def unproject(terms, w_pieces, direct, y, x, alpha):
+def unproject(chunk, kept, terms, w_pieces, direct, y, x, alpha):
     n_head, n_terms = len(w_pieces), len(terms)
     rows, model = y.shape
     cols = w_pieces[0].shape[0]
     outs = pl.pallas_call(
-        functools.partial(unproject_kernel, n_head, n_terms, cols),
+        functools.partial(unproject_kernel, n_head, n_terms, len(kept)),
         grid=(1,),
         in_specs=[whole((rows, model))] * n_terms
         + [whole((cols, model))] * n_head
         + [whole((rows, model))] * 3
-        + [whole((1, model))],
-        out_specs=[whole((cols, rows))] * n_head
-        + [whole((rows, model))] * 2
-        + [whole((1, model))],
-        out_shape=[shape((cols, rows), BF16)] * n_head
-        + [shape((rows, model), BF16), shape((rows, model), F32), shape((1, model), F32)],
+        + [whole((1, model))]
+        + [pl.BlockSpec(memory_space=pl.ANY)] * len(kept),
+        out_specs=[pl.BlockSpec((rows, model), lambda i: (chunk, 0))]
+        + [whole((cols, rows))] * n_head
+        + [whole((rows, model)), whole((1, model))],
+        input_output_aliases={n_terms + n_head + 4 + i: i for i in range(len(kept))},
+        out_shape=[kept_shape((CHUNKS * rows, model), BF16)]
+        + [shape((cols, rows), BF16)] * n_head
+        + [shape((rows, model), F32), shape((1, model), F32)],
         compiler_params=params(32),
         cost_estimate=cost(2.0 * rows * model * model, 8e6),
         name="unproject",
-    )(*terms, *w_pieces, direct, y, x, alpha)
-    return list(outs[:n_head]), outs[n_head], outs[n_head + 1], outs[n_head + 2]
-
-
-def spread_kernel(n_head, share, info, d_ref, w_ref, direct_ref, *out_refs):
+    )(*terms, *w_pieces, direct, y, x, alpha, *kept)
+    return outs[0], list(outs[1 : n_head + 1]), outs[n_head + 1], outs[n_head + 2]
+
+
+def spread_kernel(n_head, share, pairs, info, *refs):
+    d_refs, (w_ref, direct_ref), out_refs = refs[:pairs], refs[pairs : pairs + 2], refs[pairs + 2 :]
     me = info[0]
     block = pl.program_id(0)
-    d_all = d_ref[...].T
+    d_all = jnp.concatenate([r[...] for r in d_refs], axis=0).T
     for e in range(n_head):
         at = pl.ds(pl.multiple_of((me ^ e) * share, share), share)
         term = dot(d_all, w_ref[:, at])
@@ -773,12 +915,12 @@
     share = model // n_head
     rows = chunk_len // n_head
     return pl.pallas_call(
-        functools.partial(spread_kernel, n_head, share),
+        functools.partial(spread_kernel, n_head, share, len(d_all)),
         grid_spec=pltpu.PrefetchScalarGridSpec(
             num_scalar_prefetch=1,
             grid=(n_head,),
             in_specs=[
-                pl.BlockSpec((rows3, rows), lambda i, info: (0, chunk * n_head + i)),
+                *[pl.BlockSpec((d.shape[0], rows), lambda i, info: (0, chunk * n_head + i)) for d in d_all],
                 whole((rows3, model)),
                 whole((rows, model)),
             ],
@@ -788,7 +930,7 @@
         compiler_params=params(32),
         cost_estimate=cost(2.0 * chunk_len * model * rows3, 8e6),
         name="spread",
-    )(info, d_all, w_t, direct)
+    )(info, *d_all, w_t, direct)
 
 
 def on_device(
@@ -843,111 +985,279 @@
     def block_of(values, e):
         return lax.dynamic_slice_in_dim(values, (me ^ e) * rows, rows, 0)
 
-    x_pieces = [gather_pieces(part(x_own, c), n_head) for c in chunks]
-    w_t = jnp.concatenate([w_query.T, w_key.T, w_value.T], axis=0)
-    out_pieces = gather_pieces(w_out, n_head)
-
-    buffers = []
-    state = []
+    order = Order()
+    pair = min(2, cols // HD) * HD
+    pairs = cols // pair
+    w_t = turn(w_query, w_key, w_value, pair)
+
+    def block_parts(values):
+        return [values] + [block_of(values, e) for e in range(1, n_head)]
+
+    bit = lax.axis_index("batch") % 2
+    half = model // 2
+    out_half = lax.dynamic_slice_in_dim(w_out, bit * half, half, 1)
+    out_half = jnp.concatenate(
+        [out_half[:, i : i + share] for i in range(0, half, share)], axis=0
+    )
+    far = n_head // 2
+    x_far = gather_far(part(x_own, 0), n_head)
+
+    buffers, x_pieces, o_flying = [], [], []
     for c in chunks:
-        buffers, o_chunk = attend_chunk(
-            c, x_pieces[c], w_t, cosine, sine, gain, starts, info, buffers, row_len
+        near = x_far if c == 0 else {e: p[:chunk_len] for e, p in x_far.items()}
+        x_pieces.append(gather_near(near, n_head))
+        if c < CHUNKS - 1:
+            following = part(x_own, c + 1)
+            if c == 0:
+                following = jnp.concatenate([following, out_half], axis=0)
+            x_far = gather_far(after(following, x_far[far]), n_head)
+        buffers, o_chunk = order.run(
+            lambda w: attend_chunk(
+                c, x_pieces[c], w, cosine, sine, gain, starts, info, buffers, row_len, chunk_len
+            ),
+            w_t,
+            need=x_pieces[c],
         )
-        o_pieces = exchange_pieces(
-            [o_chunk] + [block_of(o_chunk, e) for e in range(1, n_head)], n_head
+        order.last = o_chunk
+        pieces = block_parts(o_chunk)
+        if c == 0:
+            cots = [block_parts(part(cot_own, i)) for i in chunks]
+            pieces[1:] = [
+                jnp.concatenate([p] + [cot[e] for cot in cots], axis=0)
+                for e, p in enumerate(pieces)
+                if e
+            ]
+        o_flying.append(exchange_pieces(pieces, n_head))
+        if c == 0:
+            x_far = order.land(x_far)
+            out_far = {e: p[chunk_len:] for e, p in x_far.items()}
+            out_far = {e: (v, swap(v, "batch", 1, n_batch)) for e, v in out_far.items() if e}
+
+    def out_of(first, second):
+        blocks = [
+            v[i : i + cols] for v in (first, second) for i in range(0, first.shape[0], cols)
+        ]
+        return jnp.concatenate(blocks, axis=1)
+
+    out_far = {
+        e: jnp.where(bit == 0, out_of(v, w), out_of(w, v))
+        for e, (v, w) in order.land(out_far).items()
+    }
+    out_far[0] = w_out
+    out_pieces = gather_near(out_far, n_head)
+
+    state, h_fars, joined = [], [], []
+    for c in chunks:
+        o_pieces = order.land(o_flying[c])
+        joined, y, x_rows, h_one, h_low = order.run(
+            lambda first: project(
+                c,
+                joined,
+                [first] + o_pieces[1:],
+                out_pieces,
+                x_pieces[c],
+                attn_alpha,
+                info,
+                chunk_len,
+            ),
+            o_pieces[0],
+            need=o_pieces[1:],
         )
-        y, x_rows, h_one, h_low = project(o_pieces, out_pieces, x_pieces[c], attn_alpha, info)
-        o_pieces[0] = block_of(o_chunk, 0)
-        state.append((o_pieces, y, x_rows, h_one, h_low))
-    cot_pieces = []
+        joined = [joined]
+        order.last = h_low
+        state.append((y, x_rows, h_one))
+        before = h_fars[-1][far] if c else None
+        if c < CHUNKS - 1:
+            before = o_flying[c + 1][far]
+        h_fars.append(gather_far(after(h_low, before), n_head))
+    cot_pieces = [cot_own] + o_flying[0][1:]
+
+    fed, raws, z_all, z_flying, sent = [], [], [], [], None
     for c in chunks:
-        cot = part(cot_own, c)
-        cot_pieces.append(
-            exchange_pieces([cot] + [block_of(cot, e) for e in range(1, n_head)], n_head)
+        h_pieces = gather_near(order.land(h_fars[c]), n_head)
+        fed, raw, z_pieces = order.run(
+            lambda first: feed(
+                c,
+                fed,
+                [first] + h_pieces[1:],
+                w_up,
+                w_gate,
+                w_down,
+                up_scale,
+                gate_scale,
+            ),
+            h_pieces[0],
+            need=h_pieces[1:] + [sent],
         )
-    after = []
+        order.last = z_pieces[0]
+        raws.append(raw)
+        z_all.append(z_pieces)
+        if c < CHUNKS - 1:
+            terms, sent = reduce_pieces(z_pieces, n_head)
+            z_flying.append(terms)
+    mixed, h_cat = fed
+
+    mids, dz_fars = [], []
     for c in chunks:
-        o_pieces, y, x_rows, h_one, h_low = state[c]
-        (mixed, up_raw, gate_raw, h_cat), z_pieces = feed(
-            gather_pieces(h_low, n_head), w_up, w_gate, w_down, up_scale, gate_scale
+        if c == CHUNKS - 1:
+            terms, _ = reduce_pieces(order.land(z_all[c]) if c else z_all[c], n_head)
+            z_flying.append(terms)
+        terms = order.land(z_flying[c])
+        mid = order.run(
+            lambda first: middle(
+                c, [first] + terms[1:], cot_pieces, state[c][2], ffn_alpha, info
+            ),
+            terms[0],
+            need=terms[1:],
         )
-        z_terms = reduce_pieces(z_pieces, n_head)
-        two_pieces, dz, direct, grad_alpha_ffn = middle(
-            z_terms, cot_pieces[c], h_one, ffn_alpha, info
+        mids.append(mid)
+        dz = mid[1]
+        order.last = dz
+        dz_fars.append(gather_far(after(dz, dz_fars[-1][far]) if c else dz, n_head))
+
+    place = lax.axis_index("batch")[None].astype(jnp.int32)
+    unfed, scale_sums, dh_all, dh_flying, dzs, sent = [], [], [], [], [], None
+    for c in chunks:
+        dz_pieces = gather_near(order.land(dz_fars[c]), n_head)
+        dzs.append(
+            order.run(lambda first: join([first] + dz_pieces[1:]), dz_pieces[0], need=dz_pieces[1:])
         )
-        after.append((mixed, up_raw, gate_raw, h_cat, two_pieces, dz, direct, grad_alpha_ffn))
-
-    ffn = []
-    for c in chunks:
-        mixed, up_raw, gate_raw, h_cat, two_pieces, dz, direct, _ = after[c]
-        (du, dg, dz_cat, gsu, gsg), dh_pieces = unfeed(
-            gather_pieces(dz, n_head), up_raw, gate_raw, w_up, w_gate, w_down, up_scale, gate_scale
+        need = [sent]
+        if c == CHUNKS - 1:
+            grad_down = order.run(
+                lambda first: sum(
+                    dot(part(mixed, i), (dzs[:-1] + [first])[i], 0, 0) for i in chunks
+                ).astype(BF16),
+                dzs[c],
+                need=[sent],
+            )
+            sum_down = BatchSum(grad_down, n_batch)
+            need.append(sum_down.sent)
+        unfed, sums, pieces = order.run(
+            lambda first: unfeed(
+                c, unfed, first, *raws[c], w_up, w_gate, w_down, up_scale, gate_scale, n_head
+            ),
+            dzs[c],
+            need=need,
         )
-        ffn.append((mixed, h_cat, du, dg, dz_cat, gsu, gsg, dh_pieces))
-
-    grad_down = sum(dot(f[0], f[4], 0, 0) for f in ffn).astype(BF16)
-    grad_up = sum(dot(f[1], f[2], 0, 0) for f in ffn).astype(BF16)
-    grad_gate = sum(dot(f[1], f[3], 0, 0) for f in ffn).astype(BF16)
-    place = ring_place(lax.axis_index("batch"), n_batch)[None].astype(jnp.int32)
-    grad_down = assemble(rings(grad_down, n_batch), place)
-    grad_up = assemble(rings(grad_up, n_batch, (1,)), place)
-    grad_gate = assemble(rings(grad_gate, n_batch, (-1,)), place)
-
-    do_pieces, zeros, dys, alphas = [], [], [], []
-    for c in chunks:
-        terms = reduce_pieces(ffn[c][7], n_head)
-        _, y, x_rows, _, _ = state[c]
-        pieces, dy, zero, grad_alpha_attn = unproject(
-            terms, out_pieces, after[c][6], y, x_rows, attn_alpha
+        order.last = pieces[0]
+        scale_sums.append(jnp.concatenate(sums, axis=0))
+        dh_all.append(pieces)
+        if c < CHUNKS - 1:
+            terms, sent = reduce_pieces(pieces, n_head)
+            dh_flying.append(terms)
+
+    do_pieces, zeros, alphas, dys = [], [], [], []
+
+    def back(c):
+        y, x_rows, _ = state[c]
+        terms = order.land(dh_flying[c])
+        dy, d_pieces, zero, grad_alpha_attn = order.run(
+            lambda first: unproject(
+                c, dys, [first] + terms[1:], out_pieces, mids[c][2], y, x_rows, attn_alpha
+            ),
+            terms[0],
+            need=terms[1:],
         )
-        do_pieces += exchange_pieces(pieces, n_head)
+        order.last = d_pieces[0]
+        dys[:] = [dy]
+        do_pieces.extend(exchange_pieces(d_pieces, n_head))
         zeros.append(zero)
-        dys.append(dy)
         alphas.append(grad_alpha_attn)
 
-    out_terms = [
-        sum(dot(state[c][0][e], dys[c], 0, 0) for c in chunks).astype(BF16) for e in range(n_head)
-    ]
-    grad_out = total(reduce_pieces(out_terms, n_head))
-
-    d_all, grad_gain = unattend(
-        do_pieces, buffers, starts, cosine, sine, gain, info, n_head
+    for c in chunks[:-1]:
+        back(c)
+    terms, sent = reduce_pieces(order.land(dh_all[-1]) if CHUNKS > 1 else dh_all[-1], n_head)
+    dh_flying.append(terms)
+    moved = sum_down.advance(order)
+    grad_up = order.run(
+        lambda h: dot(h, unfed[0], 0, 0).astype(BF16), h_cat, need=[sent] + moved
     )
-    d_all = d_all.reshape(3 * cols, row_len)
+    sum_up = BatchSum(grad_up, n_batch)
+    grad_gate = order.run(
+        lambda h: dot(h, unfed[1], 0, 0).astype(BF16), h_cat, need=[sum_up.sent]
+    )
+    back(CHUNKS - 1)
+    sum_gate = BatchSum(after(grad_gate, sum_up.flying), n_batch)
+    moved = sum_down.advance(order) + sum_up.advance(order) + [sum_gate.sent]
+    do_pieces = order.land(do_pieces)
+
+    alpha_sums = jnp.concatenate([sum(alphas), sum(m[3] for m in mids)], axis=0)
+    alpha_sums = sum_small(alpha_sums, "head", n_head)
+    d_all, gains, attn_sums = [], [], []
+    sums = [sum_down, sum_up, sum_gate]
+    for g in range(pairs):
+        d_pair, grad_gain = order.run(
+            lambda first: unattend(
+                g, [first] + do_pieces[1:], buffers, starts, cosine, sine, gain, info, n_head
+            ),
+            do_pieces[0],
+            need=do_pieces[1:] + moved,
+        )
+        order.last = d_pair
+        moved = [m for b in sums for m in b.advance(order)]
+        d_pair = d_pair.reshape(3 * pair, row_len)
+        d_all.append(d_pair)
+        gains.append(grad_gain[:, 0])
+        if g == 0:
+            out_terms = order.run(lambda o: dot(o, dys[0], 0, 0).astype(BF16), joined[0])
+            out_terms = [out_terms[e * cols : (e + 1) * cols] for e in range(n_head)]
+            out_flying, _ = reduce_pieces(out_terms, n_head)
+            outgoing = order.land(
+                [jnp.concatenate([m[0][e] for m in mids], axis=0) for e in range(n_head)]
+            )
+            hidden_flying = exchange_pieces(outgoing, n_head)
+        grads = order.run(lambda d: weigh(d, x_pieces, chunk_len), d_pair, need=moved)
+        if g == pairs - 1:
+            small = jnp.concatenate(
+                [alpha_sums]
+                + [
+                    jnp.pad(v, ((0, 0), (0, model - v.shape[1])))
+                    for v in (sum(scale_sums), jnp.concatenate(gains)[None])
+                ],
+                axis=0,
+            )
+            unit = 32 if n_batch == 8 else 16 * n_batch
+            rows_now = 3 * pair + cols + 5
+            small = jnp.pad(small, ((0, 5 - small.shape[0] + -rows_now % unit), (0, 0)))
+            grads = jnp.concatenate(
+                [grads, total(order.land(out_flying)), small.astype(BF16)], axis=0
+            )
+        attn_sums.append(BatchSum(grads, n_batch))
+        moved = [attn_sums[-1].sent]
+    sums += attn_sums
 
     grad_hidden = []
     for c in chunks:
-        pieces = spread(c, chunk_len, d_all, w_t, zeros[c], info, n_head)
-        terms = reduce_pieces(pieces, n_head)
+        d_pieces = order.run(
+            lambda w: spread(c, chunk_len, d_all, w, zeros[c], info, n_head), w_t, need=moved
+        )
+        moved = [m for b in sums for m in b.advance(order)]
+        terms, _ = reduce_pieces(d_pieces, n_head)
         grad_hidden.append(sum(t.astype(F32) for t in terms))
     grad_hidden = jnp.concatenate(grad_hidden, axis=0)[None]
-
-    def lanes(c):
-        return lax.slice_in_dim(d_all, c * chunk_len, (c + 1) * chunk_len, axis=1)
-
-    grad_t = jnp.concatenate(
-        [sum(dot(lanes(c), x_pieces[c][e]) for c in chunks) for e in range(n_head)], axis=1
-    ).astype(BF16)
-    grad_attn = rings(jnp.concatenate([grad_t, grad_out], axis=0), n_batch)
-    grad_query, grad_key, grad_value, grad_out = assemble_turned(
-        grad_attn, place, info, cols, n_head
+    while any(b.todo for b in sums):
+        for b in sums:
+            b.advance()
+
+    grad_down = assemble(sum_down.finish(), place)
+    grad_up = assemble(sum_up.finish(), place)
+    grad_gate = assemble(sum_gate.finish(), place)
+    grad_query, grad_key, grad_value, grad_out, small = assemble_turned(
+        [b.finish() for b in attn_sums], place, info, cols, n_head, cols, small.shape[0]
     )
-
-    alpha_sums = jnp.concatenate([sum(alphas), sum(a[7] for a in after)], axis=0)
-    alpha_sums = sum_small(sum_small(alpha_sums, "head", n_head), "batch", n_batch)
-    alpha_own = lax.dynamic_slice_in_dim(alpha_sums, me * share, share, 1)
-    scale_sums = jnp.concatenate([sum(f[5] for f in ffn), sum(f[6] for f in ffn)], axis=0)
-    scale_sums = sum_small(scale_sums, "batch", n_batch)
-    gain_sums = sum_small(grad_gain[:, 0], "batch", n_batch)
-
-    hidden_out = []
-    for c in chunks:
-        pieces = exchange_pieces(after[c][4], n_head)
-        stacked = jnp.stack(pieces)
-        hidden_out += [
-            lax.dynamic_index_in_dim(stacked, b ^ me, 0, keepdims=False) for b in range(n_head)
-        ]
-    hidden_out = jnp.concatenate(hidden_out, axis=0)[None]
+    alpha_own = lax.dynamic_slice_in_dim(small[:2], me * share, share, 1)
+    hidden_units = w_up.shape[1]
+
+    stacked = jnp.stack(hidden_flying)
+    hidden_out = jnp.concatenate(
+        [
+            lax.dynamic_index_in_dim(stacked, b ^ me, 0, keepdims=False)[c * rows : (c + 1) * rows]
+            for c in chunks
+            for b in range(n_head)
+        ],
+        axis=0,
+    )[None]
     return (
         hidden_out,
         grad_hidden,
@@ -958,9 +1268,9 @@
         grad_up,
         grad_gate,
         grad_down,
-        gain_sums,
-        scale_sums[0],
-        scale_sums[1],
+        small[4, :cols],
+        small[2, :hidden_units],
+        small[3, :hidden_units],
         alpha_own[0],
         alpha_own[1],
     )

time: 662 us -> 502 us (0.76)
  the two profiles are of different devices: /device:TPU:8 before, /device:TPU:0 now
where the time goes in v2:
time: 502 us; the launch traced here: 493 us
  waiting for transfers between devices  179 us (36%)
  Pallas kernels  175 us (35%)
  starting transfers between devices  82.1 us (16%)
  local copies, waits for them, and re-layouts  19.4 us (4%)
  other arithmetic  18.7 us (4%)
  matrix products  16.2 us (3%)
    ppermute x69, waiting for transfers between devices, swap(): return lax.ppermute(value, axis, [(i, i ^ mask) for i in range(size)])  128 us
    ppermute x69, starting transfers between devices, swap(): return lax.ppermute(value, axis, [(i, i ^ mask) for i in range(size)])  61 us
    ppermute x15, waiting for transfers between devices, start(): self.flying = lax.ppermute(self.sent, 'batch', pairs)  51.1 us
    pallas_call x2, Pallas kernels, unfeed(): pl.pallas_call(functools.partial(unfeed_kernel, n_head, rows, len(kept)),...  36.8 us
    pallas_call x2, Pallas kernels, attend_chunk(): pl.pallas_call(body, grid_spec=pltpu.PrefetchScalarGridSpec(num_scalar_pr...  32.1 us
    pallas_call x2, Pallas kernels, unattend(): pl.pallas_call(functools.partial(unattend_kernel, n_head, chunks, row_len...  26.3 us
    pallas_call x2, Pallas kernels, feed(): pl.pallas_call(functools.partial(feed_kernel, n_head, rows, len(kept)), g...  25.6 us
    ppermute x15, starting transfers between devices, start(): self.flying = lax.ppermute(self.sent, 'batch', pairs)  21 us
  transfers between devices with their start and end apart: 84, of which 34 were waited for; matrix products, arithmetic and copies ran while one was open for 7% of the time, Pallas kernels for 34%

profile of v2, /device:TPU:0, one launch (start us, length us, event | category | flops | bytes accessed | tf_op | source)
XLA Modules:
  0.0 493.2 jit_solution(11735193391076695951)
XLA Ops:
  0.7 2.2 slice_bitcast_fusion.1
  2.9 3.0 collective-permute-start.1
  6.6 3.3 subtract_convert_fusion
  13.4 4.5 collective-permute-done.1.refs_2_.refs_10_
  17.9 1.7 collective-permute-start.4
  21.8 17.4 %attend.2 = (bf16[4,2048,64]{2,1,0:T(8,128)(2,1)}, bf16[4,80,2048]{2,1,0:T(8,128)(2,1)}, bf16[4,2048,64]{2,1,0:T(8,128)(2,1)}, bf16[256,2048]{1,0:T(8,128)(2,1)}...) custom-call(s32[10]{0:T(128)S(1)} %pad_add_fusion.info, ...), custom_call_target="tpu_custom_call" | custom-call | flops 1 | bytes 1 | tf_op jit(solution)/shard_map/attend/pallas_call | solution.py:390
  45.3 14.8 %attend.3 = (bf16[4,2048,64]{2,1,0:T(8,128)(2,1)}, bf16[4,80,2048]{2,1,0:T(8,128)(2,1)}, bf16[4,2048,64]{2,1,0:T(8,128)(2,1)}, bf16[256,2048]{1,0:T(8,128)(2,1)}...) custom-call(s32[10]{0:T(128)S(1)} %pad_add_fusion.info, ...), custom_call_target="tpu_custom_call", output_to_operand_aliasing={{0}: (10, {}), {1}: (11, {}), {2}: (12, {}), {3}: (13, {}),... | custom-call | flops 1 | bytes 1 | tf_op jit(solution)/shard_map/attend/pallas_call | solution.py:390
  62.9 8.5 %collective-permute-done.8.refs_3_.refs_6_ = bf16[768,256]{1,0:T(8,128)(2,1)S(1)} collective-permute-done((bf16[768,256]{1,0:T(8,128)(2,1)S(1)}, bf16[768,256]{1,0:T(8,128)(2,1)S(1)}, u32[]{:S(2)}, u32[]{:S(2)}) %collective-permute-start.8) | collective-permute-done | bytes 393248 | tf_op jit(solution)/shard_map/ppermute | solution.py:67
  72.2 8.9 %collective-permute-done.7.refs_2_.refs_5_ = bf16[768,256]{1,0:T(8,128)(2,1)S(1)} collective-permute-done((bf16[768,256]{1,0:T(8,128)(2,1)S(1)}, bf16[768,256]{1,0:T(8,128)(2,1)S(1)}, u32[]{:S(2)}, u32[]{:S(2)}) %collective-permute-start.7) | collective-permute-done | bytes 393248 | tf_op jit(solution)/shard_map/ppermute | solution.py:67
  81.1 4.2 project.2
  85.9 1.6 collective-permute-start.13
  87.5 11.4 %collective-permute-done.14.refs_3_ = bf16[256,256]{1,0:T(8,128)(2,1)S(1)} collective-permute-done((bf16[256,256]{1,0:T(8,128)(2,1)S(1)}, bf16[256,256]{1,0:T(8,128)(2,1)S(1)}, u32[]{:S(2)}, u32[]{:S(2)}) %collective-permute-start.14) | collective-permute-done | bytes 131104 | tf_op jit(solution)/shard_map/ppermute | solution.py:67
  98.9 4.2 project.3
  103.1 1.8 collective-permute-start.15
  107.2 12.9 %feed.2 = (bf16[2048,1024]{1,0:T(8,128)(2,1)}, bf16[2048,1024]{1,0:T(8,128)(2,1)}, bf16[1024,1024]{1,0:T(8,128)(2,1)}, bf16[1024,1024]{1,0:T(8,128)(2,1)}, bf16[...) custom-call(bf16[256,1024]{1,0:T(8,128)(2,1)S(1)} %get-tuple-element, ...), custom_call_target="tpu_custom_call" | custom-call | flops 1 | bytes 1 | tf_op jit(solution)/shard_map/feed/pallas_call | solution.py:643
  123.6 12.7 %feed.3 = (bf16[2048,1024]{1,0:T(8,128)(2,1)}, bf16[2048,1024]{1,0:T(8,128)(2,1)}, bf16[1024,1024]{1,0:T(8,128)(2,1)}, bf16[1024,1024]{1,0:T(8,128)(2,1)}, bf16[...) custom-call(bf16[256,1024]{1,0:T(8,128)(2,1)S(1)} %get-tuple-element, ...), custom_call_target="tpu_custom_call", output_to_operand_aliasing={{0}: (9, {}), {1}: (10, {})} | custom-call | flops 1 | bytes 1 | tf_op jit(solution)/shard_map/feed/pallas_call | solution.py:643
  136.5 1.9 middle.2
  143.3 12.7 %collective-permute-done.26.refs_2_ = bf16[256,1024]{1,0:T(8,128)(2,1)S(1)} collective-permute-done((bf16[256,1024]{1,0:T(8,128)(2,1)S(1)}, bf16[256,1024]{1,0:T(8,128)(2,1)S(1)}, u32[]{:S(2)}, u32[]{:S(2)}) %collective-permute-start.26) | collective-permute-done | bytes 524320 | tf_op jit(solution)/shard_map/ppermute | solution.py:67
  156.1 2.7 middle.3
  159.0 7.6 %collective-permute-done.28.refs_2_ = bf16[256,1024]{1,0:T(8,128)(2,1)S(1)} collective-permute-done((bf16[256,1024]{1,0:T(8,128)(2,1)S(1)}, bf16[256,1024]{1,0:T(8,128)(2,1)S(1)}, u32[]{:S(2)}, u32[]{:S(2)}) %collective-permute-start.28) | collective-permute-done | bytes 524320 | tf_op jit(solution)/shard_map/ppermute | solution.py:67
  168.6 18.7 %unfeed.2 = (bf16[2048,1024]{1,0:T(8,128)(2,1)}, bf16[2048,1024]{1,0:T(8,128)(2,1)}, f32[1,1024]{1,0:T(1,128)S(1)}, f32[1,1024]{1,0:T(1,128)S(1)}, bf16[256,1024...) custom-call(bf16[1024,1024]{1,0:T(8,128)(2,1)S(1)} %join.2.cat_ref, ...), custom_call_target="tpu_custom_call" | custom-call | flops 1 | bytes 1 | tf_op jit(solution)/shard_map/unfeed/pallas_call | solution.py:817
  190.8 1.6 collective-permute-done.30.refs_1_
  193.2 1.7 join.3.cat_ref
  194.9 2.0 add_convert_fusion.18
  196.9 2.4 fusion.1
  200.7 2.5 add_convert_fusion
  205.7 8.3 %collective-permute-start.37 = (bf16[512,1024]{1,0:T(8,128)(2,1)}, bf16[512,1024]{1,0:T(8,128)(2,1)}, u32[]{:S(2)}, u32[]{:S(2)}) collective-permute-start(bf16[512,1024]{1,0:T(8,128)(2,1)} %constant_dynamic-slice_fusion.6), channel_id=1, source_target_pairs={{0,4},{4,0},{8,12},{12,8},{16,20},{20,16},{24,28},{28,24},{1,5},{5... | collective-permute-start | bytes 3145736 | tf_op jit(solution)/shard_map/ppermute | solution.py:67
  214.6 1.6 copy-done.9
  217.0 18.0 %unfeed.3 = (bf16[2048,1024]{1,0:T(8,128)(2,1)}, bf16[2048,1024]{1,0:T(8,128)(2,1)}, f32[1,1024]{1,0:T(1,128)S(1)}, f32[1,1024]{1,0:T(1,128)S(1)}, bf16[256,1024...) custom-call(bf16[1024,1024]{1,0:T(8,128)(2,1)S(1)} %copy-done.9, ...), custom_call_target="tpu_custom_call", output_to_operand_aliasing={{0}: (8, {}), {1}: (9, {})} | custom-call | flops 1 | bytes 1 | tf_op jit(solution)/shard_map/unfeed/pallas_call | solution.py:817
  235.2 4.2 unproject.2
  245.5 5.2 %convolution_convert_fusion.2 = bf16[1024,1024]{1,0:T(8,128)(2,1)S(1)} fusion(bf16[2048,1024]{1,0:T(8,128)(2,1)S(1)} %copy-done.75, bf16[2048,1024]{1,0:T(8,128)(2,1)S(1)} %copy-done.72), kind=kOutput, calls=%fused_computation.19 | convolution fusion | flops 4296015872 | bytes 10485760 | tf_op jit(solution)/shard_map/dot_general | solution.py:23
  250.9 4.8 convolution_convert_fusion.1
  255.8 2.8 collective-permute-done.39.refs_2_
  259.6 3.7 unproject.3
  266.6 3.8 collective-permute-done.44.refs_6_
  272.8 3.1 collective-permute-done.47
  276.5 13.2 %unattend.2 = (bf16[3,128,2048]{2,1,0:T(8,128)(2,1)S(1)}, f32[128,1]{1,0:T(8,128)S(1)}) custom-call(s32[10]{0:T(128)S(1)} %pad_add_fusion.info, bf16[256,256]{1,0:T(8,128)(2,1)S(1)} %get-tuple-element.385.refs_0_, bf16[256,256]{1,0:T(8,128)(2,1)S(1)} %collective-permute-done.40.refs_1_, bf16[256,256]{1,0:T(8,128)(2,1)S(1)} %collective-permute-done.41.refs_2_, ...), custom_call_target="tpu_custom_call" | custom-call | flops 1 | bytes 1 | tf_op jit(solution)/shard_map/unattend/pallas_call | solution.py:508
  291.2 2.8 collective-permute-start.52
  294.0 4.3 collective-permute-start.53
  300.1 7.3 %collective-permute-done.49 = bf16[512,256]{1,0:T(8,128)(2,1)S(1)} collective-permute-done((bf16[512,256]{1,0:T(8,128)(2,1)S(1)}, bf16[512,256]{1,0:T(8,128)(2,1)S(1)}, u32[]{:S(2)}, u32[]{:S(2)}) %collective-permute-start.49) | collective-permute-done | bytes 262176 | tf_op jit(solution)/shard_map/ppermute | solution.py:67
  307.4 4.1 collective-permute-done.50
  314.3 2.5 collective-permute-done.52
  317.2 4.9 collective-permute-done.53
  323.2 3.9 collective-permute-start.56
  328.4 3.3 weigh.2
  331.8 13.2 %unattend.3 = (bf16[3,128,2048]{2,1,0:T(8,128)(2,1)S(1)}, f32[128,1]{1,0:T(8,128)S(1)}) custom-call(s32[10]{0:T(128)S(1)} %pad_add_fusion.info, bf16[256,256]{1,0:T(8,128)(2,1)S(1)} %get-tuple-element.385.refs_0_, bf16[256,256]{1,0:T(8,128)(2,1)S(1)} %collective-permute-done.40.refs_1_, bf16[256,256]{1,0:T(8,128)(2,1)S(1)} %collective-permute-done.41.refs_2_, ...), custom_call_target="tpu_custom_call" | custom-call | flops 1 | bytes 1 | tf_op jit(solution)/shard_map/unattend/pallas_call | solution.py:508
  345.2 6.8 %collective-permute-start.67 = (bf16[192,1024]{1,0:T(8,128)(2,1)S(1)}, bf16[192,1024]{1,0:T(8,128)(2,1)S(1)}, u32[]{:S(2)}, u32[]{:S(2)}) collective-permute-start(bf16[192,1024]{1,0:T(8,128)(2,1)S(1)} %constant_dynamic-slice_fusion.3), channel_id=1, source_target_pairs={{0,4},{4,0},{8,12},{12,8},{16,20},{20,16},{24,28},{28,24},{1,5},{5... | collective-permute-start | bytes 1179656 | tf_op jit(solution)/shard_map/ppermute | solution.py:67
  352.9 3.3 weigh.3
  358.9 6.8 %spread.2 = (bf16[1024,256]{1,0:T(8,128)(2,1)S(1)}, bf16[1024,256]{1,0:T(8,128)(2,1)S(1)}, bf16[1024,256]{1,0:T(8,128)(2,1)S(1)}, bf16[1024,256]{1,0:T(8,128)(2,1)S(1)}) custom-call(s32[10]{0:T(128)S(1)} %pad_add_fusion.info, bf16[384,2048]{1,0:T(8,128)(2,1)S(1)} %bitcast.81, bf16[384,2048]{1,0:T(8,128)(2,1)S(1)} %bitcast.84, ...), custom_call_target="tpu_custom_call" | custom-call | flops 1 | bytes 1 | tf_op jit(solution)/shard_map/spread/pallas_call | solution.py:917
  365.8 2.1 collective-permute-start.83
  368.1 8.6 %collective-permute-done.68 = bf16[336,1024]{1,0:T(8,128)(2,1)S(1)} collective-permute-done((bf16[336,1024]{1,0:T(8,128)(2,1)S(1)}, bf16[336,1024]{1,0:T(8,128)(2,1)S(1)}, u32[]{:S(2)}, u32[]{:S(2)}) %collective-permute-start.68) | collective-permute-done | bytes 688160 | tf_op jit(solution)/shard_map/ppermute | solution.py:67
  380.1 2.8 collective-permute-done.65
  384.4 6.8 %spread.3 = (bf16[1024,256]{1,0:T(8,128)(2,1)S(1)}, bf16[1024,256]{1,0:T(8,128)(2,1)S(1)}, bf16[1024,256]{1,0:T(8,128)(2,1)S(1)}, bf16[1024,256]{1,0:T(8,128)(2,1)S(1)}) custom-call(s32[10]{0:T(128)S(1)} %pad_add_fusion.info, bf16[384,2048]{1,0:T(8,128)(2,1)S(1)} %bitcast.82, bf16[384,2048]{1,0:T(8,128)(2,1)S(1)} %bitcast.85, ...), custom_call_target="tpu_custom_call" | custom-call | flops 1 | bytes 1 | tf_op jit(solution)/shard_map/spread/pallas_call | solution.py:917
  391.2 7.6 %collective-permute-done.76 = bf16[336,1024]{1,0:T(8,128)(2,1)S(1)} collective-permute-done((bf16[336,1024]{1,0:T(8,128)(2,1)S(1)}, bf16[336,1024]{1,0:T(8,128)(2,1)S(1)}, u32[]{:S(2)}, u32[]{:S(2)}) %collective-permute-start.76) | collective-permute-done | bytes 688160 | tf_op jit(solution)/shard_map/ppermute | solution.py:141
  399.9 2.3 assemble.5
  410.0 20.9 %collective-permute-done.81 = bf16[512,1024]{1,0:T(8,128)(2,1)S(1)} collective-permute-done((bf16[512,1024]{1,0:T(8,128)(2,1)S(1)}, bf16[512,1024]{1,0:T(8,128)(2,1)S(1)}, u32[]{:S(2)}, u32[]{:S(2)}) %collective-permute-start.81) | collective-permute-done | bytes 1048608 | tf_op jit(solution)/shard_map/ppermute | solution.py:141
  431.9 13.6 %collective-permute-done.78 = bf16[336,1024]{1,0:T(8,128)(2,1)S(1)} collective-permute-done((bf16[336,1024]{1,0:T(8,128)(2,1)S(1)}, bf16[336,1024]{1,0:T(8,128)(2,1)S(1)}, u32[]{:S(2)}, u32[]{:S(2)}) %collective-permute-start.78) | collective-permute-done | bytes 688160 | tf_op jit(solution)/shard_map/ppermute | solution.py:141
  445.6 1.6 collective-permute-start.82
  447.2 3.7 collective-permute-done.74
  453.1 2.3 assemble.3
  457.0 14.7 %collective-permute-done.82.other_ref = bf16[512,1024]{1,0:T(8,128)(2,1)S(1)} collective-permute-done((bf16[512,1024]{1,0:T(8,128)(2,1)S(1)}, bf16[512,1024]{1,0:T(8,128)(2,1)S(1)}, u32[]{:S(2)}, u32[]{:S(2)}) %collective-permute-start.82) | collective-permute-done | bytes 1048608 | tf_op jit(solution)/shard_map/ppermute | solution.py:67
  471.7 2.3 assemble.4
  474.0 13.8 %collective-permute-done.75.refs_1_ = bf16[192,1024]{1,0:T(8,128)(2,1)S(1)} collective-permute-done((bf16[192,1024]{1,0:T(8,128)(2,1)S(1)}, bf16[192,1024]{1,0:T(8,128)(2,1)S(1)}, u32[]{:S(2)}, u32[]{:S(2)}) %collective-permute-start.75) | collective-permute-done | bytes 393248 | tf_op jit(solution)/shard_map/ppermute | solution.py:67
  487.8 3.4 assemble_turned.1
  (390 shorter events, 84.6 us)
Async XLA Ops:
  2.9 15.0 %collective-permute-start.1 = (bf16[1024,256]{1,0:T(8,128)(2,1)S(1)}, bf16[1024,256]{1,0:T(8,128)(2,1)}, u32[]{:S(2)}, u32[]{:S(2)}) collective-permute-start(bf16[1024,256]{1,0:T(8,128)(2,1)S(1)} %get-tuple-element.442.refs_0_.refs_8_), channel_id=1, source_target_pairs={{0,2},{1,3},{2,0},{3,1},{4,6},{5,7},{6,4},{7,5},{8,10},{9,11},{10,... | collective-permute-start | bytes 1572872 | tf_op jit(solution)/shard_map/ppermute | solution.py:67
  5.8 14.9 %collective-permute-start = (bf16[1024,256]{1,0:T(8,128)(2,1)S(1)}, bf16[1024,256]{1,0:T(8,128)(2,1)}, u32[]{:S(2)}, u32[]{:S(2)}) collective-permute-start(bf16[1024,256]{1,0:T(8,128)(2,1)S(1)} %get-tuple-element.442.refs_0_.refs_8_), channel_id=1, source_target_pairs={{0,1},{1,0},{2,3},{3,2},{4,5},{5,4},{6,7},{7,6},{8,9},{9,8},{10,11... | collective-permute-start | bytes 1572872 | tf_op jit(solution)/shard_map/ppermute | solution.py:67
  17.9 21.6 %collective-permute-start.4 = (bf16[1536,256]{1,0:T(8,128)(2,1)S(1)}, bf16[1536,256]{1,0:T(8,128)(2,1)S(1)}, u32[]{:S(2)}, u32[]{:S(2)}) collective-permute-start(bf16[1536,256]{1,0:T(8,128)(2,1)S(1)} %pad_maximum_fusion.1), channel_id=1, source_target_pairs={{0,2},{1,3},{2,0},{3,1},{4,6},{5,7},{6,4},{7,5},{8,10},{9,11},{10,... | collective-permute-start | bytes 2359304 | tf_op jit(solution)/shard_map/ppermute | solution.py:67
  41.0 40.1 %collective-permute-start.9 = (bf16[256,1024]{1,0:T(8,128)(2,1)}, bf16[256,1024]{1,0:T(8,128)(2,1)}, u32[]{:S(2)}, u32[]{:S(2)}) collective-permute-start(bf16[256,1024]{1,0:T(8,128)(2,1)} %refs_3_.7), channel_id=1, source_target_pairs={{0,1},{1,0},{2,3},{3,2},{4,5},{5,4},{6,7},{7,6},{8,9},{9,8},{10,11... | collective-permute-start | bytes 1572872 | tf_op jit(solution)/shard_map/ppermute | solution.py:67
  43.7 16.5 %collective-permute-start.10 = (bf16[512,256]{1,0:T(8,128)(2,1)S(1)}, bf16[512,256]{1,0:T(8,128)(2,1)S(1)}, u32[]{:S(2)}, u32[]{:S(2)}) collective-permute-start(bf16[512,256]{1,0:T(8,128)(2,1)S(1)} %slice.149), channel_id=1, source_target_pairs={{0,4},{4,0},{8,12},{12,8},{16,20},{20,16},{24,28},{28,24},{1,5},{5... | collective-permute-start | bytes 786440 | tf_op jit(solution)/shard_map/ppermute | solution.py:67
  60.4 20.7 %collective-permute-start.11 = (bf16[256,1024]{1,0:T(8,128)(2,1)S(1)}, bf16[256,1024]{1,0:T(8,128)(2,1)S(1)}, u32[]{:S(2)}, u32[]{:S(2)}) collective-permute-start(bf16[256,1024]{1,0:T(8,128)(2,1)S(1)} %maximum_select_fusion.refs_6_.refs_5_), channel_id=1, source_target_pairs={{0,1},{1,0},{2,3},{3,2},{4,5},{5,4},{6,7},{7,6},{8,9},{9,8},{10,11... | collective-permute-start | bytes 1572872 | tf_op jit(solution)/shard_map/ppermute | solution.py:67
  60.5 10.9 %collective-permute-start.8 = (bf16[768,256]{1,0:T(8,128)(2,1)S(1)}, bf16[768,256]{1,0:T(8,128)(2,1)S(1)}, u32[]{:S(2)}, u32[]{:S(2)}) collective-permute-start(bf16[768,256]{1,0:T(8,128)(2,1)S(1)} %pad_maximum_fusion.4), channel_id=1, source_target_pairs={{0,3},{1,2},{2,1},{3,0},{4,7},{5,6},{6,5},{7,4},{8,11},{9,10},{10,... | collective-permute-start | bytes 1179656 | tf_op jit(solution)/shard_map/ppermute | solution.py:67
  61.3 19.8 %collective-permute-start.7 = (bf16[768,256]{1,0:T(8,128)(2,1)S(1)}, bf16[768,256]{1,0:T(8,128)(2,1)S(1)}, u32[]{:S(2)}, u32[]{:S(2)}) collective-permute-start(bf16[768,256]{1,0:T(8,128)(2,1)S(1)} %pad_maximum_fusion.3), channel_id=1, source_target_pairs={{0,2},{1,3},{2,0},{3,1},{4,6},{5,7},{6,4},{7,5},{8,10},{9,11},{10,... | collective-permute-start | bytes 1179656 | tf_op jit(solution)/shard_map/ppermute | solution.py:67
  62.8 18.2 %collective-permute-start.6 = (bf16[768,256]{1,0:T(8,128)(2,1)S(1)}, bf16[768,256]{1,0:T(8,128)(2,1)S(1)}, u32[]{:S(2)}, u32[]{:S(2)}) collective-permute-start(bf16[768,256]{1,0:T(8,128)(2,1)S(1)} %pad_maximum_fusion.2), channel_id=1, source_target_pairs={{0,1},{1,0},{2,3},{3,2},{4,5},{5,4},{6,7},{7,6},{8,9},{9,8},{10,11... | collective-permute-start | bytes 1179656 | tf_op jit(solution)/shard_map/ppermute | solution.py:67
  71.4 13.9 %collective-permute-start.12 = (bf16[256,256]{1,0:T(8,128)(2,1)S(1)}, bf16[256,256]{1,0:T(8,128)(2,1)S(1)}, u32[]{:S(2)}, u32[]{:S(2)}) collective-permute-start(bf16[256,256]{1,0:T(8,128)(2,1)S(1)} %get-tuple-element.446), channel_id=1, source_target_pairs={{0,2},{1,3},{2,0},{3,1},{4,6},{5,7},{6,4},{7,5},{8,10},{9,11},{10,... | collective-permute-start | bytes 393224 | tf_op jit(solution)/shard_map/ppermute | solution.py:67
  85.3 19.6 %collective-permute-start.16 = (bf16[256,1024]{1,0:T(8,128)(2,1)S(1)}, bf16[256,1024]{1,0:T(8,128)(2,1)S(1)}, u32[]{:S(2)}, u32[]{:S(2)}) collective-permute-start(bf16[256,1024]{1,0:T(8,128)(2,1)S(1)} %get-tuple-element.256.refs_0_), channel_id=1, source_target_pairs={{0,2},{1,3},{2,0},{3,1},{4,6},{5,7},{6,4},{7,5},{8,10},{9,11},{10,... | collective-permute-start | bytes 1572872 | tf_op jit(solution)/shard_map/ppermute | solution.py:67
  85.9 13.0 %collective-permute-start.14 = (bf16[256,256]{1,0:T(8,128)(2,1)S(1)}, bf16[256,256]{1,0:T(8,128)(2,1)S(1)}, u32[]{:S(2)}, u32[]{:S(2)}) collective-permute-start(bf16[256,256]{1,0:T(8,128)(2,1)S(1)} %get-tuple-element.444), channel_id=1, source_target_pairs={{0,3},{1,2},{2,1},{3,0},{4,7},{5,6},{6,5},{7,4},{8,11},{9,10},{10,... | collective-permute-start | bytes 393224 | tf_op jit(solution)/shard_map/ppermute | solution.py:67
  85.9 13.0 %collective-permute-start.13 = (bf16[256,256]{1,0:T(8,128)(2,1)S(1)}, bf16[256,256]{1,0:T(8,128)(2,1)S(1)}, u32[]{:S(2)}, u32[]{:S(2)}) collective-permute-start(bf16[256,256]{1,0:T(8,128)(2,1)S(1)} %get-tuple-element.445), channel_id=1, source_target_pairs={{0,1},{1,0},{2,3},{3,2},{4,5},{5,4},{6,7},{7,6},{8,9},{9,8},{10,11... | collective-permute-start | bytes 393224 | tf_op jit(solution)/shard_map/ppermute | solution.py:67
  105.0 15.5 %collective-permute-start.19 = (bf16[256,1024]{1,0:T(8,128)(2,1)S(1)}, bf16[256,1024]{1,0:T(8,128)(2,1)S(1)}, u32[]{:S(2)}, u32[]{:S(2)}) collective-permute-start(bf16[256,1024]{1,0:T(8,128)(2,1)S(1)} %get-tuple-element.263.refs_0_), channel_id=1, source_target_pairs={{0,2},{1,3},{2,0},{3,1},{4,6},{5,7},{6,4},{7,5},{8,10},{9,11},{10,... | collective-permute-start | bytes 1572872 | tf_op jit(solution)/shard_map/ppermute | solution.py:67
  121.0 15.2 %collective-permute-start.22 = (bf16[256,1024]{1,0:T(8,128)(2,1)S(1)}, bf16[256,1024]{1,0:T(8,128)(2,1)S(1)}, u32[]{:S(2)}, u32[]{:S(2)}) collective-permute-start(bf16[256,1024]{1,0:T(8,128)(2,1)S(1)} %get-tuple-element.268), channel_id=1, source_target_pairs={{0,1},{1,0},{2,3},{3,2},{4,5},{5,4},{6,7},{7,6},{8,9},{9,8},{10,11... | collective-permute-start | bytes 1572872 | tf_op jit(solution)/shard_map/ppermute | solution.py:67
  122.3 14.3 %collective-permute-start.23 = (bf16[256,1024]{1,0:T(8,128)(2,1)S(1)}, bf16[256,1024]{1,0:T(8,128)(2,1)S(1)}, u32[]{:S(2)}, u32[]{:S(2)}) collective-permute-start(bf16[256,1024]{1,0:T(8,128)(2,1)S(1)} %add_convert_fusion.20), channel_id=1, source_target_pairs={{0,2},{1,3},{2,0},{3,1},{4,6},{5,7},{6,4},{7,5},{8,10},{9,11},{10,... | collective-permute-start | bytes 1572872 | tf_op jit(solution)/shard_map/ppermute | solution.py:67
  141.2 14.8 %collective-permute-start.26 = (bf16[256,1024]{1,0:T(8,128)(2,1)S(1)}, bf16[256,1024]{1,0:T(8,128)(2,1)S(1)}, u32[]{:S(2)}, u32[]{:S(2)}) collective-permute-start(bf16[256,1024]{1,0:T(8,128)(2,1)S(1)} %add_convert_fusion.19), channel_id=1, source_target_pairs={{0,2},{1,3},{2,0},{3,1},{4,6},{5,7},{6,4},{7,5},{8,10},{9,11},{10,... | collective-permute-start | bytes 1572872 | tf_op jit(solution)/shard_map/ppermute | solution.py:67
  141.9 24.6 %collective-permute-start.28 = (bf16[256,1024]{1,0:T(8,128)(2,1)S(1)}, bf16[256,1024]{1,0:T(8,128)(2,1)S(1)}, u32[]{:S(2)}, u32[]{:S(2)}) collective-permute-start(bf16[256,1024]{1,0:T(8,128)(2,1)S(1)} %get-tuple-element.292.refs_0_), channel_id=1, source_target_pairs={{0,2},{1,3},{2,0},{3,1},{4,6},{5,7},{6,4},{7,5},{8,10},{9,11},{10,... | collective-permute-start | bytes 1572872 | tf_op jit(solution)/shard_map/ppermute | solution.py:67
  158.9 8.3 %collective-permute-start.27 = (bf16[256,1024]{1,0:T(8,128)(2,1)S(1)}, bf16[256,1024]{1,0:T(8,128)(2,1)S(1)}, u32[]{:S(2)}, u32[]{:S(2)}) collective-permute-start(bf16[256,1024]{1,0:T(8,128)(2,1)S(1)} %get-tuple-element.292.refs_0_), channel_id=1, source_target_pairs={{0,1},{1,0},{2,3},{3,2},{4,5},{5,4},{6,7},{7,6},{8,9},{9,8},{10,11... | collective-permute-start | bytes 1572872 | tf_op jit(solution)/shard_map/ppermute | solution.py:67
  166.5 23.7 %collective-permute-start.31 = (bf16[256,1024]{1,0:T(8,128)(2,1)}, bf16[256,1024]{1,0:T(8,128)(2,1)}, u32[]{:S(2)}, u32[]{:S(2)}) collective-permute-start(bf16[256,1024]{1,0:T(8,128)(2,1)} %get-tuple-element.300.refs_0_), channel_id=1, source_target_pairs={{0,2},{1,3},{2,0},{3,1},{4,6},{5,7},{6,4},{7,5},{8,10},{9,11},{10,... | collective-permute-start | bytes 1572872 | tf_op jit(solution)/shard_map/ppermute | solution.py:67
  205.7 35.6 %collective-permute-start.37 = (bf16[512,1024]{1,0:T(8,128)(2,1)}, bf16[512,1024]{1,0:T(8,128)(2,1)}, u32[]{:S(2)}, u32[]{:S(2)}) collective-permute-start(bf16[512,1024]{1,0:T(8,128)(2,1)} %constant_dynamic-slice_fusion.6), channel_id=1, source_target_pairs={{0,4},{4,0},{8,12},{12,8},{16,20},{20,16},{24,28},{28,24},{1,5},{5... | collective-permute-start | bytes 3145736 | tf_op jit(solution)/shard_map/ppermute | solution.py:67
  214.0 20.9 %collective-permute-start.34 = (bf16[256,1024]{1,0:T(8,128)(2,1)}, bf16[256,1024]{1,0:T(8,128)(2,1)}, u32[]{:S(2)}, u32[]{:S(2)}) collective-permute-start(bf16[256,1024]{1,0:T(8,128)(2,1)} %get-tuple-element.312), channel_id=1, source_target_pairs={{0,1},{1,0},{2,3},{3,2},{4,5},{5,4},{6,7},{7,6},{8,9},{9,8},{10,11... | collective-permute-start | bytes 1572872 | tf_op jit(solution)/shard_map/ppermute | solution.py:67
  214.0 20.9 %collective-permute-start.35 = (bf16[256,1024]{1,0:T(8,128)(2,1)}, bf16[256,1024]{1,0:T(8,128)(2,1)}, u32[]{:S(2)}, u32[]{:S(2)}) collective-permute-start(bf16[256,1024]{1,0:T(8,128)(2,1)} %add_convert_fusion.18), channel_id=1, source_target_pairs={{0,2},{1,3},{2,0},{3,1},{4,6},{5,7},{6,4},{7,5},{8,10},{9,11},{10,... | collective-permute-start | bytes 1572872 | tf_op jit(solution)/shard_map/ppermute | solution.py:67
  239.7 23.6 %collective-permute-start.42 = (bf16[256,256]{1,0:T(8,128)(2,1)S(1)}, bf16[256,256]{1,0:T(8,128)(2,1)S(1)}, u32[]{:S(2)}, u32[]{:S(2)}) collective-permute-start(bf16[256,256]{1,0:T(8,128)(2,1)S(1)} %get-tuple-element.347), channel_id=1, source_target_pairs={{0,3},{1,2},{2,1},{3,0},{4,7},{5,6},{6,5},{7,4},{8,11},{9,10},{10,... | collective-permute-start | bytes 393224 | tf_op jit(solution)/shard_map/ppermute | solution.py:67
  241.1 14.6 %collective-permute-start.38 = (bf16[256,1024]{1,0:T(8,128)(2,1)S(1)}, bf16[256,1024]{1,0:T(8,128)(2,1)S(1)}, u32[]{:S(2)}, u32[]{:S(2)}) collective-permute-start(bf16[256,1024]{1,0:T(8,128)(2,1)S(1)} %get-tuple-element.333), channel_id=1, source_target_pairs={{0,1},{1,0},{2,3},{3,2},{4,5},{5,4},{6,7},{7,6},{8,9},{9,8},{10,11... | collective-permute-start | bytes 1572872 | tf_op jit(solution)/shard_map/ppermute | solution.py:67
  242.9 28.6 %collective-permute-start.46 = (bf16[512,1024]{1,0:T(8,128)(2,1)S(1)}, bf16[512,1024]{1,0:T(8,128)(2,1)S(1)}, u32[]{:S(2)}, u32[]{:S(2)}) collective-permute-start(bf16[512,1024]{1,0:T(8,128)(2,1)S(1)} %add_convert_fusion.9), channel_id=1, source_target_pairs={{0,8},{4,12},{24,16},{28,20},{1,9},{5,13},{25,17},{29,21},{2,10},{... | collective-permute-start | bytes 3145736 | tf_op jit(solution)/shard_map/ppermute | solution.py:141
  244.5 14.1 %collective-permute-start.39 = (bf16[256,1024]{1,0:T(8,128)(2,1)S(1)}, bf16[256,1024]{1,0:T(8,128)(2,1)S(1)}, u32[]{:S(2)}, u32[]{:S(2)}) collective-permute-start(bf16[256,1024]{1,0:T(8,128)(2,1)S(1)} %add_convert_fusion.17), channel_id=1, source_target_pairs={{0,2},{1,3},{2,0},{3,1},{4,6},{5,7},{6,4},{7,5},{8,10},{9,11},{10,... | collective-permute-start | bytes 1572872 | tf_op jit(solution)/shard_map/ppermute | solution.py:67
  250.8 25.1 %collective-permute-start.47 = (bf16[512,1024]{1,0:T(8,128)(2,1)S(1)}, bf16[512,1024]{1,0:T(8,128)(2,1)S(1)}, u32[]{:S(2)}, u32[]{:S(2)}) collective-permute-start(bf16[512,1024]{1,0:T(8,128)(2,1)S(1)} %constant_dynamic-slice_fusion.5), channel_id=1, source_target_pairs={{0,4},{4,0},{8,12},{12,8},{16,20},{20,16},{24,28},{28,24},{1,5},{5... | collective-permute-start | bytes 3145736 | tf_op jit(solution)/shard_map/ppermute | solution.py:67
  255.7 7.9 %collective-permute-start.40 = (bf16[256,256]{1,0:T(8,128)(2,1)S(1)}, bf16[256,256]{1,0:T(8,128)(2,1)S(1)}, u32[]{:S(2)}, u32[]{:S(2)}) collective-permute-start(bf16[256,256]{1,0:T(8,128)(2,1)S(1)} %get-tuple-element.343), channel_id=1, source_target_pairs={{0,1},{1,0},{2,3},{3,2},{4,5},{5,4},{6,7},{7,6},{8,9},{9,8},{10,11... | collective-permute-start | bytes 393224 | tf_op jit(solution)/shard_map/ppermute | solution.py:67
  264.0 6.4 %collective-permute-start.44 = (bf16[256,256]{1,0:T(8,128)(2,1)S(1)}, bf16[256,256]{1,0:T(8,128)(2,1)S(1)}, u32[]{:S(2)}, u32[]{:S(2)}) collective-permute-start(bf16[256,256]{1,0:T(8,128)(2,1)S(1)} %get-tuple-element.352), channel_id=1, source_target_pairs={{0,2},{1,3},{2,0},{3,1},{4,6},{5,7},{6,4},{7,5},{8,10},{9,11},{10,... | collective-permute-start | bytes 393224 | tf_op jit(solution)/shard_map/ppermute | solution.py:67
  265.1 6.4 %collective-permute-start.45 = (bf16[256,256]{1,0:T(8,128)(2,1)S(1)}, bf16[256,256]{1,0:T(8,128)(2,1)S(1)}, u32[]{:S(2)}, u32[]{:S(2)}) collective-permute-start(bf16[256,256]{1,0:T(8,128)(2,1)S(1)} %get-tuple-element.354), channel_id=1, source_target_pairs={{0,3},{1,2},{2,1},{3,0},{4,7},{5,6},{6,5},{7,4},{8,11},{9,10},{10,... | collective-permute-start | bytes 393224 | tf_op jit(solution)/shard_map/ppermute | solution.py:67
  265.5 28.5 %collective-permute-start.61 = (f32[2,1024]{1,0:T(2,128)S(1)}, f32[2,1024]{1,0:T(2,128)S(1)}, u32[]{:S(2)}, u32[]{:S(2)}) collective-permute-start(f32[2,1024]{1,0:T(2,128)S(1)} %fusion.28), channel_id=1, source_target_pairs={{0,2},{1,3},{2,0},{3,1},{4,6},{5,7},{6,4},{7,5},{8,10},{9,11},{10,... | collective-permute-start | bytes 24584 | tf_op jit(solution)/shard_map/ppermute | solution.py:67
  271.9 40.6 %collective-permute-start.51 = (bf16[512,1024]{1,0:T(8,128)(2,1)S(1)}, bf16[512,1024]{1,0:T(8,128)(2,1)S(1)}, u32[]{:S(2)}, u32[]{:S(2)}) collective-permute-start(bf16[512,1024]{1,0:T(8,128)(2,1)S(1)} %add_convert_fusion.8), channel_id=1, source_target_pairs={{8,16},{12,20},{16,8},{20,12},{9,17},{13,21},{17,9},{21,13},{10,18... | collective-permute-start | bytes 3145736 | tf_op jit(solution)/shard_map/ppermute | solution.py:141
  291.0 8.3 %collective-permute-start.48 = (bf16[512,256]{1,0:T(8,128)(2,1)S(1)}, bf16[512,256]{1,0:T(8,128)(2,1)S(1)}, u32[]{:S(2)}, u32[]{:S(2)}) collective-permute-start(bf16[512,256]{1,0:T(8,128)(2,1)S(1)} %pad_maximum_fusion.6), channel_id=1, source_target_pairs={{0,1},{1,0},{2,3},{3,2},{4,5},{5,4},{6,7},{7,6},{8,9},{9,8},{10,11... | collective-permute-start | bytes 786440 | tf_op jit(solution)/shard_map/ppermute | solution.py:67
  291.2 25.6 %collective-permute-start.52 = (bf16[512,1024]{1,0:T(8,128)(2,1)S(1)}, bf16[512,1024]{1,0:T(8,128)(2,1)S(1)}, u32[]{:S(2)}, u32[]{:S(2)}) collective-permute-start(bf16[512,1024]{1,0:T(8,128)(2,1)S(1)} %add_convert_fusion.7), channel_id=1, source_target_pairs={{0,8},{4,12},{24,16},{28,20},{1,9},{5,13},{25,17},{29,21},{2,10},{... | collective-permute-start | bytes 3145736 | tf_op jit(solution)/shard_map/ppermute | solution.py:141
  294.0 28.1 %collective-permute-start.53 = (bf16[512,1024]{1,0:T(8,128)(2,1)S(1)}, bf16[512,1024]{1,0:T(8,128)(2,1)S(1)}, u32[]{:S(2)}, u32[]{:S(2)}) collective-permute-start(bf16[512,1024]{1,0:T(8,128)(2,1)S(1)} %constant_dynamic-slice_fusion.4), channel_id=1, source_target_pairs={{0,4},{4,0},{8,12},{12,8},{16,20},{20,16},{24,28},{28,24},{1,5},{5... | collective-permute-start | bytes 3145736 | tf_op jit(solution)/shard_map/ppermute | solution.py:67
  298.3 9.1 %collective-permute-start.49 = (bf16[512,256]{1,0:T(8,128)(2,1)S(1)}, bf16[512,256]{1,0:T(8,128)(2,1)S(1)}, u32[]{:S(2)}, u32[]{:S(2)}) collective-permute-start(bf16[512,256]{1,0:T(8,128)(2,1)S(1)} %pad_maximum_fusion.7), channel_id=1, source_target_pairs={{0,2},{1,3},{2,0},{3,1},{4,6},{5,7},{6,4},{7,5},{8,10},{9,11},{10,... | collective-permute-start | bytes 786440 | tf_op jit(solution)/shard_map/ppermute | solution.py:67
  299.3 12.3 %collective-permute-start.50 = (bf16[512,256]{1,0:T(8,128)(2,1)S(1)}, bf16[512,256]{1,0:T(8,128)(2,1)S(1)}, u32[]{:S(2)}, u32[]{:S(2)}) collective-permute-start(bf16[512,256]{1,0:T(8,128)(2,1)S(1)} %pad_maximum_fusion.8), channel_id=1, source_target_pairs={{0,3},{1,2},{2,1},{3,0},{4,7},{5,6},{6,5},{7,4},{8,11},{9,10},{10,... | collective-permute-start | bytes 786440 | tf_op jit(solution)/shard_map/ppermute | solution.py:67
  307.4 19.7 %collective-permute-start.58 = (bf16[256,1024]{1,0:T(8,128)(2,1)S(1)}, bf16[256,1024]{1,0:T(8,128)(2,1)S(1)}, u32[]{:S(2)}, u32[]{:S(2)}) collective-permute-start(bf16[256,1024]{1,0:T(8,128)(2,1)S(1)} %get-tuple-element.438), channel_id=1, source_target_pairs={{0,1},{1,0},{2,3},{3,2},{4,5},{5,4},{6,7},{7,6},{8,9},{9,8},{10,11... | collective-permute-start | bytes 1572872 | tf_op jit(solution)/shard_map/ppermute | solution.py:67
  311.5 44.7 %collective-permute-start.57 = (bf16[256,1024]{1,0:T(8,128)(2,1)S(1)}, bf16[256,1024]{1,0:T(8,128)(2,1)S(1)}, u32[]{:S(2)}, u32[]{:S(2)}) collective-permute-start(bf16[256,1024]{1,0:T(8,128)(2,1)S(1)} %get-tuple-element.439), channel_id=1, source_target_pairs={{0,1},{1,0},{2,3},{3,2},{4,5},{5,4},{6,7},{7,6},{8,9},{9,8},{10,11... | collective-permute-start | bytes 1572872 | tf_op jit(solution)/shard_map/ppermute | solution.py:67
  313.0 32.2 %collective-permute-start.54 = (bf16[512,1024]{1,0:T(8,128)(2,1)S(1)}, bf16[512,1024]{1,0:T(8,128)(2,1)S(1)}, u32[]{:S(2)}, u32[]{:S(2)}) collective-permute-start(bf16[512,1024]{1,0:T(8,128)(2,1)S(1)} %add_convert_fusion.6), channel_id=1, source_target_pairs={{8,0},{12,4},{16,24},{20,28},{9,1},{13,5},{17,25},{21,29},{10,2},{... | collective-permute-start | bytes 3145736 | tf_op jit(solution)/shard_map/ppermute | solution.py:141
  322.1 30.0 %collective-permute-start.55 = (bf16[512,1024]{1,0:T(8,128)(2,1)S(1)}, bf16[512,1024]{1,0:T(8,128)(2,1)S(1)}, u32[]{:S(2)}, u32[]{:S(2)}) collective-permute-start(bf16[512,1024]{1,0:T(8,128)(2,1)S(1)} %add_convert_fusion.5), channel_id=1, source_target_pairs={{8,16},{12,20},{16,8},{20,12},{9,17},{13,21},{17,9},{21,13},{10,18... | collective-permute-start | bytes 3145736 | tf_op jit(solution)/shard_map/ppermute | solution.py:141
  323.2 28.8 %collective-permute-start.56 = (bf16[512,1024]{1,0:T(8,128)(2,1)S(1)}, bf16[512,1024]{1,0:T(8,128)(2,1)S(1)}, u32[]{:S(2)}, u32[]{:S(2)}) collective-permute-start(bf16[512,1024]{1,0:T(8,128)(2,1)S(1)} %add_convert_fusion.4), channel_id=1, source_target_pairs={{0,8},{4,12},{24,16},{28,20},{1,9},{5,13},{25,17},{29,21},{2,10},{... | collective-permute-start | bytes 3145736 | tf_op jit(solution)/shard_map/ppermute | solution.py:141
  327.3 28.9 %collective-permute-start.59 = (bf16[256,1024]{1,0:T(8,128)(2,1)S(1)}, bf16[256,1024]{1,0:T(8,128)(2,1)S(1)}, u32[]{:S(2)}, u32[]{:S(2)}) collective-permute-start(bf16[256,1024]{1,0:T(8,128)(2,1)S(1)} %add_convert_fusion.16), channel_id=1, source_target_pairs={{0,2},{1,3},{2,0},{3,1},{4,6},{5,7},{6,4},{7,5},{8,10},{9,11},{10,... | collective-permute-start | bytes 1572872 | tf_op jit(solution)/shard_map/ppermute | solution.py:67
  345.2 20.7 %collective-permute-start.67 = (bf16[192,1024]{1,0:T(8,128)(2,1)S(1)}, bf16[192,1024]{1,0:T(8,128)(2,1)S(1)}, u32[]{:S(2)}, u32[]{:S(2)}) collective-permute-start(bf16[192,1024]{1,0:T(8,128)(2,1)S(1)} %constant_dynamic-slice_fusion.3), channel_id=1, source_target_pairs={{0,4},{4,0},{8,12},{12,8},{16,20},{20,16},{24,28},{28,24},{1,5},{5... | collective-permute-start | bytes 1179656 | tf_op jit(solution)/shard_map/ppermute | solution.py:67
  356.7 20.0 %collective-permute-start.68 = (bf16[336,1024]{1,0:T(8,128)(2,1)S(1)}, bf16[336,1024]{1,0:T(8,128)(2,1)S(1)}, u32[]{:S(2)}, u32[]{:S(2)}) collective-permute-start(bf16[336,1024]{1,0:T(8,128)(2,1)S(1)} %constant_dynamic-slice_fusion.2), channel_id=1, source_target_pairs={{0,4},{4,0},{8,12},{12,8},{16,20},{20,16},{24,28},{28,24},{1,5},{5... | collective-permute-start | bytes 2064392 | tf_op jit(solution)/shard_map/ppermute | solution.py:67
  356.8 26.0 %collective-permute-start.65 = (bf16[512,1024]{1,0:T(8,128)(2,1)S(1)}, bf16[512,1024]{1,0:T(8,128)(2,1)S(1)}, u32[]{:S(2)}, u32[]{:S(2)}) collective-permute-start(bf16[512,1024]{1,0:T(8,128)(2,1)S(1)} %add_convert_fusion.3), channel_id=1, source_target_pairs={{8,0},{12,4},{16,24},{20,28},{9,1},{13,5},{17,25},{21,29},{10,2},{... | collective-permute-start | bytes 3145736 | tf_op jit(solution)/shard_map/ppermute | solution.py:141
  358.1 21.9 %collective-permute-start.66 = (bf16[512,1024]{1,0:T(8,128)(2,1)S(1)}, bf16[512,1024]{1,0:T(8,128)(2,1)S(1)}, u32[]{:S(2)}, u32[]{:S(2)}) collective-permute-start(bf16[512,1024]{1,0:T(8,128)(2,1)S(1)} %add_convert_fusion.2), channel_id=1, source_target_pairs={{8,16},{12,20},{16,8},{20,12},{9,17},{13,21},{17,9},{21,13},{10,18... | collective-permute-start | bytes 3145736 | tf_op jit(solution)/shard_map/ppermute | solution.py:141
  365.7 12.5 %collective-permute-start.63 = (bf16[1024,256]{1,0:T(8,128)(2,1)S(1)}, bf16[1024,256]{1,0:T(8,128)(2,1)S(1)}, u32[]{:S(2)}, u32[]{:S(2)}) collective-permute-start(bf16[1024,256]{1,0:T(8,128)(2,1)S(1)} %get-tuple-element.409), channel_id=1, source_target_pairs={{0,1},{1,0},{2,3},{3,2},{4,5},{5,4},{6,7},{7,6},{8,9},{9,8},{10,11... | collective-permute-start | bytes 1572872 | tf_op jit(solution)/shard_map/ppermute | solution.py:67
  365.8 34.0 %collective-permute-start.83 = (bf16[512,1024]{1,0:T(8,128)(2,1)S(1)}, bf16[512,1024]{1,0:T(8,128)(2,1)S(1)}, u32[]{:S(2)}, u32[]{:S(2)}) collective-permute-start(bf16[512,1024]{1,0:T(8,128)(2,1)S(1)} %broadcast_select_fusion.2.own_ref), channel_id=1, source_target_pairs={{0,4},{4,0},{8,12},{12,8},{16,20},{20,16},{24,28},{28,24},{1,5},{5... | collective-permute-start | bytes 3145736 | tf_op jit(solution)/shard_map/ppermute | solution.py:67
  376.7 27.0 %collective-permute-start.72 = (bf16[192,1024]{1,0:T(8,128)(2,1)S(1)}, bf16[192,1024]{1,0:T(8,128)(2,1)S(1)}, u32[]{:S(2)}, u32[]{:S(2)}) collective-permute-start(bf16[192,1024]{1,0:T(8,128)(2,1)S(1)} %add_convert_fusion.23), channel_id=1, source_target_pairs={{0,8},{4,12},{24,16},{28,20},{1,9},{5,13},{25,17},{29,21},{2,10},{... | collective-permute-start | bytes 1179656 | tf_op jit(solution)/shard_map/ppermute | solution.py:141
  378.3 20.6 %collective-permute-start.76 = (bf16[336,1024]{1,0:T(8,128)(2,1)S(1)}, bf16[336,1024]{1,0:T(8,128)(2,1)S(1)}, u32[]{:S(2)}, u32[]{:S(2)}) collective-permute-start(bf16[336,1024]{1,0:T(8,128)(2,1)S(1)} %add_convert_fusion.12), channel_id=1, source_target_pairs={{0,8},{4,12},{24,16},{28,20},{1,9},{5,13},{25,17},{29,21},{2,10},{... | collective-permute-start | bytes 2064392 | tf_op jit(solution)/shard_map/ppermute | solution.py:141
  380.0 25.1 %collective-permute-start.62 = (bf16[1024,256]{1,0:T(8,128)(2,1)S(1)}, bf16[1024,256]{1,0:T(8,128)(2,1)S(1)}, u32[]{:S(2)}, u32[]{:S(2)}) collective-permute-start(bf16[1024,256]{1,0:T(8,128)(2,1)S(1)} %get-tuple-element.407), channel_id=1, source_target_pairs={{0,1},{1,0},{2,3},{3,2},{4,5},{5,4},{6,7},{7,6},{8,9},{9,8},{10,11... | collective-permute-start | bytes 1572872 | tf_op jit(solution)/shard_map/ppermute | solution.py:67
  382.8 23.0 %collective-permute-start.64 = (bf16[1024,256]{1,0:T(8,128)(2,1)S(1)}, bf16[1024,256]{1,0:T(8,128)(2,1)S(1)}, u32[]{:S(2)}, u32[]{:S(2)}) collective-permute-start(bf16[1024,256]{1,0:T(8,128)(2,1)S(1)} %add_convert_fusion.14), channel_id=1, source_target_pairs={{0,2},{1,3},{2,0},{3,1},{4,6},{5,7},{6,4},{7,5},{8,10},{9,11},{10,... | collective-permute-start | bytes 1572872 | tf_op jit(solution)/shard_map/ppermute | solution.py:67
  399.1 7.0 %collective-permute-start.77 = (bf16[336,1024]{1,0:T(8,128)(2,1)S(1)}, bf16[336,1024]{1,0:T(8,128)(2,1)S(1)}, u32[]{:S(2)}, u32[]{:S(2)}) collective-permute-start(bf16[336,1024]{1,0:T(8,128)(2,1)S(1)} %add_convert_fusion.11), channel_id=1, source_target_pairs={{8,16},{12,20},{16,8},{20,12},{9,17},{13,21},{17,9},{21,13},{10,18... | collective-permute-start | bytes 2064392 | tf_op jit(solution)/shard_map/ppermute | solution.py:141
  402.2 50.0 %collective-permute-start.80 = (bf16[512,1024]{1,0:T(8,128)(2,1)S(1)}, bf16[512,1024]{1,0:T(8,128)(2,1)S(1)}, u32[]{:S(2)}, u32[]{:S(2)}) collective-permute-start(bf16[512,1024]{1,0:T(8,128)(2,1)S(1)} %broadcast_select_fusion.1.own_ref), channel_id=1, source_target_pairs={{0,4},{4,0},{8,12},{12,8},{16,20},{20,16},{24,28},{28,24},{1,5},{5... | collective-permute-start | bytes 3145736 | tf_op jit(solution)/shard_map/ppermute | solution.py:67
  403.7 27.2 %collective-permute-start.81 = (bf16[512,1024]{1,0:T(8,128)(2,1)S(1)}, bf16[512,1024]{1,0:T(8,128)(2,1)S(1)}, u32[]{:S(2)}, u32[]{:S(2)}) collective-permute-start(bf16[512,1024]{1,0:T(8,128)(2,1)S(1)} %add_convert_fusion.1), channel_id=1, source_target_pairs={{8,0},{12,4},{16,24},{20,28},{9,1},{13,5},{17,25},{21,29},{10,2},{... | collective-permute-start | bytes 3145736 | tf_op jit(solution)/shard_map/ppermute | solution.py:141
  405.8 49.6 %collective-permute-start.69 = (bf16[1024,256]{1,0:T(8,128)(2,1)S(1)}, bf16[1024,256]{1,0:T(8,128)(2,1)S(1)}, u32[]{:S(2)}, u32[]{:S(2)}) collective-permute-start(bf16[1024,256]{1,0:T(8,128)(2,1)S(1)} %get-tuple-element.417), channel_id=1, source_target_pairs={{0,1},{1,0},{2,3},{3,2},{4,5},{5,4},{6,7},{7,6},{8,9},{9,8},{10,11... | collective-permute-start | bytes 1572872 | tf_op jit(solution)/shard_map/ppermute | solution.py:67
  407.0 38.6 %collective-permute-start.78 = (bf16[336,1024]{1,0:T(8,128)(2,1)S(1)}, bf16[336,1024]{1,0:T(8,128)(2,1)S(1)}, u32[]{:S(2)}, u32[]{:S(2)}) collective-permute-start(bf16[336,1024]{1,0:T(8,128)(2,1)S(1)} %add_convert_fusion.10), channel_id=1, source_target_pairs={{8,0},{12,4},{16,24},{20,28},{9,1},{13,5},{17,25},{21,29},{10,2},{... | collective-permute-start | bytes 2064392 | tf_op jit(solution)/shard_map/ppermute | solution.py:141
  408.5 42.4 %collective-permute-start.74 = (bf16[192,1024]{1,0:T(8,128)(2,1)S(1)}, bf16[192,1024]{1,0:T(8,128)(2,1)S(1)}, u32[]{:S(2)}, u32[]{:S(2)}) collective-permute-start(bf16[192,1024]{1,0:T(8,128)(2,1)S(1)} %add_convert_fusion.21), channel_id=1, source_target_pairs={{8,0},{12,4},{16,24},{20,28},{9,1},{13,5},{17,25},{21,29},{10,2},{... | collective-permute-start | bytes 1179656 | tf_op jit(solution)/shard_map/ppermute | solution.py:141
  430.8 24.5 %collective-permute-start.71 = (bf16[1024,256]{1,0:T(8,128)(2,1)S(1)}, bf16[1024,256]{1,0:T(8,128)(2,1)S(1)}, u32[]{:S(2)}, u32[]{:S(2)}) collective-permute-start(bf16[1024,256]{1,0:T(8,128)(2,1)S(1)} %add_convert_fusion.13), channel_id=1, source_target_pairs={{0,2},{1,3},{2,0},{3,1},{4,6},{5,7},{6,4},{7,5},{8,10},{9,11},{10,... | collective-permute-start | bytes 1572872 | tf_op jit(solution)/shard_map/ppermute | solution.py:67
  445.6 26.1 %collective-permute-start.82 = (bf16[512,1024]{1,0:T(8,128)(2,1)S(1)}, bf16[512,1024]{1,0:T(8,128)(2,1)S(1)}, u32[]{:S(2)}, u32[]{:S(2)}) collective-permute-start(bf16[512,1024]{1,0:T(8,128)(2,1)S(1)} %broadcast_select_fusion.own_ref), channel_id=1, source_target_pairs={{0,4},{4,0},{8,12},{12,8},{16,20},{20,16},{24,28},{28,24},{1,5},{5... | collective-permute-start | bytes 3145736 | tf_op jit(solution)/shard_map/ppermute | solution.py:67
  450.9 36.8 %collective-permute-start.79 = (bf16[336,1024]{1,0:T(8,128)(2,1)S(1)}, bf16[336,1024]{1,0:T(8,128)(2,1)S(1)}, u32[]{:S(2)}, u32[]{:S(2)}) collective-permute-start(bf16[336,1024]{1,0:T(8,128)(2,1)S(1)} %broadcast_select_fusion.3.refs_2_), channel_id=1, source_target_pairs={{0,4},{4,0},{8,12},{12,8},{16,20},{20,16},{24,28},{28,24},{1,5},{5... | collective-permute-start | bytes 2064392 | tf_op jit(solution)/shard_map/ppermute | solution.py:67
  452.2 35.6 %collective-permute-start.75 = (bf16[192,1024]{1,0:T(8,128)(2,1)S(1)}, bf16[192,1024]{1,0:T(8,128)(2,1)S(1)}, u32[]{:S(2)}, u32[]{:S(2)}) collective-permute-start(bf16[192,1024]{1,0:T(8,128)(2,1)S(1)} %broadcast_select_fusion.4.refs_0_), channel_id=1, source_target_pairs={{0,4},{4,0},{8,12},{12,8},{16,20},{20,16},{24,28},{28,24},{1,5},{5... | collective-permute-start | bytes 1179656 | tf_op jit(solution)/shard_map/ppermute | solution.py:67
  (104 other events, 828.8 us)
